TPU v7x, 32 devices: a whole 2x2x4 slice. The times are simulated.
32 devices in a mesh: fsdp: 2 (over x), ctx: 4 (over y, core), tp: 4 (over z).
Axes of the slice: x: 2, y: 2, z: 4, core: 2. Of those that a mesh axis runs over, the one named last changes fastest.
Arguments:
- q_in: bfloat16 [2, 1024, 4096], P('fsdp', 'ctx', 'tp'), may hold values from -6 to 6
- k_in: bfloat16 [2, 1024, 4096], P('fsdp', 'ctx', 'tp'), may hold values from -6 to 6
- v_in: bfloat16 [2, 1024, 4096], P('fsdp', 'ctx', 'tp'), may hold values from -6 to 6
- grad_out: bfloat16 [2, 1024, 4096], P('fsdp', 'ctx', 'tp'), may hold values from -6 to 6
- genome_ids: int32 [2, 1024], P('fsdp', 'ctx'), may hold values from 0 to 7, never falling along the last dimension, each value on 1 to 256 neighbouring positions
- long_filter: bfloat16 [256, 128], P('tp', 'fsdp'), may hold values from -0.5 to 0.5
- short_filter: float32 [3, 7, 4096], P(None, None, 'tp'), may hold values from -2 to 2
Outputs:
- grad_q: bfloat16 [2, 1024, 4096], P('fsdp', 'ctx', 'tp')
- grad_k: bfloat16 [2, 1024, 4096], P('fsdp', 'ctx', 'tp')
- grad_v: bfloat16 [2, 1024, 4096], P('fsdp', 'ctx', 'tp')
- grad_long: float32 [256, 128], P('tp', 'fsdp')
- grad_short: float32 [3, 7, 4096], P(None, None, 'tp')
Inputs may be any that keep to these rules, and one draw needn't show every extreme that they name: `genome_ids`: along each sequence the genome ids never fall; each genome covers 1 to 256 positions, and one covers exactly that many.
All inputs are finite; a program needn't handle non-finite values.
Results may differ from a plain program's by a relative error of at most 0.005.
Values may be sent and summed in bfloat16 or wider, within the bound.
No kernel may reach another device: no remote copies, remote signals or barrier semaphores. Data moves between devices by JAX's collectives and lax.ppermute only.
A program may use at most 128 MiB of HBM per device.

v0:
```python
import functools
import math

import jax
import jax.numpy as jnp
from jax import lax
from jax.experimental import pallas as pl
from jax.experimental.pallas import tpu as pltpu
from jax.sharding import PartitionSpec as P

TAPS = 128
SHORT = 7
LANES = 128
LEAD = 16
REACH = TAPS + LEAD
F32 = jnp.float32
BF16 = jnp.bfloat16
NT = (((1,), (1,)), ((), ()))
NN = (((1,), (0,)), ((), ()))


def shifted(block, axis, distance):
    devices = range(lax.axis_size(axis))
    route = [(i - distance, i) for i in devices if i - distance in devices]
    return lax.ppermute(block, axis, route)


def dot(a, b, dims):
    return lax.dot_general(a, b, dims, preferred_element_type=F32)


def mixer_kernel(
    rows,
    long_scale,
    short_scale,
    ids_ref,
    taps_ref,
    w_ref,
    pk_ref,
    pv_ref,
    pq_ref,
    nq_ref,
    ng_ref,
    nk_ref,
    nv_ref,
    q_ref,
    k_ref,
    v_ref,
    g_ref,
    oq_ref,
    ok_ref,
    ov_ref,
    part_ref,
    idc,
    mj,
    ml,
    mn,
    mp,
    flip,
    xk,
    xv,
    xq,
    xg,
    ks,
    vs,
    uf,
    dzf,
    ut,
    utr,
    dzt,
    dzr,
    zt,
    dut,
    dq,
    dk,
    dv,
    gl,
):
    blocks = rows // TAPS
    frame = 2 * TAPS
    width = TAPS // LANES * LANES

    @pl.when(pl.program_id(0) == 0)
    def prepare():
        row = lax.broadcasted_iota(jnp.int32, (TAPS, TAPS), 0)
        col = lax.broadcasted_iota(jnp.int32, (TAPS, TAPS), 1)
        for b in range(blocks + 4):
            line = jnp.broadcast_to(ids_ref[:, TAPS * b : TAPS * (b + 1)], (TAPS, TAPS))
            idc[TAPS * b : TAPS * (b + 1), :] = line.T
        step = 8

        def short_masks(i, carry):
            base = pl.multiple_of(TAPS + step * i, 8)
            here = idc[pl.ds(base, step), :]
            for j in range(1, SHORT):
                mj[j - 1, pl.ds(base, step), :] = (here == idc[pl.ds(base - j, step), :]).astype(F32)
            return carry

        lax.fori_loop(0, (rows + TAPS + REACH) // step, short_masks, 0)

        def same(t_block, s_block, count):
            start = TAPS * (t_block + 2)
            line = ids_ref[:, TAPS * (s_block + 2) : TAPS * (s_block + 3)]
            return (idc[start : start + count, :] == line).astype(F32)

        lower = (row >= col).astype(F32)
        upper = 1.0 - lower
        flip[...] = (row + col == TAPS - 1).astype(BF16)
        for b in range(blocks):
            ml[b] = (same(b, b, TAPS) * lower).astype(BF16)
        for b in range(blocks + 1):
            ml[blocks + b] = (same(b, b - 1, TAPS) * upper).astype(BF16)
        mn[0] = (same(blocks, blocks, 16) * lower[:16]).astype(BF16)
        mn[1] = (same(blocks, blocks, 16) * (row <= col).astype(F32)[:16]).astype(BF16)
        mn[2] = (same(blocks, blocks + 1, 16) * (row > col).astype(F32)[:16]).astype(BF16)
        for b in range(blocks):
            both = same(b, b, TAPS) * lower + same(b, b - 1, TAPS) * upper
            mp[b] = dot(both.astype(BF16), flip[...], NN)
        uf[...] = jnp.zeros_like(uf)
        dzf[...] = jnp.zeros_like(dzf)

    xk[0:REACH] = pk_ref[...].astype(F32)
    xv[0:REACH] = pv_ref[...].astype(F32)
    xk[REACH : REACH + rows] = k_ref[0].astype(F32)
    xv[REACH : REACH + rows] = v_ref[0].astype(F32)
    xk[REACH + rows : REACH + rows + LEAD] = nk_ref[...].astype(F32)
    xv[REACH + rows : REACH + rows + LEAD] = nv_ref[...].astype(F32)
    xq[0:LEAD] = pq_ref[...].astype(F32)
    xq[LEAD : LEAD + rows] = q_ref[0].astype(F32)
    xq[LEAD + rows : LEAD + rows + REACH] = nq_ref[...].astype(F32)
    xg[0:rows] = g_ref[0].astype(F32)
    xg[rows : rows + REACH] = ng_ref[...].astype(F32)

    weights = [[w_ref[i, j : j + 1, :] for j in range(SHORT)] for i in range(3)]
    chunk = 40

    def convolve(i, carry):
        low = pl.multiple_of(chunk * i, 8)
        key = weights[1][0] * xk[pl.ds(low + LEAD, chunk), :]
        value = weights[2][0] * xv[pl.ds(low + LEAD, chunk), :]
        for j in range(1, SHORT):
            mask = mj[j - 1, pl.ds(low + TAPS, chunk), :]
            key += weights[1][j] * (mask * xk[pl.ds(low + LEAD - j, chunk), :])
            value += weights[2][j] * (mask * xv[pl.ds(low + LEAD - j, chunk), :])
        ks[pl.ds(low, chunk), :] = key
        vs[pl.ds(low, chunk), :] = value
        uf[pl.ds(low, chunk), :] = key * value
        query = weights[0][0] * xq[pl.ds(low + LEAD, chunk), :]
        for j in range(1, SHORT):
            mask = mj[j - 1, pl.ds(low + frame, chunk), :]
            query += weights[0][j] * (mask * xq[pl.ds(low + LEAD - j, chunk), :])
        dzf[pl.ds(low, chunk), :] = xg[pl.ds(low, chunk), :] * query
        return carry

    lax.fori_loop(0, (rows + REACH) // chunk, convolve, 0)

    for b in range(blocks + 2):
        here = slice(TAPS * b, TAPS * (b + 1))
        turned = uf[here, :].T.astype(BF16)
        ut[:, here] = turned
        if b <= blocks:
            utr[:, here] = dot(turned, flip[...], NN).astype(BF16)
        dzt[:, here] = dzf[here, :].T.astype(BF16)
        if b < blocks:
            dzr[here, :] = dzf[here, :].astype(BF16)

    lane_group = lax.broadcasted_iota(jnp.int32, (TAPS, LANES), 1) // 16
    row = lax.broadcasted_iota(jnp.int32, (TAPS, TAPS), 0)
    col = lax.broadcasted_iota(jnp.int32, (TAPS, TAPS), 1)
    lower_flipped = row + col >= TAPS - 1

    for g in range(LANES // 16):
        c = slice(16 * g, 16 * g + 16)
        line = jnp.broadcast_to(taps_ref[g : g + 1, 0:TAPS], (TAPS, TAPS))
        band = pltpu.roll(line, 0, 1, stride=1, stride_axis=0).astype(BF16)
        line = jnp.broadcast_to(taps_ref[g : g + 1, TAPS:], (16, TAPS))
        other = pltpu.roll(line, 0, 1, stride=1, stride_axis=0).astype(BF16)
        near = [band * ml[b] for b in range(blocks)]
        far = [band * ml[blocks + b] for b in range(blocks + 1)]
        for b in range(blocks):
            window = slice(TAPS * b, TAPS * (b + 2))
            here = slice(TAPS * b, TAPS * (b + 1))
            zt[c, here] = dot(ut[c, window], jnp.concatenate([far[b], near[b]], axis=1), NT)
            dut[c, here] = dot(dzt[c, window], jnp.concatenate([near[b], far[b + 1]], axis=0), NN)
        window = slice(TAPS * blocks, TAPS * (blocks + 2))
        here = slice(TAPS * blocks, TAPS * blocks + 16)
        edge = jnp.concatenate([far[blocks][:16], band[:16] * mn[0]], axis=1)
        zt[c, here] = dot(ut[c, window], edge, NT)
        edge = jnp.concatenate([other * mn[1], other * mn[2]], axis=1)
        dut[c, here] = dot(dzt[c, window], edge, NT)
        total = None
        for b in range(blocks):
            here = slice(TAPS * b, TAPS * (b + 1))
            mine = jnp.where(lane_group == g, dzr[here, :], jnp.zeros((), BF16))
            pairs = dot(mine, utr[:, TAPS * b : TAPS * (b + 2)], NN)
            term = jnp.where(lower_flipped, pairs[:, TAPS:], pairs[:, :TAPS]) * mp[b]
            total = term if total is None else total + term
        skewed = pltpu.roll(total, 1, 1, stride=1, stride_axis=0)
        gl[g : g + 1, :] = jnp.sum(skewed, axis=0, keepdims=True)

    for b in range(blocks + 1):
        count = TAPS if b < blocks else 16
        here = slice(TAPS * b, TAPS * b + count)
        z = zt[:, TAPS * b : TAPS * (b + 1)].T[:count]
        du = dut[:, TAPS * b : TAPS * (b + 1)].T[:count]
        there = slice(TAPS * (b + 1), TAPS * (b + 1) + count)
        dq[here, :] = xg[here, :] * z
        dk[here, :] = du * vs[there, :]
        dv[here, :] = du * ks[there, :]

    part = 32

    def finish(i, sums):
        low = pl.multiple_of(part * i, part)
        fresh = []
        for grad, source, lead, w, out in (
            (dq, xq, LEAD, weights[0], oq_ref),
            (dk, xk, REACH, weights[1], ok_ref),
            (dv, xv, REACH, weights[2], ov_ref),
        ):
            x = source[pl.ds(low + lead, part), :]
            total = None
            for j in range(SHORT):
                piece = grad[pl.ds(low + j, part), :]
                if j:
                    piece = piece * mj[j - 1, pl.ds(low + frame + j, part), :]
                total = w[j] * piece if total is None else total + w[j] * piece
                fresh.append(jnp.sum((x * piece).reshape(part // 8, 8, LANES), axis=0))
            out[0, pl.ds(low, part), :] = total.astype(BF16)
        return tuple(a + b for a, b in zip(sums, fresh))

    zero = jnp.zeros((8, LANES), F32)
    sums = lax.fori_loop(0, rows // part, finish, (zero,) * (3 * SHORT))
    lines = [jnp.sum(s, axis=0, keepdims=True) * short_scale for s in sums]
    for n, line in enumerate(lines):
        part_ref[n : n + 1, :] = line
    part_ref[3 * SHORT : 24, :] = jnp.zeros((24 - 3 * SHORT, LANES), F32)
    part_ref[24:32, :] = gl[...] * long_scale


def mixer(ids, taps, short_filter, prev, succ, q_in, k_in, v_in, grad_out, scales):
    rows, channels = q_in.shape[1:]
    blocks = rows // TAPS
    tail = pl.BlockSpec
    local = pl.BlockSpec((1, rows, LANES), lambda i: (0, 0, i))
    vm = lambda *shape: pltpu.VMEM(shape, F32)
    vb = lambda *shape: pltpu.VMEM(shape, BF16)
    out = jax.ShapeDtypeStruct((1, rows, channels), BF16)
    place = 2 * REACH // LEAD
    return pl.pallas_call(
        functools.partial(mixer_kernel, rows, *scales),
        grid=(channels // LANES,),
        in_specs=[
            pl.BlockSpec(ids.shape, lambda i: (0, 0)),
            pl.BlockSpec((LANES // 16, 2 * TAPS), lambda i: (i, 0)),
            pl.BlockSpec((3, SHORT, LANES), lambda i: (0, 0, i)),
            pl.BlockSpec((REACH, LANES), lambda i: (0, i)),
            pl.BlockSpec((REACH, LANES), lambda i: (1, i)),
            pl.BlockSpec((LEAD, LANES), lambda i: (place, i)),
            pl.BlockSpec((REACH, LANES), lambda i: (0, i)),
            pl.BlockSpec((REACH, LANES), lambda i: (1, i)),
            pl.BlockSpec((LEAD, LANES), lambda i: (place, i)),
            pl.BlockSpec((LEAD, LANES), lambda i: (place + 1, i)),
            local,
            local,
            local,
            local,
        ],
        out_specs=[local, local, local, pl.BlockSpec((32, LANES), lambda i: (0, i))],
        out_shape=[out, out, out, jax.ShapeDtypeStruct((32, channels), F32)],
        scratch_shapes=[
            vm(rows + 4 * TAPS, LANES),
            vm(SHORT - 1, rows + 4 * TAPS, LANES),
            vb(2 * blocks + 1, TAPS, TAPS),
            vb(3, 16, TAPS),
            vm(blocks, TAPS, TAPS),
            vb(TAPS, TAPS),
            vm(rows + REACH + LEAD, LANES),
            vm(rows + REACH + LEAD, LANES),
            vm(rows + REACH + LEAD, LANES),
            vm(rows + REACH, LANES),
            vm(rows + REACH, LANES),
            vm(rows + REACH, LANES),
            vm(rows + 2 * TAPS, LANES),
            vm(rows + 2 * TAPS, LANES),
            vb(LANES, rows + 2 * TAPS),
            vb(LANES, rows + TAPS),
            vb(LANES, rows + 2 * TAPS),
            vb(rows, LANES),
            vm(LANES, rows + TAPS),
            vm(LANES, rows + TAPS),
            vm(rows + 16, LANES),
            vm(rows + 16, LANES),
            vm(rows + 16, LANES),
            vm(8, LANES),
        ],
        compiler_params=pltpu.CompilerParams(vmem_limit_bytes=40 << 20),
        name="mixer",
    )(
        ids,
        taps,
        short_filter,
        prev,
        prev,
        prev,
        succ,
        succ,
        succ,
        succ,
        q_in,
        k_in,
        v_in,
        grad_out,
    )


def total_over(x, axis):
    size = lax.axis_size(axis)
    if size & (size - 1):
        return lax.psum(x, axis)
    bit = 1
    while bit < size:
        x = x + lax.ppermute(x, axis, [(i, i ^ bit) for i in range(size)])
        bit *= 2
    return x


def body(q_in, k_in, v_in, grad_out, genome_ids, long_filter, short_filter):
    rows, channels = q_in.shape[1:]
    seq_count = lax.axis_size("fsdp")
    length = rows * lax.axis_size("ctx")
    ids = genome_ids + 1
    wide = jnp.zeros((1, channels - REACH), BF16)
    tail_ids = jnp.concatenate([ids[:, rows - REACH :].astype(BF16), wide], axis=1)
    head_ids = jnp.concatenate([ids[:, :REACH].astype(BF16), wide], axis=1)
    tail = jnp.concatenate(
        [k_in[0, rows - REACH :], v_in[0, rows - REACH :], q_in[0, rows - LEAD :], tail_ids]
    )
    head = jnp.concatenate(
        [q_in[0, :REACH], grad_out[0, :REACH], k_in[0, :LEAD], v_in[0, :LEAD], head_ids]
    )
    prev = shifted(tail, "ctx", 1)
    succ = shifted(head, "ctx", -1)
    filters = lax.all_gather(long_filter, "fsdp", axis=1, tiled=True).astype(F32)
    blank = jnp.zeros((1, 2 * TAPS - REACH), F32)
    ids_ext = jnp.concatenate(
        [
            blank,
            prev[2 * REACH + LEAD :, :REACH].astype(F32),
            ids.astype(F32),
            succ[2 * REACH + 2 * LEAD :, :REACH].astype(F32),
            blank,
        ],
        axis=1,
    )
    turned = jnp.concatenate([filters[:, :1], filters[:, :0:-1]], axis=1)
    taps = jnp.concatenate([turned, filters], axis=1)
    groups = filters.shape[0]
    scales = (
        1.0 / math.sqrt(seq_count * length * (channels // groups)),
        1.0 / math.sqrt(seq_count * length),
    )
    out_q, out_k, out_v, sums = mixer(
        ids_ext, taps, short_filter, prev, succ, q_in, k_in, v_in, grad_out, scales
    )
    sums = total_over(total_over(sums, "ctx"), "fsdp")
    grad_short = sums[: 3 * SHORT].reshape(3, SHORT, channels)
    grad_long = sums[24:].reshape(8, channels // LANES, LANES).transpose(1, 0, 2)
    grad_long = grad_long.reshape(groups, TAPS)
    own = TAPS // seq_count
    grad_long = lax.dynamic_slice_in_dim(grad_long, lax.axis_index("fsdp") * own, own, 1)
    return out_q, out_k, out_v, grad_long, grad_short


def solution(mesh):
    return jax.shard_map(
        body,
        mesh=mesh,
        in_specs=(
            P("fsdp", "ctx", "tp"),
            P("fsdp", "ctx", "tp"),
            P("fsdp", "ctx", "tp"),
            P("fsdp", "ctx", "tp"),
            P("fsdp", "ctx"),
            P("tp", "fsdp"),
            P(None, None, "tp"),
        ),
        out_specs=(
            P("fsdp", "ctx", "tp"),
            P("fsdp", "ctx", "tp"),
            P("fsdp", "ctx", "tp"),
            P("tp", "fsdp"),
            P(None, None, "tp"),
        ),
        check_vma=False,
    )
```

profile of v0, /device:TPU:0, one launch (start us, length us, event | category | flops | bytes accessed | tf_op | source)
XLA Modules:
  0.0 63.8 jit_solution(15415224163707726208)
XLA Ops:
  0.6 0.7 %add_convert_fusion = (f32[1,256]{1,0:T(1,128)S(1)}, bf16[1,256]{1,0:T(2,128)(2,1)S(1)}) fusion(s32[1,256]{1,0:T(1,128)} %param.11), kind=kLoop, calls=%fused_computation.15 | loop fusion | flops 768 | bytes 2560 | tf_op jit(solution)/shard_map/convert_element_type | solution.py:350
  1.3 0.1 fusion.2
  1.4 0.8 %slice_bitcast_fusion.3 = bf16[16,1024]{1,0:T(8,128)(2,1)S(1)} fusion(bf16[1,256,1024]{2,1,0:T(8,128)(2,1)} %q_ref.1), kind=kLoop, calls=%fused_computation.11 | loop fusion | bytes 65536 | tf_op jit(solution)/shard_map/squeeze | solution.py:337
  2.2 1.1 %slice_bitcast_fusion = (bf16[144,1024]{1,0:T(8,128)(2,1)S(1)}, bf16[144,1024]{1,0:T(8,128)(2,1)S(1)}) fusion(bf16[1,256,1024]{2,1,0:T(8,128)(2,1)} %v_ref.1, bf16[1,256,1024]{2,1,0:T(8,128)(2,1)} %k_ref.1), kind=kLoop, calls=%fused_computation.5 | loop fusion | bytes 1179648 | tf_op jit(solution)/shard_map/squeeze | solution.py:337
  3.2 0.0 copy-start
  3.3 0.0 copy-start.3
  3.3 0.9 %fusion.1 = bf16[305,1024]{1,0:T(8,128)(2,1)} fusion(bf16[1,144]{1,0:T(2,128)(2,1)S(1)} %get-tuple-element.14, bf16[16,1024]{1,0:T(8,128)(2,1)S(1)} %slice_bitcast_fusion.3, bf16[144,1024]{1,0:T(8,128)(2,1)S(1)} %get-tuple-element.17, bf16[144,1024]{1,0:T(8,128)(2,1)S(1)} %get-tuple-element.18), kind=kLoop, calls=%fused_computation.2 | loop fusion | flops 3123200 | bytes 1247520 | tf_op jit(solution)/shard_map/concatenate | solution.py:336
  4.2 0.0 copy-start.2
  4.2 0.0 copy-start.1
  4.2 0.0 copy-start.5
  4.2 2.5 %collective-permute-start = (bf16[305,1024]{1,0:T(8,128)(2,1)}, bf16[305,1024]{1,0:T(8,128)(2,1)S(1)}, u32[]{:S(2)}, u32[]{:S(2)}) collective-permute-start(bf16[305,1024]{1,0:T(8,128)(2,1)} %fusion.1), channel_id=1, source_target_pairs={{0,4},{4,8},{8,12},{1,5},{5,9},{9,13},{2,6},{6,10},{10,14},{3,7},{... | collective-permute-start | bytes 1873928 | tf_op jit(solution)/shard_map/ppermute | solution.py:25
  6.7 0.0 copy-done
  6.7 0.7 %bitcast_dynamic-update-slice_fusion.1 = bf16[321,1024]{1,0:T(8,128)(2,1)} fusion(bf16[1,256,1024]{2,1,0:T(8,128)(2,1)S(1)} %copy-done), kind=kLoop, calls=%fused_computation.4 | loop fusion | bytes 589824
  7.4 0.0 copy-done.3
  7.4 0.7 %bitcast_dynamic-update-slice_fusion = bf16[321,1024]{1,0:T(8,128)(2,1)} fusion(bf16[321,1024]{1,0:T(8,128)(2,1)} %bitcast_dynamic-update-slice_fusion.1, bf16[1,256,1024]{2,1,0:T(8,128)(2,1)S(1)} %copy-done.3), kind=kLoop, calls=%fused_computation.3 | loop fusion | bytes 589824
  8.2 0.0 copy-done.2
  8.2 0.6 bitcast_dynamic-update-slice_fusion.3
  8.8 0.0 copy-done.1
  8.8 0.6 bitcast_dynamic-update-slice_fusion.2
  9.4 0.6 constant_dynamic-update-slice_fusion
  10.0 1.3 %collective-permute-start.1 = (bf16[321,1024]{1,0:T(8,128)(2,1)}, bf16[321,1024]{1,0:T(8,128)(2,1)S(1)}, u32[]{:S(2)}, u32[]{:S(2)}) collective-permute-start(bf16[321,1024]{1,0:T(8,128)(2,1)} %constant_dynamic-update-slice_fusion), channel_id=1, source_target_pairs={{4,0},{8,4},{12,8},{5,1},{9,5},{13,9},{6,2},{10,6},{14,10},{7,3},{... | collective-permute-start | bytes 1972232 | tf_op jit(solution)/shard_map/ppermute | solution.py:25
  11.3 0.0 copy-done.5
  11.3 0.1 copy.12
  11.4 4.7 %all_gather.3 = bf16[64,128]{0,1:T(8,128)(2,1)S(1)} all-gather(bf16[64,64]{0,1:T(8,128)(2,1)S(1)} %copy.12), channel_id=1, replica_groups=mesh['fsdp'=2,'ctx'=4,'tp'=4] {'fsdp'}, dimensions={1}, use_global_device_ids=true | all-gather | bytes 24576 | tf_op jit(solution)/shard_map/all_gather | solution.py:344
  16.1 0.1 copy.13
  16.2 0.1 slice.67
  16.3 0.7 %rev.3 = f32[64,127]{1,0:T(8,128)} reverse(f32[64,127]{1,0:T(8,128)S(1)} %slice.67), dimensions={1} | reverse | bytes 65024 | tf_op jit(solution)/shard_map/rev | solution.py:356
  17.0 0.8 %pad_maximum_fusion.taps_ref = f32[64,256]{1,0:T(8,128)S(1)} fusion(f32[64,128]{1,0:T(8,128)S(1)} %convert_element_type.17, f32[64,127]{1,0:T(8,128)} %rev.3, f32[64,1]{1,0:T(8,128)S(1)} %slice.66), kind=kLoop, calls=%fused_computation.7 | loop fusion | flops 32768 | bytes 131072 | tf_op jit(solution)/shard_map/concatenate | solution.py:357
  17.8 0.0 collective-permute-done.pk_ref.pv_ref.pq_ref
  17.8 0.0 collective-permute-done.1.nq_ref.ng_ref.nk_ref.nv_ref
  17.9 0.1 concatenate.22.ids_ref
  18.0 0.0 copy-start.4
  18.0 0.9 %copy-done.4 = f32[3,7,1024]{2,1,0:T(8,128)S(1)} copy-done((f32[3,7,1024]{2,1,0:T(8,128)S(1)}, f32[3,7,1024]{2,1,0:T(8,128)}, u32[]{:S(2)}) %copy-start.4) | copy-done | bytes 86040
  18.8 24.6 %mixer.1 = (bf16[1,256,1024]{2,1,0:T(8,128)(2,1)}, bf16[1,256,1024]{2,1,0:T(8,128)(2,1)}, bf16[1,256,1024]{2,1,0:T(8,128)(2,1)}, f32[32,1024]{1,0:T(8,128)S(1)}) custom-call(f32[1,768]{1,0:T(1,128)S(1)} %concatenate.22.ids_ref, f32[64,256]{1,0:T(8,128)S(1)} %pad_maximum_fusion.taps_ref, f32[3,7,1024]{2,1,0:T(8,128)S(1)} %copy-done.4, ...), custom_call_target="tpu_custom_call" | custom-call | tf_op jit(solution)/shard_map/mixer/pallas_call | solution.py:250
  43.5 7.0 %collective-permute-start.2 = (f32[32,1024]{1,0:T(8,128)S(1)}, f32[32,1024]{1,0:T(8,128)S(1)}, u32[]{:S(2)}, u32[]{:S(2)}) collective-permute-start(f32[32,1024]{1,0:T(8,128)S(1)} %get-tuple-element.12), channel_id=1, source_target_pairs={{0,4},{4,0},{8,12},{12,8},{1,5},{5,1},{9,13},{13,9},{2,6},{6,2},{1... | collective-permute-start | bytes 393224 | tf_op jit(solution)/shard_map/ppermute | solution.py:323
  50.5 1.0 %collective-permute-done.2 = f32[32,1024]{1,0:T(8,128)S(1)} collective-permute-done((f32[32,1024]{1,0:T(8,128)S(1)}, f32[32,1024]{1,0:T(8,128)S(1)}, u32[]{:S(2)}, u32[]{:S(2)}) %collective-permute-start.2) | collective-permute-done | bytes 131104 | tf_op jit(solution)/shard_map/ppermute | solution.py:323
  51.5 0.3 collective-permute-start.3
  51.7 5.6 %collective-permute-done.3 = f32[32,1024]{1,0:T(8,128)S(1)} collective-permute-done((f32[32,1024]{1,0:T(8,128)S(1)}, f32[32,1024]{1,0:T(8,128)S(1)}, u32[]{:S(2)}, u32[]{:S(2)}) %collective-permute-start.3) | collective-permute-done | bytes 131104 | tf_op jit(solution)/shard_map/ppermute | solution.py:323
  57.3 1.6 %collective-permute-start.4 = (f32[32,1024]{1,0:T(8,128)S(1)}, f32[32,1024]{1,0:T(8,128)S(1)}, u32[]{:S(2)}, u32[]{:S(2)}) collective-permute-start(f32[32,1024]{1,0:T(8,128)S(1)} %add.25), channel_id=1, source_target_pairs={{0,16},{16,0},{1,17},{17,1},{2,18},{18,2},{3,19},{19,3},{4,20},{20... | collective-permute-start | bytes 393224 | tf_op jit(solution)/shard_map/ppermute | solution.py:323
  58.9 3.5 %collective-permute-done.4 = f32[32,1024]{1,0:T(8,128)S(1)} collective-permute-done((f32[32,1024]{1,0:T(8,128)S(1)}, f32[32,1024]{1,0:T(8,128)S(1)}, u32[]{:S(2)}, u32[]{:S(2)}) %collective-permute-start.4) | collective-permute-done | bytes 131104 | tf_op jit(solution)/shard_map/ppermute | solution.py:323
  62.4 0.7 %reshape.21 = f32[3,7,1024]{2,1,0:T(8,128)} reshape(f32[21,1024]{1,0:T(8,128)S(1)} %slice.69) | data formatting | bytes 172032 | tf_op jit(solution)/shard_map/reshape | solution.py:367
  63.1 0.7 %constant_dynamic-slice_fusion = f32[64,64]{1,0:T(8,128)} fusion(f32[64,128]{1,0:T(8,128)S(1)} %slice_bitcast_fusion.2, s32[]{:T(128)S(6)} %select_n.3), kind=kLoop, calls=%fused_computation.17 | loop fusion | bytes 32772 | tf_op jit(solution)/shard_map/dynamic_slice | solution.py:371
  (10 shorter events, 0.1 us)
Async XLA Ops:
  3.2 3.5 %copy-start = (bf16[1,256,1024]{2,1,0:T(8,128)(2,1)S(1)}, bf16[1,256,1024]{2,1,0:T(8,128)(2,1)}, u32[]{:S(2)}) copy-start(bf16[1,256,1024]{2,1,0:T(8,128)(2,1)} %q_ref.1) | copy-start | bytes 1572868
  3.3 4.2 %copy-start.3 = (bf16[1,256,1024]{2,1,0:T(8,128)(2,1)S(1)}, bf16[1,256,1024]{2,1,0:T(8,128)(2,1)}, u32[]{:S(2)}) copy-start(bf16[1,256,1024]{2,1,0:T(8,128)(2,1)} %g_ref.1) | copy-start | bytes 1572868
  4.2 4.0 %copy-start.2 = (bf16[1,256,1024]{2,1,0:T(8,128)(2,1)S(1)}, bf16[1,256,1024]{2,1,0:T(8,128)(2,1)}, u32[]{:S(2)}) copy-start(bf16[1,256,1024]{2,1,0:T(8,128)(2,1)} %k_ref.1) | copy-start | bytes 1572868
  4.2 4.6 %copy-start.1 = (bf16[1,256,1024]{2,1,0:T(8,128)(2,1)S(1)}, bf16[1,256,1024]{2,1,0:T(8,128)(2,1)}, u32[]{:S(2)}) copy-start(bf16[1,256,1024]{2,1,0:T(8,128)(2,1)} %v_ref.1) | copy-start | bytes 1572868
  4.2 7.1 %copy-start.5 = (bf16[64,64]{1,0:T(8,128)(2,1)S(1)}, bf16[64,64]{1,0:T(8,128)(2,1)}, u32[]{:S(2)}) copy-start(bf16[64,64]{1,0:T(8,128)(2,1)} %param.12) | copy-start | bytes 24580
  4.2 13.6 %collective-permute-start = (bf16[305,1024]{1,0:T(8,128)(2,1)}, bf16[305,1024]{1,0:T(8,128)(2,1)S(1)}, u32[]{:S(2)}, u32[]{:S(2)}) collective-permute-start(bf16[305,1024]{1,0:T(8,128)(2,1)} %fusion.1), channel_id=1, source_target_pairs={{0,4},{4,8},{8,12},{1,5},{5,9},{9,13},{2,6},{6,10},{10,14},{3,7},{... | collective-permute-start | bytes 1873928 | tf_op jit(solution)/shard_map/ppermute | solution.py:25
  10.0 7.8 %collective-permute-start.1 = (bf16[321,1024]{1,0:T(8,128)(2,1)}, bf16[321,1024]{1,0:T(8,128)(2,1)S(1)}, u32[]{:S(2)}, u32[]{:S(2)}) collective-permute-start(bf16[321,1024]{1,0:T(8,128)(2,1)} %constant_dynamic-update-slice_fusion), channel_id=1, source_target_pairs={{4,0},{8,4},{12,8},{5,1},{9,5},{13,9},{6,2},{10,6},{14,10},{7,3},{... | collective-permute-start | bytes 1972232 | tf_op jit(solution)/shard_map/ppermute | solution.py:25
  18.0 0.9 %copy-start.4 = (f32[3,7,1024]{2,1,0:T(8,128)S(1)}, f32[3,7,1024]{2,1,0:T(8,128)}, u32[]{:S(2)}) copy-start(f32[3,7,1024]{2,1,0:T(8,128)} %w_ref.1) | copy-start | bytes 258052
  43.5 8.0 %collective-permute-start.2 = (f32[32,1024]{1,0:T(8,128)S(1)}, f32[32,1024]{1,0:T(8,128)S(1)}, u32[]{:S(2)}, u32[]{:S(2)}) collective-permute-start(f32[32,1024]{1,0:T(8,128)S(1)} %get-tuple-element.12), channel_id=1, source_target_pairs={{0,4},{4,0},{8,12},{12,8},{1,5},{5,1},{9,13},{13,9},{2,6},{6,2},{1... | collective-permute-start | bytes 393224 | tf_op jit(solution)/shard_map/ppermute | solution.py:323
  51.5 5.8 %collective-permute-start.3 = (f32[32,1024]{1,0:T(8,128)S(1)}, f32[32,1024]{1,0:T(8,128)S(1)}, u32[]{:S(2)}, u32[]{:S(2)}) collective-permute-start(f32[32,1024]{1,0:T(8,128)S(1)} %add.24), channel_id=1, source_target_pairs={{0,8},{4,12},{8,0},{12,4},{1,9},{5,13},{9,1},{13,5},{2,10},{6,14},... | collective-permute-start | bytes 393224 | tf_op jit(solution)/shard_map/ppermute | solution.py:323
  57.3 5.0 %collective-permute-start.4 = (f32[32,1024]{1,0:T(8,128)S(1)}, f32[32,1024]{1,0:T(8,128)S(1)}, u32[]{:S(2)}, u32[]{:S(2)}) collective-permute-start(f32[32,1024]{1,0:T(8,128)S(1)} %add.25), channel_id=1, source_target_pairs={{0,16},{16,0},{1,17},{17,1},{2,18},{18,2},{3,19},{19,3},{4,20},{20... | collective-permute-start | bytes 393224 | tf_op jit(solution)/shard_map/ppermute | solution.py:323
where the time goes:
time: 64.1 us; the launch traced here: 63.8 us
  Pallas kernels  24.6 us (38%)
  starting transfers between devices  12.6 us (20%)
  waiting for transfers between devices  10 us (16%)
  local copies, waits for them, and re-layouts  8.53 us (13%)
  blocking collectives  4.69 us (7%)
  other arithmetic  2.48 us (4%)
  between operations  0.79 us (1%)
    pallas_call x1, Pallas kernels, mixer(): pl.pallas_call(functools.partial(mixer_kernel, rows, *scales), grid=(chan...  24.6 us
    ppermute x3, waiting for transfers between devices, total_over(): x = x + lax.ppermute(x, axis, [(i, i ^ bit) for i in range(size)])  10 us
    ppermute x3, starting transfers between devices, total_over(): x = x + lax.ppermute(x, axis, [(i, i ^ bit) for i in range(size)])  8.82 us
    all_gather x1, blocking collectives, body(): lax.all_gather(long_filter, 'fsdp', axis=1, tiled=True).astype(F32)  4.69 us
    ppermute x2, starting transfers between devices, shifted(): return lax.ppermute(block, axis, route)  3.8 us
    unnamed x17, local copies, waits for them, and re-layouts  3.69 us
  transfers between devices with their start and end apart: 5, of which 3 were waited for; matrix products, arithmetic and copies ran while one was open for 8% of the time, Pallas kernels for 0%

commit v1 on v0

v1 whole, which is shorter than its diff:
```python
import functools
import math

import jax
import jax.numpy as jnp
from jax import lax
from jax.experimental import pallas as pl
from jax.experimental.pallas import tpu as pltpu
from jax.sharding import PartitionSpec as P

TAPS = 128
SHORT = 7
LANES = 128
GROUP = 16
EDGE = 8
HEAD_ROWS = LANES + 48
F32 = jnp.float32
BF16 = jnp.bfloat16
NT = (((1,), (1,)), ((), ()))
NN = (((1,), (0,)), ((), ()))
VMEM = pl.BlockSpec(memory_space=pltpu.VMEM)
HBM = pl.BlockSpec(memory_space=pltpu.HBM)


def swapped(near, far, axis):
    size = lax.axis_size(axis)
    near_route = [(i, i ^ 1) for i in range(size) if i ^ 1 < size]
    far_route = [(i + 1, i) for i in range(1, size - 1, 2)]
    far_route = far_route + [(i, j) for j, i in far_route]
    return lax.ppermute(near, axis, near_route), lax.ppermute(far, axis, far_route)


def dot(a, b, dims):
    return lax.dot_general(a, b, dims, preferred_element_type=F32)


def lanes_of(i):
    return pl.ds(pl.multiple_of(i * LANES, LANES), LANES)


def spread(line):
    return jnp.broadcast_to(line, (TAPS, TAPS)).T


def copy_all(pairs, sems, i, wait=False):
    for n, (source, target) in enumerate(pairs):
        copy = pltpu.make_async_copy(source, target, sems.at[i, n])
        if wait:
            copy.wait()
        else:
            copy.start()


def local_kernel(
    rows,
    ids_hbm,
    w_hbm,
    q_hbm,
    k_hbm,
    v_hbm,
    g_hbm,
    conv_hbm,
    turn_hbm,
    dzr_hbm,
    near_hbm,
    far_hbm,
    ids_ref,
    w_ref,
    bq,
    bk,
    bv,
    bg,
    conv_ref,
    turn_ref,
    dzr_ref,
    tail_ref,
    head_ref,
    idc,
    mj,
    xq,
    xk,
    xv,
    uf,
    dzf,
    small_sems,
    in_sems,
    out_sems,
):
    blocks = rows // TAPS
    count = q_hbm.shape[2] // LANES
    odd = lax.rem(lax.axis_index("ctx"), 2)

    def small():
        return ((ids_hbm, ids_ref), (w_hbm, w_ref))

    def inputs(i):
        lane = lanes_of(i)
        pairs = ((q_hbm, bq), (k_hbm, bk), (v_hbm, bv), (g_hbm, bg))
        return [(a.at[0, :, lane], b.at[i]) for a, b in pairs]

    def outputs(i):
        pairs = ((conv_ref, conv_hbm), (turn_ref, turn_hbm), (dzr_ref, dzr_hbm))
        return [(a.at[i], b.at[i]) for a, b in pairs]

    def packets(to_near, to_far):
        return ((to_near, near_hbm), (to_far, far_hbm))

    copy_all(small(), small_sems, 0)

    def fetch(i, carry):
        copy_all(inputs(i), in_sems, i)
        return carry

    lax.fori_loop(0, count, fetch, 0)
    copy_all(small(), small_sems, 0, wait=True)
    ids = (ids_ref[...] + 1).astype(F32)
    idc[0:EDGE] = jnp.zeros((EDGE, LANES), F32)
    for b in range(blocks):
        idc[EDGE + TAPS * b : EDGE + TAPS * (b + 1)] = spread(ids[:, TAPS * b : TAPS * (b + 1)])
    for x in (xq, xk, xv):
        x[0:EDGE] = jnp.zeros((EDGE, LANES), F32)

    def masks(i, carry):
        base = pl.multiple_of(16 * i, 16)
        here = idc[pl.ds(base + EDGE, 16), :]
        for j in range(1, SHORT):
            mj[j - 1, pl.ds(base, 16), :] = (here == idc[pl.ds(base + EDGE - j, 16), :]).astype(F32)
        return carry

    lax.fori_loop(0, rows // 16, masks, 0)
    pad = jnp.zeros((EDGE - blocks, LANES), F32)
    id_rows = [ids[:, TAPS * b : TAPS * (b + 1)] for b in range(blocks)]
    id_tile = jnp.concatenate(id_rows + [pad], axis=0)
    part = 32

    def one_block(i, carry):
        lane = lanes_of(i)
        copy_all(inputs(i), in_sems, i, wait=True)
        w = [[w_ref[n, j : j + 1, lane] for j in range(SHORT)] for n in range(3)]
        for x, source in ((xq, bq), (xk, bk), (xv, bv)):
            x[EDGE : EDGE + rows] = source[i].astype(F32)

        def convolve(n, inner):
            low = pl.multiple_of(part * n, part)
            out = []
            for x, taps in ((xq, w[0]), (xk, w[1]), (xv, w[2])):
                total = taps[0] * x[pl.ds(low + EDGE, part), :]
                for j in range(1, SHORT):
                    mask = mj[j - 1, pl.ds(low, part), :]
                    total += taps[j] * (mask * x[pl.ds(low + EDGE - j, part), :])
                out.append(total)
            conv_ref[i, 0, pl.ds(low, part), :] = out[1]
            conv_ref[i, 1, pl.ds(low, part), :] = out[2]
            uf[pl.ds(low, part), :] = out[1] * out[2]
            dz = bg[i, pl.ds(low, part), :].astype(F32) * out[0]
            dzf[pl.ds(low, part), :] = dz
            dzr_ref[i, pl.ds(low, part), :] = dz.astype(BF16)
            return inner

        lax.fori_loop(0, rows // part, convolve, 0)
        for b in range(blocks):
            here = slice(TAPS * b, TAPS * (b + 1))
            turned = uf[here, :].T.astype(BF16)
            turn_ref[i, 0:LANES, here] = turned
            if b == blocks - 1:
                tail_ref[i, 0:LANES, :] = turned
            turned = dzf[here, :].T.astype(BF16)
            turn_ref[i, LANES : 2 * LANES, here] = turned
            if b == 0:
                head_ref[i, 0:LANES, :] = turned

        def pair(a, b):
            return jnp.concatenate([a, b], axis=0).astype(BF16)

        last = slice(rows, rows + EDGE)
        first = slice(EDGE, 2 * EDGE)
        g_first = bg[i, 0 : 2 * EDGE, :].astype(F32)[:EDGE]
        beyond = slice(TAPS, TAPS + EDGE)
        tail_ref[i, LANES : LANES + 16, :] = pair(xk[last, :], xv[last, :])
        tail_ref[i, LANES + 16 : LANES + 32, :] = pair(xq[last, :], id_tile)
        tail_ref[i, LANES + 32 : LANES + 48, :] = jnp.zeros((16, LANES), BF16)
        head_ref[i, LANES : LANES + 16, :] = pair(xq[first, :], g_first)
        head_ref[i, LANES + 16 : LANES + 32, :] = pair(xk[first, :], xv[first, :])
        head_ref[i, LANES + 32 : LANES + 48, :] = pair(dzf[beyond, :], id_tile)
        copy_all(outputs(i), out_sems, i)
        return carry

    lax.fori_loop(0, count, one_block, 0)

    @pl.when(odd == 0)
    def even_packets():
        copy_all(packets(tail_ref, head_ref), small_sems, 0)
        copy_all(packets(tail_ref, head_ref), small_sems, 0, wait=True)

    @pl.when(odd == 1)
    def odd_packets():
        copy_all(packets(head_ref, tail_ref), small_sems, 0)
        copy_all(packets(head_ref, tail_ref), small_sems, 0, wait=True)

    def drain(i, carry):
        copy_all(outputs(i), out_sems, i, wait=True)
        return carry

    lax.fori_loop(0, count, drain, 0)


def local_part(ids, short_filter, q_in, k_in, v_in, grad_out):
    rows, channels = q_in.shape[1:]
    count = channels // LANES
    vm = lambda *shape: pltpu.VMEM(shape, F32)
    vb = lambda *shape: pltpu.VMEM(shape, BF16)
    shape = jax.ShapeDtypeStruct
    results = (
        ((count, 2, rows, LANES), F32),
        ((count, 2 * LANES, rows), BF16),
        ((count, rows, LANES), BF16),
    )
    packet = (count, HEAD_ROWS, LANES)
    return pl.pallas_call(
        functools.partial(local_kernel, rows),
        in_specs=[HBM] * 6,
        out_specs=[HBM] * 5,
        out_shape=[shape(*r) for r in results] + [shape(packet, BF16)] * 2,
        scratch_shapes=[
            pltpu.VMEM(ids.shape, jnp.int32),
            vm(*short_filter.shape),
            vb(count, rows, LANES),
            vb(count, rows, LANES),
            vb(count, rows, LANES),
            vb(count, rows, LANES),
            *[pltpu.VMEM(*r) for r in results],
            vb(*packet),
            vb(*packet),
            vm(rows + EDGE, LANES),
            vm(SHORT - 1, rows, LANES),
            vm(rows + EDGE, LANES),
            vm(rows + EDGE, LANES),
            vm(rows + EDGE, LANES),
            vm(rows, LANES),
            vm(rows, LANES),
            pltpu.SemaphoreType.DMA((1, 2)),
            pltpu.SemaphoreType.DMA((count, 4)),
            pltpu.SemaphoreType.DMA((count, 3)),
        ],
        compiler_params=pltpu.CompilerParams(vmem_limit_bytes=63 << 20),
        name="local_part",
    )(ids, short_filter, q_in, k_in, v_in, grad_out)


def mixer_kernel(
    rows,
    long_scale,
    short_scale,
    ids_hbm,
    filters_hbm,
    w_hbm,
    near_hbm,
    far_hbm,
    q_hbm,
    k_hbm,
    v_hbm,
    g_hbm,
    conv_hbm,
    turn_hbm,
    dzr_hbm,
    oq_hbm,
    ok_hbm,
    ov_hbm,
    part_ref,
    ids_ref,
    filters_ref,
    w_ref,
    prev_ref,
    next_ref,
    bq,
    bk,
    bv,
    bg,
    conv_ref,
    turn_ref,
    dzr_ref,
    oq_ref,
    ok_ref,
    ov_ref,
    taps_ref,
    idr,
    idc,
    mj,
    ml,
    mn,
    mp,
    flip,
    edges,
    ut,
    utr,
    dzt,
    dzr,
    zt,
    dut,
    dq,
    dk,
    dv,
    gl,
    small_sems,
    in_sems,
    out_sems,
):
    blocks = rows // TAPS
    frame = rows
    count = q_hbm.shape[2] // LANES
    per = LANES // GROUP
    odd = lax.rem(lax.axis_index("ctx"), 2)

    def small():
        return ((ids_hbm, ids_ref), (filters_hbm, filters_ref), (w_hbm, w_ref))

    def halos(i):
        return (
            ((far_hbm.at[i], prev_ref.at[i]), (near_hbm.at[i], next_ref.at[i])),
            ((near_hbm.at[i], prev_ref.at[i]), (far_hbm.at[i], next_ref.at[i])),
        )

    def inputs(i):
        lane = lanes_of(i)
        pairs = ((q_hbm, bq), (k_hbm, bk), (v_hbm, bv), (g_hbm, bg))
        pairs = [(a.at[0, :, lane], b.at[i]) for a, b in pairs]
        more = ((conv_hbm, conv_ref), (turn_hbm, turn_ref), (dzr_hbm, dzr_ref))
        return pairs + [(a.at[i], b.at[i]) for a, b in more]

    def outputs(i):
        lane = lanes_of(i)
        pairs = ((oq_ref, oq_hbm), (ok_ref, ok_hbm), (ov_ref, ov_hbm))
        return [(a.at[i], b.at[0, :, lane]) for a, b in pairs]

    copy_all(small(), small_sems, 0)

    def fetch(i, carry):
        @pl.when(odd == 0)
        def even_halos():
            copy_all(halos(i)[0], in_sems, i)

        @pl.when(odd == 1)
        def odd_halos():
            copy_all(halos(i)[1], in_sems, i)

        for n, (source, target) in enumerate(inputs(i)):
            pltpu.make_async_copy(source, target, in_sems.at[i, n + 2]).start()
        return carry

    lax.fori_loop(0, count, fetch, 0)

    def arrive(i):
        copy_all(halos(i)[0], in_sems, i, wait=True)
        for n, (source, target) in enumerate(inputs(i)):
            pltpu.make_async_copy(source, target, in_sems.at[i, n + 2]).wait()

    copy_all(small(), small_sems, 0, wait=True)
    arrive(0)

    row = lax.broadcasted_iota(jnp.int32, (TAPS, TAPS), 0)
    col = lax.broadcasted_iota(jnp.int32, (TAPS, TAPS), 1)
    own_ids = (ids_ref[...] + 1).astype(F32)
    prev_ids = prev_ref[0, LANES + 16 : LANES + 32, :].astype(F32)
    next_ids = next_ref[0, LANES + 32 : LANES + 48, :].astype(F32)
    for b in range(blocks):
        idr[b : b + 1, :] = prev_ids[EDGE + b : EDGE + b + 1]
        idr[blocks + b : blocks + b + 1, :] = own_ids[:, TAPS * b : TAPS * (b + 1)]
        idr[2 * blocks + b : 2 * blocks + b + 1, :] = next_ids[EDGE + b : EDGE + b + 1]
    for b in range(3 * blocks):
        idc[TAPS * b : TAPS * (b + 1), :] = spread(idr[b : b + 1, :])

    def short_masks(i, carry):
        base = pl.multiple_of(frame + EDGE * i, EDGE)
        here = idc[pl.ds(base, EDGE), :]
        for j in range(1, SHORT):
            mj[j - 1, pl.ds(base, EDGE), :] = (here == idc[pl.ds(base - j, EDGE), :]).astype(F32)
        return carry

    lax.fori_loop(0, (rows + 2 * EDGE) // EDGE, short_masks, 0)

    def same(t_block, s_block, length):
        start = frame + TAPS * t_block
        line = idr[blocks + s_block : blocks + s_block + 1, :]
        return (idc[start : start + length, :] == line).astype(F32)

    lower = (row >= col).astype(F32)
    upper = 1.0 - lower
    flip[...] = (row + col == TAPS - 1).astype(BF16)
    for b in range(blocks):
        ml[b] = (same(b, b, TAPS) * lower).astype(BF16)
    for b in range(blocks + 1):
        ml[blocks + b] = (same(b, b - 1, TAPS) * upper).astype(BF16)
    mn[0] = (same(blocks, blocks, 16) * lower[:16]).astype(BF16)
    mn[1] = (same(blocks, blocks, 16) * (row <= col).astype(F32)[:16]).astype(BF16)
    mn[2] = (same(blocks, blocks + 1, 16) * (row > col).astype(F32)[:16]).astype(BF16)
    for b in range(blocks):
        both = same(b, b, TAPS) * lower + same(b, b - 1, TAPS) * upper
        mp[b] = dot(both.astype(BF16), flip[...], NN)
    negated = jnp.logical_or(row + col == TAPS, row + col == 0).astype(BF16)
    reversed_taps = dot(filters_ref[...], negated, NN)
    forward_taps = filters_ref[...].astype(F32)
    for i in range(count):
        taps_ref[i, :, 0:TAPS] = reversed_taps[per * i : per * (i + 1)]
        taps_ref[i, :, TAPS:] = forward_taps[per * i : per * (i + 1)]

    lane_group = col // GROUP
    lower_flipped = row + col >= TAPS - 1
    first_lanes = col < EDGE
    blank = jnp.zeros((TAPS - EDGE, LANES), F32)

    def turned(x):
        return jnp.concatenate([x, blank], axis=0).T.astype(BF16)

    def filters_of(i):
        return [[w_ref[n, j : j + 1, lanes_of(i)] for j in range(SHORT)] for n in range(3)]

    def long_steps(i):
        w = filters_of(i)
        prev_kv = prev_ref[i, LANES : LANES + 16, :].astype(F32)
        prev_q = prev_ref[i, LANES + 16 : LANES + 32, :].astype(F32)
        next_qg = next_ref[i, LANES : LANES + 16, :].astype(F32)
        next_kv = next_ref[i, LANES + 16 : LANES + 32, :].astype(F32)
        next_dz = next_ref[i, LANES + 32 : LANES + 48, :].astype(F32)
        for n, (source, before, after) in enumerate(
            (
                (bq, prev_q[:EDGE], next_qg[:EDGE]),
                (bk, prev_kv[:EDGE], next_kv[:EDGE]),
                (bv, prev_kv[EDGE:], next_kv[EDGE:]),
            )
        ):
            edges[n, 0, 0:EDGE] = before
            edges[n, 0, EDGE : 2 * EDGE] = source[i, 0:16, :].astype(F32)[:EDGE]
            edges[n, 1, 0:EDGE] = source[i, rows - 16 : rows, :].astype(F32)[EDGE:]
            edges[n, 1, EDGE : 2 * EDGE] = after

        def convolve(n, m):
            low = frame + rows * m
            total = w[n][0] * edges[n, m, EDGE : 2 * EDGE]
            for j in range(1, SHORT):
                mask = mj[j - 1, low : low + EDGE, :]
                total += w[n][j] * (mask * edges[n, m, EDGE - j : 2 * EDGE - j])
            return total

        upstream = (bg[i, 0:16, :].astype(F32)[:EDGE], next_qg[EDGE:])
        fixed = []
        for m in range(2):
            query, key, value = [convolve(n, m) for n in range(3)]
            fixed.append((key, value, key * value, upstream[m] * query))

        ut[:, 0:TAPS] = prev_ref[i, 0:LANES, :]
        ut[:, TAPS : TAPS + rows] = turn_ref[i, 0:LANES, :]
        ut[:, TAPS : 2 * TAPS] = jnp.where(
            first_lanes, turned(fixed[0][2]), turn_ref[i, 0:LANES, 0:TAPS]
        )
        ut[:, TAPS + rows : 2 * TAPS + rows] = turned(fixed[1][2])
        dzt[:, TAPS:rows] = turn_ref[i, LANES:, TAPS:rows]
        dzt[:, 0:TAPS] = jnp.where(first_lanes, turned(fixed[0][3]), turn_ref[i, LANES:, 0:TAPS])
        dzt[:, rows : rows + TAPS] = jnp.where(
            first_lanes, turned(fixed[1][3]), next_ref[i, 0:LANES, :]
        )
        dzt[:, rows + TAPS :] = turned(next_dz[:EDGE])
        dzr[...] = dzr_ref[i]
        rest = dzr_ref[i, 0:16, :].astype(F32)[EDGE:]
        dzr[0:16] = jnp.concatenate([fixed[0][3], rest], axis=0).astype(BF16)
        for b in range(blocks + 1):
            here = slice(TAPS * b, TAPS * (b + 1))
            utr[:, here] = dot(ut[:, here], flip[...], NN).astype(BF16)

        def one_group(n):
            c = slice(GROUP * n, GROUP * (n + 1))
            line = jnp.broadcast_to(taps_ref[i, n : n + 1, 0:TAPS], (TAPS, TAPS))
            band = pltpu.roll(line, 0, 1, stride=1, stride_axis=0).astype(BF16)
            line = jnp.broadcast_to(taps_ref[i, n : n + 1, TAPS:], (16, TAPS))
            other = pltpu.roll(line, 0, 1, stride=1, stride_axis=0).astype(BF16)
            near = [band * ml[b] for b in range(blocks)]
            far = [band * ml[blocks + b] for b in range(blocks + 1)]
            for b in range(blocks):
                window = slice(TAPS * b, TAPS * (b + 2))
                here = slice(TAPS * b, TAPS * (b + 1))
                zt[c, here] = dot(ut[c, window], jnp.concatenate([far[b], near[b]], axis=1), NT)
                dut[c, here] = dot(dzt[c, window], jnp.concatenate([near[b], far[b + 1]], axis=0), NN)
            window = slice(TAPS * blocks, TAPS * (blocks + 2))
            here = slice(TAPS * blocks, TAPS * blocks + 16)
            edge = jnp.concatenate([far[blocks][:16], band[:16] * mn[0]], axis=1)
            zt[c, here] = dot(ut[c, window], edge, NT)
            edge = jnp.concatenate([other * mn[1], other * mn[2]], axis=1)
            dut[c, here] = dot(dzt[c, window], edge, NT)
            total = None
            for b in range(blocks):
                here = slice(TAPS * b, TAPS * (b + 1))
                mine = jnp.where(lane_group == n, dzr[here, :], jnp.zeros((), BF16))
                pairs = dot(mine, utr[:, TAPS * b : TAPS * (b + 2)], NN)
                term = jnp.where(lower_flipped, pairs[:, TAPS:], pairs[:, :TAPS]) * mp[b]
                total = term if total is None else total + term
            skewed = pltpu.roll(total, 1, 1, stride=1, stride_axis=0)
            gl[n : n + 1, :] = jnp.sum(skewed, axis=0, keepdims=True)

        def close():
            for b in range(blocks + 1):
                length = TAPS if b < blocks else EDGE
                here = slice(TAPS * b, TAPS * b + length)
                z = zt[:, TAPS * b : TAPS * (b + 1)].T[:length]
                du = dut[:, TAPS * b : TAPS * (b + 1)].T[:length]
                if b < blocks:
                    dq[here, :] = bg[i, here, :].astype(F32) * z
                    dk[here, :] = du * conv_ref[i, 1, here, :]
                    dv[here, :] = du * conv_ref[i, 0, here, :]
                else:
                    dq[here, :] = upstream[1] * z
                if b in (0, blocks):
                    key, value = fixed[0 if b == 0 else 1][:2]
                    there = slice(TAPS * b, TAPS * b + EDGE)
                    dk[there, :] = du[:EDGE] * value
                    dv[there, :] = du[:EDGE] * key
            part_ref[24:32, lanes_of(i)] = gl[...] * long_scale

        return one_group, close

    part = rows // per

    def finish_steps(i):
        w = filters_of(i)
        sums = [None] * (3 * SHORT)

        def one_part(m):
            low = part * m
            for n, (grad, source, out) in enumerate(
                ((dq, bq, oq_ref), (dk, bk, ok_ref), (dv, bv, ov_ref))
            ):
                x = source[i, low : low + part, :].astype(F32)
                total = None
                for j in range(SHORT):
                    piece = grad[low + j : low + j + part, :]
                    if j:
                        start = low + frame + j
                        piece = piece * mj[j - 1, start : start + part, :]
                    total = w[n][j] * piece if total is None else total + w[n][j] * piece
                    fresh = jnp.sum((x * piece).reshape(part // 8, 8, LANES), axis=0)
                    at = SHORT * n + j
                    sums[at] = fresh if m == 0 else sums[at] + fresh
                out[i, low : low + part, :] = total.astype(BF16)

        def close():
            lines = [jnp.sum(s, axis=0, keepdims=True) * short_scale for s in sums]
            lines.append(jnp.zeros((24 - 3 * SHORT, LANES), F32))
            part_ref[0:24, lanes_of(i)] = jnp.concatenate(lines, axis=0)
            copy_all(outputs(i), out_sems, i)

        return one_part, close

    one_group, close = long_steps(0)
    for n in range(per):
        one_group(n)
    close()

    def both(i, carry):
        arrive(i)
        one_group, close_long = long_steps(i)
        one_part, close_finish = finish_steps(i - 1)
        for n in range(per):
            one_group(n)
            one_part(n)
        close_finish()
        close_long()
        return carry

    lax.fori_loop(1, count, both, 0)
    one_part, close = finish_steps(count - 1)
    for n in range(per):
        one_part(n)
    close()

    def drain(i, carry):
        copy_all(outputs(i), out_sems, i, wait=True)
        return carry

    lax.fori_loop(0, count, drain, 0)


def mixer(operands, rows, channels, scales):
    blocks = rows // TAPS
    count = channels // LANES
    ids, filters, short_filter = operands[:3]
    vm = lambda *shape: pltpu.VMEM(shape, F32)
    vb = lambda *shape: pltpu.VMEM(shape, BF16)
    out = jax.ShapeDtypeStruct((1, rows, channels), BF16)
    buffered = [vb(count, rows, LANES)] * 4
    return pl.pallas_call(
        functools.partial(mixer_kernel, rows, *scales),
        in_specs=[HBM] * len(operands),
        out_specs=[HBM, HBM, HBM, VMEM],
        out_shape=[out, out, out, jax.ShapeDtypeStruct((32, channels), F32)],
        scratch_shapes=[
            pltpu.VMEM(ids.shape, jnp.int32),
            vb(*filters.shape),
            vm(*short_filter.shape),
            vb(count, HEAD_ROWS, LANES),
            vb(count, HEAD_ROWS, LANES),
            *buffered,
            vm(count, 2, rows, LANES),
            vb(count, 2 * LANES, rows),
            vb(count, rows, LANES),
            *buffered[:3],
            vm(count, LANES // GROUP, 2 * TAPS),
            vm(8, LANES),
            vm(3 * rows, LANES),
            vm(SHORT - 1, 3 * rows, LANES),
            vb(2 * blocks + 1, TAPS, TAPS),
            vb(3, 16, TAPS),
            vm(blocks, TAPS, TAPS),
            vb(TAPS, TAPS),
            vm(3, 2, 2 * EDGE, LANES),
            vb(LANES, rows + 2 * TAPS),
            vb(LANES, rows + TAPS),
            vb(LANES, rows + 2 * TAPS),
            vb(rows, LANES),
            vm(LANES, rows + TAPS),
            vm(LANES, rows + TAPS),
            vm(rows + 16, LANES),
            vm(rows + 16, LANES),
            vm(rows + 16, LANES),
            vm(8, LANES),
            pltpu.SemaphoreType.DMA((1, 3)),
            pltpu.SemaphoreType.DMA((count, 9)),
            pltpu.SemaphoreType.DMA((count, 3)),
        ],
        compiler_params=pltpu.CompilerParams(vmem_limit_bytes=63 << 20),
        name="mixer",
    )(*operands)


def total_over(x, axis):
    size = lax.axis_size(axis)
    if size & (size - 1):
        return lax.psum(x, axis)
    bit = 1
    while bit < size:
        x = x + lax.ppermute(x, axis, [(i, i ^ bit) for i in range(size)])
        bit *= 2
    return x


def all_taps(long_filter):
    if lax.axis_size("fsdp") != 2:
        return lax.all_gather(long_filter, "fsdp", axis=1, tiled=True)
    other = lax.ppermute(long_filter, "fsdp", [(0, 1), (1, 0)])
    first = lax.axis_index("fsdp") == 0
    return jnp.where(
        first,
        jnp.concatenate([long_filter, other], axis=1),
        jnp.concatenate([other, long_filter], axis=1),
    )


def body(q_in, k_in, v_in, grad_out, genome_ids, long_filter, short_filter):
    rows, channels = q_in.shape[1:]
    seq_count = lax.axis_size("fsdp")
    length = rows * lax.axis_size("ctx")
    filters = all_taps(long_filter)
    groups = filters.shape[0]
    conv, turn, dzr, near, far = local_part(
        genome_ids, short_filter, q_in, k_in, v_in, grad_out
    )
    near, far = swapped(near, far, "ctx")
    scales = (
        1.0 / math.sqrt(seq_count * length * (channels // groups)),
        1.0 / math.sqrt(seq_count * length),
    )
    operands = (
        genome_ids, filters, short_filter, near, far, q_in, k_in, v_in, grad_out, conv, turn, dzr,
    )
    out_q, out_k, out_v, sums = mixer(operands, rows, channels, scales)
    sums = total_over(total_over(sums, "ctx"), "fsdp")
    grad_short = sums[: 3 * SHORT].reshape(3, SHORT, channels)
    grad_long = sums[24:].reshape(8, channels // LANES, LANES).transpose(1, 0, 2)
    grad_long = grad_long.reshape(groups, TAPS)
    own = TAPS // seq_count
    grad_long = lax.dynamic_slice_in_dim(grad_long, lax.axis_index("fsdp") * own, own, 1)
    return out_q, out_k, out_v, grad_long, grad_short


def solution(mesh):
    return jax.shard_map(
        body,
        mesh=mesh,
        in_specs=(
            P("fsdp", "ctx", "tp"),
            P("fsdp", "ctx", "tp"),
            P("fsdp", "ctx", "tp"),
            P("fsdp", "ctx", "tp"),
            P("fsdp", "ctx"),
            P("tp", "fsdp"),
            P(None, None, "tp"),
        ),
        out_specs=(
            P("fsdp", "ctx", "tp"),
            P("fsdp", "ctx", "tp"),
            P("fsdp", "ctx", "tp"),
            P("tp", "fsdp"),
            P(None, None, "tp"),
        ),
        check_vma=False,
    )
```

time: 64.1 us -> 51.4 us (0.80)
  local copies, waits for them, and re-layouts: 8.53 us -> 2.22 us
  blocking collectives: 4.69 us -> 0 us
  other arithmetic: 2.48 us -> 1.65 us
    all_gather x1 -> x0, blocking collectives: 4.69 us -> none  [body(): lax.all_gather(long_filter, 'fsdp', axis=1, tiled=True).astype(F32)]
    unnamed x17 -> x6, local copies, waits for them, and re-layouts: 3.69 us -> 0.86 us
    squeeze x2 -> x0, local copies, waits for them, and re-layouts: 1.85 us -> none  [the longest x1 1.09 us: body(): v_in[0, rows - REACH:]]
    ppermute x3, waiting for transfers between devices: 10 us -> 8.21 us  [total_over(): x = x + lax.ppermute(x, axis, [(i, i ^ bit) for i in range(size)])]
    concatenate x2 -> x0, other arithmetic: 1.73 us -> none  [the longest x1 0.89 us: body(): jnp.concatenate([k_in[0, rows - REACH:], v_in[0, rows - REACH:], q_in[0,...]
    ppermute x2 -> x3, waiting for transfers between devices: 0.01 us -> 1.72 us  [the longest x1 1.72 us: all_taps(): other = lax.ppermute(long_filter, 'fsdp', [(0, 1), (1, 0)])]
    add x3, other arithmetic: 0.05 us -> 0.96 us  [total_over(): x = x + lax.ppermute(x, axis, [(i, i ^ bit) for i in range(size)])]
    convert_element_type x4 -> x0, other arithmetic: 0.7 us -> none  [the longest x1 0.68 us: body(): ids.astype(F32)]
  transfers between devices with their start and end apart: 5 -> 6, of which waited for: 3 -> 4; matrix products, arithmetic and copies ran while one was open for 8% -> 1% of each run, Pallas kernels for 0% -> 0%
where the time goes in v1:
time: 51.4 us; the launch traced here: 51.2 us
  Pallas kernels  24.6 us (48%)
  starting transfers between devices  12 us (23%)
  waiting for transfers between devices  9.94 us (19%)
  local copies, waits for them, and re-layouts  2.22 us (4%)
  other arithmetic  1.65 us (3%)
  between operations  0.71 us (1%)
    pallas_call x1, Pallas kernels, mixer(): pl.pallas_call(functools.partial(mixer_kernel, rows, *scales), in_specs=[...  17.6 us
    ppermute x3, starting transfers between devices, total_over(): x = x + lax.ppermute(x, axis, [(i, i ^ bit) for i in range(size)])  8.28 us
    ppermute x3, waiting for transfers between devices, total_over(): x = x + lax.ppermute(x, axis, [(i, i ^ bit) for i in range(size)])  8.21 us
    pallas_call x1, Pallas kernels, local_part(): pl.pallas_call(functools.partial(local_kernel, rows), in_specs=[HBM] * 6,...  7.08 us
    ppermute x1, starting transfers between devices, all_taps(): other = lax.ppermute(long_filter, 'fsdp', [(0, 1), (1, 0)])  2.58 us
    ppermute x1, waiting for transfers between devices, all_taps(): other = lax.ppermute(long_filter, 'fsdp', [(0, 1), (1, 0)])  1.72 us
  transfers between devices with their start and end apart: 6, of which 4 were waited for; matrix products, arithmetic and copies ran while one was open for 1% of the time, Pallas kernels for 0%

profile of v1, /device:TPU:0, one launch (start us, length us, event | category | flops | bytes accessed | tf_op | source)
XLA Modules:
  0.0 51.2 jit_solution(6139896126303725025)
XLA Ops:
  0.6 0.0 copy-start.2
  0.6 7.1 %local_part.1 = (f32[8,2,256,128]{3,2,1,0:T(8,128)}, bf16[8,256,256]{2,1,0:T(8,128)(2,1)}, bf16[8,256,128]{2,1,0:T(8,128)(2,1)}, bf16[8,176,128]{2,1,0:T(8,128)(2,1)}, bf16[8,176,128]{2,1,0:T(8,128)(2,1)}) custom-call(s32[1,256]{1,0:T(1,128)} %ids_hbm.3, f32[3,7,1024]{2,1,0:T(8,128)} %w_hbm.3, bf16[1,256,1024]{2,1,0:T(8,128)(2,1)} %q_hbm.3, ...), custom_call_target="tpu_custom_call" | custom-call | tf_op jit(solution)/shard_map/local_part/pallas_call | solution.py:219
  7.7 0.5 %collective-permute-start.1 = (bf16[8,176,128]{2,1,0:T(8,128)(2,1)}, bf16[8,176,128]{2,1,0:T(8,128)(2,1)S(1)}, u32[]{:S(2)}, u32[]{:S(2)}) collective-permute-start(bf16[8,176,128]{2,1,0:T(8,128)(2,1)} %get-tuple-element.14), channel_id=1, source_target_pairs={{0,4},{4,0},{8,12},{12,8},{1,5},{5,1},{9,13},{13,9},{2,6},{6,2},{1... | collective-permute-start | bytes 1081352 | tf_op jit(solution)/shard_map/ppermute | solution.py:30
  8.2 0.7 %collective-permute-start.2 = (bf16[8,176,128]{2,1,0:T(8,128)(2,1)}, bf16[8,176,128]{2,1,0:T(8,128)(2,1)S(1)}, u32[]{:S(2)}, u32[]{:S(2)}) collective-permute-start(bf16[8,176,128]{2,1,0:T(8,128)(2,1)} %get-tuple-element.15), channel_id=1, source_target_pairs={{8,4},{4,8},{9,5},{5,9},{10,6},{6,10},{11,7},{7,11},{24,20},{20,24... | collective-permute-start | bytes 1081352 | tf_op jit(solution)/shard_map/ppermute | solution.py:30
  8.9 0.0 copy-done.2
  8.9 2.6 %collective-permute-start = (bf16[64,64]{1,0:T(8,128)(2,1)S(1)}, bf16[64,64]{1,0:T(8,128)(2,1)S(1)}, u32[]{:S(2)}, u32[]{:S(2)}) collective-permute-start(bf16[64,64]{1,0:T(8,128)(2,1)S(1)} %copy-done.2), channel_id=1, source_target_pairs={{0,16},{16,0},{1,17},{17,1},{2,18},{18,2},{3,19},{19,3},{4,20},{20... | collective-permute-start | bytes 24584 | tf_op jit(solution)/shard_map/ppermute | solution.py:646
  11.5 1.7 %collective-permute-done = bf16[64,64]{1,0:T(8,128)(2,1)S(1)} collective-permute-done((bf16[64,64]{1,0:T(8,128)(2,1)S(1)}, bf16[64,64]{1,0:T(8,128)(2,1)S(1)}, u32[]{:S(2)}, u32[]{:S(2)}) %collective-permute-start) | collective-permute-done | bytes 8224 | tf_op jit(solution)/shard_map/ppermute | solution.py:646
  13.2 0.7 %maximum_select_fusion.filters_hbm = bf16[64,128]{1,0:T(8,128)(2,1)} fusion(bf16[64,64]{1,0:T(8,128)(2,1)S(1)} %collective-permute-done, bf16[64,64]{1,0:T(8,128)(2,1)S(1)} %copy-done.2, pred[]{:T(512)S(6)} %eq.3), kind=kLoop, calls=%fused_computation.1 | loop fusion | flops 73728 | bytes 32769 | tf_op jit(solution)/shard_map/jit(_where)/select_n | solution.py:648
  13.9 0.0 collective-permute-done.1.near_hbm
  13.9 0.0 copy-start
  13.9 0.0 collective-permute-done.2.far_hbm
  13.9 0.0 copy-start.1
  13.9 0.7 %copy-done = bf16[8,176,128]{2,1,0:T(8,128)(2,1)} copy-done((bf16[8,176,128]{2,1,0:T(8,128)(2,1)}, bf16[8,176,128]{2,1,0:T(8,128)(2,1)S(1)}, u32[]{:S(2)}) %copy-start) | copy-done | bytes 360472
  14.7 0.1 copy-done.1
  14.8 17.6 %mixer.1 = (bf16[1,256,1024]{2,1,0:T(8,128)(2,1)}, bf16[1,256,1024]{2,1,0:T(8,128)(2,1)}, bf16[1,256,1024]{2,1,0:T(8,128)(2,1)}, f32[32,1024]{1,0:T(8,128)}) custom-call(s32[1,256]{1,0:T(1,128)} %ids_hbm.3, bf16[64,128]{1,0:T(8,128)(2,1)} %maximum_select_fusion.filters_hbm, f32[3,7,1024]{2,1,0:T(8,128)} %w_hbm.3, bf16[8,176,128]{2,1,0:T(8,128)(2,1)} %copy-done, ...), custom_call_target="tpu_custom_call" | custom-call | tf_op jit(solution)/shard_map/mixer/pallas_call | solution.py:588
  32.4 4.1 %collective-permute-start.3 = (f32[32,1024]{1,0:T(8,128)}, f32[32,1024]{1,0:T(8,128)S(1)}, u32[]{:S(2)}, u32[]{:S(2)}) collective-permute-start(f32[32,1024]{1,0:T(8,128)} %get-tuple-element.22), channel_id=1, source_target_pairs={{0,4},{4,0},{8,12},{12,8},{1,5},{5,1},{9,13},{13,9},{2,6},{6,2},{1... | collective-permute-start | bytes 393224 | tf_op jit(solution)/shard_map/ppermute | solution.py:638
  36.5 1.2 %collective-permute-done.3 = f32[32,1024]{1,0:T(8,128)S(1)} collective-permute-done((f32[32,1024]{1,0:T(8,128)}, f32[32,1024]{1,0:T(8,128)S(1)}, u32[]{:S(2)}, u32[]{:S(2)}) %collective-permute-start.3) | collective-permute-done | bytes 131104 | tf_op jit(solution)/shard_map/ppermute | solution.py:638
  37.7 0.9 %add.12 = f32[32,1024]{1,0:T(8,128)S(1)} add(f32[32,1024]{1,0:T(8,128)} %get-tuple-element.22, f32[32,1024]{1,0:T(8,128)S(1)} %collective-permute-done.3) | non-fusion elementwise | flops 32768 | bytes 393216 | tf_op jit(solution)/shard_map/add | solution.py:638
  38.6 2.0 %collective-permute-start.4 = (f32[32,1024]{1,0:T(8,128)S(1)}, f32[32,1024]{1,0:T(8,128)S(1)}, u32[]{:S(2)}, u32[]{:S(2)}) collective-permute-start(f32[32,1024]{1,0:T(8,128)S(1)} %add.12), channel_id=1, source_target_pairs={{0,8},{4,12},{8,0},{12,4},{1,9},{5,13},{9,1},{13,5},{2,10},{6,14},... | collective-permute-start | bytes 393224 | tf_op jit(solution)/shard_map/ppermute | solution.py:638
  40.7 3.8 %collective-permute-done.4 = f32[32,1024]{1,0:T(8,128)S(1)} collective-permute-done((f32[32,1024]{1,0:T(8,128)S(1)}, f32[32,1024]{1,0:T(8,128)S(1)}, u32[]{:S(2)}, u32[]{:S(2)}) %collective-permute-start.4) | collective-permute-done | bytes 131104 | tf_op jit(solution)/shard_map/ppermute | solution.py:638
  44.5 2.1 %collective-permute-start.5 = (f32[32,1024]{1,0:T(8,128)S(1)}, f32[32,1024]{1,0:T(8,128)S(1)}, u32[]{:S(2)}, u32[]{:S(2)}) collective-permute-start(f32[32,1024]{1,0:T(8,128)S(1)} %add.13), channel_id=1, source_target_pairs={{0,16},{16,0},{1,17},{17,1},{2,18},{18,2},{3,19},{19,3},{4,20},{20... | collective-permute-start | bytes 393224 | tf_op jit(solution)/shard_map/ppermute | solution.py:638
  46.6 3.2 %collective-permute-done.5 = f32[32,1024]{1,0:T(8,128)S(1)} collective-permute-done((f32[32,1024]{1,0:T(8,128)S(1)}, f32[32,1024]{1,0:T(8,128)S(1)}, u32[]{:S(2)}, u32[]{:S(2)}) %collective-permute-start.5) | collective-permute-done | bytes 131104 | tf_op jit(solution)/shard_map/ppermute | solution.py:638
  49.9 0.7 %reshape.21 = f32[3,7,1024]{2,1,0:T(8,128)} reshape(f32[21,1024]{1,0:T(8,128)S(1)} %slice.9) | data formatting | bytes 172032 | tf_op jit(solution)/shard_map/reshape | solution.py:674
  50.5 0.7 %constant_dynamic-slice_fusion = f32[64,64]{1,0:T(8,128)} fusion(f32[64,128]{1,0:T(8,128)S(1)} %slice_bitcast_fusion, s32[]{:T(128)S(6)} %select_n.13), kind=kLoop, calls=%fused_computation.2 | loop fusion | bytes 32772 | tf_op jit(solution)/shard_map/dynamic_slice | solution.py:678
  (4 shorter events, 0.0 us)
Async XLA Ops:
  0.6 8.3 %copy-start.2 = (bf16[64,64]{1,0:T(8,128)(2,1)S(1)}, bf16[64,64]{1,0:T(8,128)(2,1)}, u32[]{:S(2)}) copy-start(bf16[64,64]{1,0:T(8,128)(2,1)} %param.12) | copy-start | bytes 24580
  7.7 6.2 %collective-permute-start.1 = (bf16[8,176,128]{2,1,0:T(8,128)(2,1)}, bf16[8,176,128]{2,1,0:T(8,128)(2,1)S(1)}, u32[]{:S(2)}, u32[]{:S(2)}) collective-permute-start(bf16[8,176,128]{2,1,0:T(8,128)(2,1)} %get-tuple-element.14), channel_id=1, source_target_pairs={{0,4},{4,0},{8,12},{12,8},{1,5},{5,1},{9,13},{13,9},{2,6},{6,2},{1... | collective-permute-start | bytes 1081352 | tf_op jit(solution)/shard_map/ppermute | solution.py:30
  8.2 5.7 %collective-permute-start.2 = (bf16[8,176,128]{2,1,0:T(8,128)(2,1)}, bf16[8,176,128]{2,1,0:T(8,128)(2,1)S(1)}, u32[]{:S(2)}, u32[]{:S(2)}) collective-permute-start(bf16[8,176,128]{2,1,0:T(8,128)(2,1)} %get-tuple-element.15), channel_id=1, source_target_pairs={{8,4},{4,8},{9,5},{5,9},{10,6},{6,10},{11,7},{7,11},{24,20},{20,24... | collective-permute-start | bytes 1081352 | tf_op jit(solution)/shard_map/ppermute | solution.py:30
  8.9 4.3 %collective-permute-start = (bf16[64,64]{1,0:T(8,128)(2,1)S(1)}, bf16[64,64]{1,0:T(8,128)(2,1)S(1)}, u32[]{:S(2)}, u32[]{:S(2)}) collective-permute-start(bf16[64,64]{1,0:T(8,128)(2,1)S(1)} %copy-done.2), channel_id=1, source_target_pairs={{0,16},{16,0},{1,17},{17,1},{2,18},{18,2},{3,19},{19,3},{4,20},{20... | collective-permute-start | bytes 24584 | tf_op jit(solution)/shard_map/ppermute | solution.py:646
  13.9 0.8 %copy-start = (bf16[8,176,128]{2,1,0:T(8,128)(2,1)}, bf16[8,176,128]{2,1,0:T(8,128)(2,1)S(1)}, u32[]{:S(2)}) copy-start(bf16[8,176,128]{2,1,0:T(8,128)(2,1)S(1)} %collective-permute-done.1.near_hbm) | copy-start | bytes 1081348
  13.9 0.9 %copy-start.1 = (bf16[8,176,128]{2,1,0:T(8,128)(2,1)}, bf16[8,176,128]{2,1,0:T(8,128)(2,1)S(1)}, u32[]{:S(2)}) copy-start(bf16[8,176,128]{2,1,0:T(8,128)(2,1)S(1)} %collective-permute-done.2.far_hbm) | copy-start | bytes 1081348
  32.4 5.3 %collective-permute-start.3 = (f32[32,1024]{1,0:T(8,128)}, f32[32,1024]{1,0:T(8,128)S(1)}, u32[]{:S(2)}, u32[]{:S(2)}) collective-permute-start(f32[32,1024]{1,0:T(8,128)} %get-tuple-element.22), channel_id=1, source_target_pairs={{0,4},{4,0},{8,12},{12,8},{1,5},{5,1},{9,13},{13,9},{2,6},{6,2},{1... | collective-permute-start | bytes 393224 | tf_op jit(solution)/shard_map/ppermute | solution.py:638
  38.6 5.9 %collective-permute-start.4 = (f32[32,1024]{1,0:T(8,128)S(1)}, f32[32,1024]{1,0:T(8,128)S(1)}, u32[]{:S(2)}, u32[]{:S(2)}) collective-permute-start(f32[32,1024]{1,0:T(8,128)S(1)} %add.12), channel_id=1, source_target_pairs={{0,8},{4,12},{8,0},{12,4},{1,9},{5,13},{9,1},{13,5},{2,10},{6,14},... | collective-permute-start | bytes 393224 | tf_op jit(solution)/shard_map/ppermute | solution.py:638
  44.5 5.3 %collective-permute-start.5 = (f32[32,1024]{1,0:T(8,128)S(1)}, f32[32,1024]{1,0:T(8,128)S(1)}, u32[]{:S(2)}, u32[]{:S(2)}) collective-permute-start(f32[32,1024]{1,0:T(8,128)S(1)} %add.13), channel_id=1, source_target_pairs={{0,16},{16,0},{1,17},{17,1},{2,18},{18,2},{3,19},{19,3},{4,20},{20... | collective-permute-start | bytes 393224 | tf_op jit(solution)/shard_map/ppermute | solution.py:638

commit v2 on v1

v2 whole, which is shorter than its diff:
```python
import functools
import math

import jax
import jax.numpy as jnp
from jax import lax
from jax.experimental import pallas as pl
from jax.experimental.pallas import tpu as pltpu
from jax.sharding import PartitionSpec as P

TAPS = 128
SHORT = 7
LANES = 128
GROUP = 16
EDGE = 8
VMEM_LIMIT = 63 << 20
HEAD_ROWS = LANES + 48
F32 = jnp.float32
BF16 = jnp.bfloat16
NT = (((1,), (1,)), ((), ()))
NN = (((1,), (0,)), ((), ()))
VMEM = pl.BlockSpec(memory_space=pltpu.VMEM)
HBM = pl.BlockSpec(memory_space=pltpu.HBM)


def swapped(near, far, axis):
    size = lax.axis_size(axis)
    near_route = [(i, i ^ 1) for i in range(size) if i ^ 1 < size]
    far_route = [(i + 1, i) for i in range(1, size - 1, 2)]
    far_route = far_route + [(i, j) for j, i in far_route]
    return lax.ppermute(near, axis, near_route), lax.ppermute(far, axis, far_route)


def dot(a, b, dims):
    return lax.dot_general(a, b, dims, preferred_element_type=F32)


def lanes_of(i):
    return pl.ds(pl.multiple_of(i * LANES, LANES), LANES)


def spread(line):
    return jnp.broadcast_to(line, (TAPS, TAPS)).T


def copy_all(pairs, sems, i, wait=False):
    for n, (source, target) in enumerate(pairs):
        copy = pltpu.make_async_copy(source, target, sems.at[i, n])
        if wait:
            copy.wait()
        else:
            copy.start()


def half_kernel(
    rows,
    edge,
    ids_hbm,
    w_hbm,
    q_hbm,
    k_hbm,
    v_hbm,
    g_hbm,
    conv_hbm,
    dzr_hbm,
    one_hbm,
    two_hbm,
    ids_ref,
    w_ref,
    bq,
    bk,
    bv,
    bg,
    conv_ref,
    dzr_ref,
    one_ref,
    two_ref,
    idc,
    mj,
    xq,
    xk,
    xv,
    uf,
    dzf,
    small_sems,
    in_sems,
    out_sems,
    packet_sems,
):
    count = q_hbm.shape[2] // LANES
    odd = lax.rem(lax.axis_index("ctx"), 2)
    kv_low, q_low = (TAPS, 0) if edge else (0, TAPS)
    lead = 16

    def small():
        return ((ids_hbm, ids_ref), (w_hbm, w_ref))

    def inputs(i):
        lane = lanes_of(i)
        pairs = ((q_hbm, bq), (k_hbm, bk), (v_hbm, bv), (g_hbm, bg))
        return [(a.at[0, :, lane], b.at[:, lane]) for a, b in pairs]

    def outputs(i):
        pairs = [(conv_ref, conv_hbm), (dzr_ref, dzr_hbm)]
        return [(a.at[i], b.at[i]) for a, b in pairs]

    def packets(i):
        one, two = one_ref.at[i], two_ref.at[i]
        near, far = one_hbm.at[i], two_hbm.at[i]
        return ((one, near), (two, far)), ((two, near), (one, far))

    def send_packets(i):
        if not edge:
            copy_all(packets(i)[0], packet_sems, i)
            return

        @pl.when(odd == 0)
        def even_packets():
            copy_all(packets(i)[0], packet_sems, i)

        @pl.when(odd == 1)
        def odd_packets():
            copy_all(packets(i)[1], packet_sems, i)

    copy_all(small(), small_sems, 0)

    def fetch(i, carry):
        copy_all(inputs(i), in_sems, i)
        return carry

    lax.fori_loop(0, count, fetch, 0)
    copy_all(small(), small_sems, 0, wait=True)
    ids = (ids_ref[...] + 1).astype(F32)
    idc[0:EDGE] = jnp.zeros((EDGE, LANES), F32)
    for b in range(2):
        idc[EDGE + TAPS * b : EDGE + TAPS * (b + 1)] = spread(ids[:, TAPS * b : TAPS * (b + 1)])
    for x in (xq, xk, xv):
        x[0:lead] = jnp.zeros((lead, LANES), F32)

    def masks(i, carry):
        base = pl.multiple_of(16 * i, 16)
        here = idc[pl.ds(base + EDGE, 16), :]
        for j in range(1, SHORT):
            mj[j - 1, pl.ds(base, 16), :] = (here == idc[pl.ds(base + EDGE - j, 16), :]).astype(F32)
        return carry

    lax.fori_loop(0, rows // 16, masks, 0)
    pad = jnp.zeros((EDGE - 2, LANES), F32)
    id_rows = [ids[:, TAPS * b : TAPS * (b + 1)] for b in range(2)]
    id_tile = jnp.concatenate(id_rows + [pad], axis=0)
    part = 32

    def pair(a, b):
        return jnp.concatenate([a, b], axis=0).astype(BF16)

    def one_block(i, carry):
        lane = lanes_of(i)
        copy_all(inputs(i), in_sems, i, wait=True)
        w = [[w_ref[n, j : j + 1, lane] for j in range(SHORT)] for n in range(3)]
        for x, source, low in ((xq, bq, q_low), (xk, bk, kv_low), (xv, bv, kv_low)):
            if low:
                x[0:lead] = source[low - lead : low, lane].astype(F32)
            size = TAPS if low else TAPS + lead
            x[lead : lead + size] = source[low : low + size, lane].astype(F32)

        def filtered(x, taps, low, at, size):
            total = taps[0] * x[pl.ds(at + lead, size), :]
            for j in range(1, SHORT):
                mask = mj[j - 1, pl.ds(at + low, size), :]
                total += taps[j] * (mask * x[pl.ds(at + lead - j, size), :])
            return total

        def convolve(n, inner):
            at = pl.multiple_of(part * n, part)
            key = filtered(xk, w[1], kv_low, at, part)
            value = filtered(xv, w[2], kv_low, at, part)
            query = filtered(xq, w[0], q_low, at, part)
            conv_ref[i, 0, pl.ds(at, part), :] = key
            conv_ref[i, 1, pl.ds(at, part), :] = value
            uf[pl.ds(at, part), :] = key * value
            dz = bg[pl.ds(at + q_low, part), lane].astype(F32) * query
            dzf[pl.ds(at, part), :] = dz
            dzr_ref[i, pl.ds(at, part), :] = dz.astype(BF16)
            return inner

        lax.fori_loop(0, TAPS // part, convolve, 0)
        one_ref[i, 0:LANES, :] = uf[...].T.astype(BF16)
        two_ref[i, 0:LANES, :] = dzf[...].T.astype(BF16)
        if edge:
            beyond = bg[TAPS : TAPS + 16, lane].astype(F32)[:EDGE]
            beyond = beyond * filtered(xq, w[0], q_low, TAPS, EDGE)
            last = slice(lead + TAPS - EDGE, lead + TAPS)
            q_last = bq[rows - 16 : rows, lane].astype(F32)[EDGE:]
            k_first = bk[0:16, lane].astype(F32)[:EDGE]
            v_first = bv[0:16, lane].astype(F32)[:EDGE]
            g_first = bg[0:16, lane].astype(F32)[:EDGE]
            one_ref[i, LANES : LANES + 16, :] = pair(xk[last, :], xv[last, :])
            one_ref[i, LANES + 16 : LANES + 32, :] = pair(q_last, id_tile)
            one_ref[i, LANES + 32 : LANES + 48, :] = jnp.zeros((16, LANES), BF16)
            two_ref[i, LANES : LANES + 16, :] = pair(xq[lead : lead + EDGE, :], g_first)
            two_ref[i, LANES + 16 : LANES + 32, :] = pair(k_first, v_first)
            two_ref[i, LANES + 32 : LANES + 48, :] = pair(beyond, id_tile)
        send_packets(i)
        copy_all(outputs(i), out_sems, i)
        return carry

    lax.fori_loop(0, count, one_block, 0)

    def drain(i, carry):
        copy_all(packets(i)[0], packet_sems, i, wait=True)
        copy_all(outputs(i), out_sems, i, wait=True)
        return carry

    lax.fori_loop(0, count, drain, 0)


def half_part(edge, ids, short_filter, q_in, k_in, v_in, grad_out):
    rows, channels = q_in.shape[1:]
    count = channels // LANES
    vm = lambda *shape: pltpu.VMEM(shape, F32)
    vb = lambda *shape: pltpu.VMEM(shape, BF16)
    packet = (count, HEAD_ROWS if edge else LANES, LANES)
    results = (
        ((count, 2, TAPS, LANES), F32),
        ((count, TAPS, LANES), BF16),
        (packet, BF16),
        (packet, BF16),
    )
    return pl.pallas_call(
        functools.partial(half_kernel, rows, edge),
        in_specs=[HBM] * 6,
        out_specs=[HBM] * 4,
        out_shape=[jax.ShapeDtypeStruct(*r) for r in results],
        scratch_shapes=[
            pltpu.VMEM(ids.shape, jnp.int32),
            vm(*short_filter.shape),
            *[vb(rows, channels)] * 4,
            *[pltpu.VMEM(*r) for r in results],
            vm(rows + EDGE, LANES),
            vm(SHORT - 1, rows, LANES),
            *[vm(TAPS + 32, LANES)] * 3,
            vm(TAPS, LANES),
            vm(TAPS, LANES),
            pltpu.SemaphoreType.DMA((1, 2)),
            pltpu.SemaphoreType.DMA((count, 4)),
            pltpu.SemaphoreType.DMA((count, 2)),
            pltpu.SemaphoreType.DMA((count, 2)),
        ],
        compiler_params=pltpu.CompilerParams(vmem_limit_bytes=VMEM_LIMIT),
        cost_estimate=pl.CostEstimate(
            flops=8_000_000_000, bytes_accessed=16_000_000, transcendentals=0
        ),
        name="edge_half" if edge else "other_half",
    )(ids, short_filter, q_in, k_in, v_in, grad_out)


def mixer_kernel(
    rows,
    long_scale,
    short_scale,
    ids_hbm,
    filters_hbm,
    w_hbm,
    near_hbm,
    far_hbm,
    q_hbm,
    k_hbm,
    v_hbm,
    g_hbm,
    sent_near_hbm,
    sent_far_hbm,
    conv_late_hbm,
    dzr_early_hbm,
    conv_early_hbm,
    dzr_late_hbm,
    u_early_hbm,
    dz_late_hbm,
    oq_hbm,
    ok_hbm,
    ov_hbm,
    part_ref,
    ids_ref,
    filters_ref,
    w_ref,
    prev_ref,
    next_ref,
    bq,
    bk,
    bv,
    bg,
    tail_ref,
    head_ref,
    conv_late,
    dzr_early,
    conv_early,
    dzr_late,
    u_early,
    dz_late,
    oq_ref,
    ok_ref,
    ov_ref,
    tiles,
    idr,
    idc,
    mj,
    ml,
    mn,
    mp,
    flip,
    edges,
    ut,
    utr,
    dzt,
    dzr,
    zt,
    dut,
    dq,
    dk,
    dv,
    gl,
    fixes,
    bands,
    others,
    tops,
    products,
    small_sems,
    halo_sems,
    in_sems,
    out_sems,
):
    blocks = rows // TAPS
    frame = rows
    count = q_hbm.shape[2] // LANES
    per = LANES // GROUP
    odd = lax.rem(lax.axis_index("ctx"), 2)

    def small():
        return ((ids_hbm, ids_ref), (filters_hbm, filters_ref), (w_hbm, w_ref))

    waves = ((0, 1), (1, count - 1))

    def halos(wave):
        span = pl.ds(*waves[wave])
        far, near = far_hbm.at[span], near_hbm.at[span]
        prev, succ = prev_ref.at[span], next_ref.at[span]
        sent_far, sent_near = sent_far_hbm.at[span], sent_near_hbm.at[span]
        tail, head = tail_ref.at[span], head_ref.at[span]
        return (
            ((far, prev), (near, succ), (sent_near, tail), (sent_far, head)),
            ((near, prev), (far, succ), (sent_far, tail), (sent_near, head)),
        )

    def inputs(wave):
        start, size = waves[wave]
        span = pl.ds(start, size)
        lane = pl.ds(start * LANES, size * LANES)
        pairs = ((q_hbm, bq), (k_hbm, bk), (v_hbm, bv), (g_hbm, bg))
        pairs = [(a.at[0, :, lane], b.at[:, lane]) for a, b in pairs]
        more = (
            (conv_late_hbm, conv_late),
            (dzr_early_hbm, dzr_early),
            (conv_early_hbm, conv_early),
            (dzr_late_hbm, dzr_late),
            (u_early_hbm, u_early),
            (dz_late_hbm, dz_late),
        )
        return [(a.at[span], b.at[span]) for a, b in more] + pairs

    def outputs(i):
        lane = lanes_of(i)
        pairs = ((oq_ref, oq_hbm), (ok_ref, ok_hbm), (ov_ref, ov_hbm))
        return [(a.at[:, lane], b.at[0, :, lane]) for a, b in pairs]

    copy_all(small(), small_sems, 0)

    for wave in range(2):

        @pl.when(odd == 0)
        def even_halos():
            copy_all(halos(wave)[0], halo_sems, wave)

        @pl.when(odd == 1)
        def odd_halos():
            copy_all(halos(wave)[1], halo_sems, wave)

        copy_all(inputs(wave), in_sems, wave)

    def arrive(wave):
        copy_all(halos(wave)[0], halo_sems, wave, wait=True)
        copy_all(inputs(wave), in_sems, wave, wait=True)

    copy_all(small(), small_sems, 0, wait=True)
    arrive(0)

    row = lax.broadcasted_iota(jnp.int32, (TAPS, TAPS), 0)
    col = lax.broadcasted_iota(jnp.int32, (TAPS, TAPS), 1)
    own_ids = (ids_ref[...] + 1).astype(F32)
    prev_ids = prev_ref[0, LANES + 16 : LANES + 32, :].astype(F32)
    next_ids = next_ref[0, LANES + 32 : LANES + 48, :].astype(F32)
    for b in range(blocks):
        idr[b : b + 1, :] = prev_ids[EDGE + b : EDGE + b + 1]
        idr[blocks + b : blocks + b + 1, :] = own_ids[:, TAPS * b : TAPS * (b + 1)]
        idr[2 * blocks + b : 2 * blocks + b + 1, :] = next_ids[EDGE + b : EDGE + b + 1]
    for b in range(3 * blocks):
        idc[TAPS * b : TAPS * (b + 1), :] = spread(idr[b : b + 1, :])

    def short_masks(i, carry):
        base = pl.multiple_of(frame + EDGE * i, EDGE)
        here = idc[pl.ds(base, EDGE), :]
        for j in range(1, SHORT):
            mj[j - 1, pl.ds(base, EDGE), :] = (here == idc[pl.ds(base - j, EDGE), :]).astype(F32)
        return carry

    lax.fori_loop(0, (rows + 2 * EDGE) // EDGE, short_masks, 0)

    def same(t_block, s_block, length):
        start = frame + TAPS * t_block
        line = idr[blocks + s_block : blocks + s_block + 1, :]
        return (idc[start : start + length, :] == line).astype(F32)

    lower = (row >= col).astype(F32)
    upper = 1.0 - lower
    flip[...] = (row + col == TAPS - 1).astype(BF16)
    for b in range(blocks):
        ml[b] = (same(b, b, TAPS) * lower).astype(BF16)
    for b in range(blocks + 1):
        ml[blocks + b] = (same(b, b - 1, TAPS) * upper).astype(BF16)
    mn[0] = (same(blocks, blocks, 16) * lower[:16]).astype(BF16)
    mn[1] = (same(blocks, blocks, 16) * (row <= col).astype(F32)[:16]).astype(BF16)
    mn[2] = (same(blocks, blocks + 1, 16) * (row > col).astype(F32)[:16]).astype(BF16)
    for b in range(blocks):
        both = same(b, b, TAPS) * lower + same(b, b - 1, TAPS) * upper
        mp[b] = dot(both.astype(BF16), flip[...], NN)
    negated = jnp.logical_or(row + col == TAPS, row + col == 0).astype(BF16)
    reversed_taps = dot(filters_ref[...], negated, NN)
    forward_taps = filters_ref[...].astype(F32)
    for i in range(count * per):
        tiles[i, 0:1, :] = reversed_taps[i : i + 1]
        tiles[i, 1:2, :] = forward_taps[i : i + 1]

    lane_group = col // GROUP
    lower_flipped = row + col >= TAPS - 1
    first_lanes = col < EDGE
    blank = jnp.zeros((TAPS - EDGE, LANES), F32)

    def turned(x):
        return jnp.concatenate([x, blank], axis=0).T.astype(BF16)

    def filters_of(i):
        return [[w_ref[n, j : j + 1, lanes_of(i)] for j in range(SHORT)] for n in range(3)]

    def prepare(i):
        w = filters_of(i)
        prev_kv = prev_ref[i, LANES : LANES + 16, :].astype(F32)
        prev_q = prev_ref[i, LANES + 16 : LANES + 32, :].astype(F32)
        next_qg = next_ref[i, LANES : LANES + 16, :].astype(F32)
        next_kv = next_ref[i, LANES + 16 : LANES + 32, :].astype(F32)
        next_dz = next_ref[i, LANES + 32 : LANES + 48, :].astype(F32)
        for n, (source, before, after) in enumerate(
            (
                (bq, prev_q[:EDGE], next_qg[:EDGE]),
                (bk, prev_kv[:EDGE], next_kv[:EDGE]),
                (bv, prev_kv[EDGE:], next_kv[EDGE:]),
            )
        ):
            edges[n, 0, 0:EDGE] = before
            edges[n, 0, EDGE : 2 * EDGE] = source[0:16, lanes_of(i)].astype(F32)[:EDGE]
            edges[n, 1, 0:EDGE] = source[rows - 16 : rows, lanes_of(i)].astype(F32)[EDGE:]
            edges[n, 1, EDGE : 2 * EDGE] = after

        def convolve(n, m):
            low = frame + rows * m
            total = w[n][0] * edges[n, m, EDGE : 2 * EDGE]
            for j in range(1, SHORT):
                mask = mj[j - 1, low : low + EDGE, :]
                total += w[n][j] * (mask * edges[n, m, EDGE - j : 2 * EDGE - j])
            return total

        upstream = (bg[0:16, lanes_of(i)].astype(F32)[:EDGE], next_qg[EDGE:])
        fixed = []
        for m in range(2):
            query, key, value = [convolve(n, m) for n in range(3)]
            fixed.append((key, value, key * value, upstream[m] * query))

        ut[:, 0:TAPS] = prev_ref[i, 0:LANES, :]
        ut[:, TAPS : 2 * TAPS] = jnp.where(first_lanes, turned(fixed[0][2]), u_early[i])
        ut[:, 2 * TAPS : 3 * TAPS] = tail_ref[i, 0:LANES, :]
        ut[:, 3 * TAPS :] = turned(fixed[1][2])
        dzt[:, 0:TAPS] = jnp.where(first_lanes, turned(fixed[0][3]), head_ref[i, 0:LANES, :])
        dzt[:, TAPS : 2 * TAPS] = dz_late[i]
        dzt[:, 2 * TAPS : 3 * TAPS] = jnp.where(
            first_lanes, turned(fixed[1][3]), next_ref[i, 0:LANES, :]
        )
        dzt[:, 3 * TAPS :] = turned(next_dz[:EDGE])
        dzr[0:TAPS] = dzr_early[i]
        dzr[TAPS:] = dzr_late[i]
        rest = dzr_early[i, 0:16, :].astype(F32)[EDGE:]
        dzr[0:16] = jnp.concatenate([fixed[0][3], rest], axis=0).astype(BF16)
        for b in range(blocks + 1):
            here = slice(TAPS * b, TAPS * (b + 1))
            utr[:, here] = dot(ut[:, here], flip[...], NN).astype(BF16)

        for m in range(2):
            for n in range(2):
                fixes[m, n] = fixed[m][n]

    def make_bands(i, m, slot):
        if True:
            g = per * i + m
            base = pltpu.roll(jnp.broadcast_to(tiles[g, 0:1, :], (16, TAPS)), 0, 1, stride=1, stride_axis=0)
            base = base.astype(BF16)
            bands[slot, 0:16] = base
            for r in range(16, TAPS, 16):
                bands[slot, r : r + 16] = pltpu.roll(base, r, 1)
            tops[16 * m : 16 * m + 16] = base
            line = jnp.broadcast_to(tiles[g, 1:2, :], (16, TAPS))
            line = pltpu.roll(line, 0, 1, stride=1, stride_axis=0).astype(BF16)
            others[16 * m : 16 * m + 16] = line

    def sum_taps(i, m):
        skewed = pltpu.roll(products[m], 1, 1, stride=1, stride_axis=0)
        gl[per * i + m] = jnp.sum(skewed.reshape(TAPS // 8, 8, TAPS), axis=0)

    def multiply_taps():
        for b in range(blocks):
            here = slice(TAPS * b, TAPS * (b + 1))
            mine = [jnp.where(lane_group == m, dzr[here, :], jnp.zeros((), BF16)) for m in range(per)]
            pairs = dot(jnp.concatenate(mine, axis=0), utr[:, TAPS * b : TAPS * (b + 2)], NN)
            for m in range(per):
                own = pairs[TAPS * m : TAPS * (m + 1)]
                term = jnp.where(lower_flipped, own[:, TAPS:], own[:, :TAPS]) * mp[b]
                products[m] = term if b == 0 else products[m] + term

    def multiply(m, slot):
        c = slice(GROUP * m, GROUP * (m + 1))
        band = bands[slot]
        near = [band * ml[b] for b in range(blocks)]
        far = [band * ml[blocks + b] for b in range(blocks + 1)]
        weights = jnp.concatenate(
            [jnp.concatenate([far[b], near[b]], axis=1) for b in range(blocks)], axis=0
        )
        both = jnp.concatenate([ut[c, TAPS * b : TAPS * (b + 2)] for b in range(blocks)], axis=0)
        result = dot(both, weights, NT)
        for b in range(blocks):
            here = slice(TAPS * b, TAPS * (b + 1))
            zt[c, here] = result[GROUP * b : GROUP * (b + 1), here]
        weights = jnp.concatenate(
            [jnp.concatenate([near[b], far[b + 1]], axis=0) for b in range(blocks)], axis=1
        )
        both = jnp.concatenate([dzt[c, TAPS * b : TAPS * (b + 2)] for b in range(blocks)], axis=0)
        result = dot(both, weights, NN)
        for b in range(blocks):
            here = slice(TAPS * b, TAPS * (b + 1))
            dut[c, here] = result[GROUP * b : GROUP * (b + 1), here]

    def edge_rows(rows_of, first, second, signal):
        left = [rows_of[16 * m : 16 * m + 16] * first for m in range(per)]
        right = [rows_of[16 * m : 16 * m + 16] * second for m in range(per)]
        left, right = jnp.concatenate(left, axis=0), jnp.concatenate(right, axis=0)
        result = dot(jnp.concatenate([left, right], axis=1), signal, NT)
        total = None
        for m in range(per):
            own = jnp.where(lane_group[:16] == m, result[16 * m : 16 * m + 16], 0.0)
            total = own if total is None else total + own
        return total

    def close(i):
        below = next_ref[i, LANES : LANES + 16, :].astype(F32)[EDGE:]
        window = slice(TAPS * blocks, TAPS * (blocks + 2))
        z2 = edge_rows(tops, ml[2 * blocks, 0:16], mn[0], ut[:, window])
        du2 = edge_rows(others, mn[1], mn[2], dzt[:, window])
        for b in range(blocks + 1):
            length = TAPS if b < blocks else EDGE
            here = slice(TAPS * b, TAPS * b + length)
            z = zt[:, here].T if b < blocks else z2[:EDGE]
            du = dut[:, here].T if b < blocks else du2[:EDGE]
            if b < blocks:
                dq[here, :] = bg[here, lanes_of(i)].astype(F32) * z
                conv = conv_late if b else conv_early
                dk[here, :] = du * conv[i, 1]
                dv[here, :] = du * conv[i, 0]
            else:
                dq[here, :] = below * z
            if b in (0, blocks):
                m = 0 if b == 0 else 1
                key, value = fixes[m, 0], fixes[m, 1]
                there = slice(TAPS * b, TAPS * b + EDGE)
                dk[there, :] = du[:EDGE] * value
                dv[there, :] = du[:EDGE] * key

    steps = per
    groups = count * per
    part = 32

    def finish_steps(i):
        arrays = ((dq, bq, oq_ref), (dk, bk, ok_ref), (dv, bv, ov_ref))
        lane = lanes_of(i)
        for n in range(3 * SHORT):
            tiles[groups + n] = jnp.zeros((8, LANES), F32)

        def one_part(m):
            for n, (grad, source, out) in enumerate(arrays):
                sums = [None] * SHORT
                for at in range(rows // steps // part):
                    low = rows // steps * m + part * at
                    x = source[pl.ds(low, part), lane].astype(F32)
                    total = None
                    for j in range(SHORT):
                        piece = grad[pl.ds(low + j, part), :]
                        if j:
                            piece = piece * mj[j - 1, pl.ds(low + frame + j, part), :]
                        scaled = w_ref[n, j : j + 1, lane] * piece
                        total = scaled if total is None else total + scaled
                        fresh = jnp.sum((x * piece).reshape(part // 8, 8, LANES), axis=0)
                        sums[j] = fresh if at == 0 else sums[j] + fresh
                    out[pl.ds(low, part), lane] = total.astype(BF16)
                for j in range(SHORT):
                    tiles[groups + SHORT * n + j] += sums[j]

        def close():
            for n in range(3 * SHORT):
                line = jnp.sum(tiles[groups + n], axis=0, keepdims=True) * short_scale
                part_ref[n : n + 1, lane] = line
            copy_all(outputs(i), out_sems, i)

        return one_part, close

    part_ref[3 * SHORT : 24, :] = jnp.zeros((24 - 3 * SHORT, part_ref.shape[1]), F32)

    def long_block(i, between):
        make_bands(i, 0, 0)
        multiply_taps()
        for m in range(per):
            if m + 1 < per:
                make_bands(i, m + 1, (m + 1) % 2)
            multiply(m, m % 2)
            sum_taps(i, m)
            between(m)

    prepare(0)
    long_block(0, lambda m: None)
    close(0)
    arrive(1)
    prepare(1)

    def both(i, carry):
        one_part, close_finish = finish_steps(i - 1)
        long_block(i, one_part)
        close_finish()
        close(i)
        prepare(jnp.minimum(i + 1, count - 1))
        return carry

    lax.fori_loop(1, count, both, 0)
    one_part, close_finish = finish_steps(count - 1)
    for m in range(per):
        one_part(m)
    close_finish()
    for i in range(count):
        lines = [jnp.sum(gl[per * i + n], axis=0, keepdims=True) for n in range(per)]
        here = slice(LANES * i, LANES * (i + 1))
        part_ref[24:32, here] = jnp.concatenate(lines, axis=0) * long_scale

    def drain(i, carry):
        copy_all(outputs(i), out_sems, i, wait=True)
        return carry

    lax.fori_loop(0, count, drain, 0)


def mixer(operands, rows, channels, scales):
    blocks = rows // TAPS
    count = channels // LANES
    ids, filters, short_filter = operands[:3]
    vm = lambda *shape: pltpu.VMEM(shape, F32)
    vb = lambda *shape: pltpu.VMEM(shape, BF16)
    out = jax.ShapeDtypeStruct((1, rows, channels), BF16)
    buffered = [vb(rows, channels)] * 4
    return pl.pallas_call(
        functools.partial(mixer_kernel, rows, *scales),
        in_specs=[HBM] * len(operands),
        out_specs=[HBM, HBM, HBM, VMEM],
        out_shape=[out, out, out, jax.ShapeDtypeStruct((32, channels), F32)],
        scratch_shapes=[
            pltpu.VMEM(ids.shape, jnp.int32),
            vb(*filters.shape),
            vm(*short_filter.shape),
            vb(count, HEAD_ROWS, LANES),
            vb(count, HEAD_ROWS, LANES),
            *buffered,
            vb(count, HEAD_ROWS, LANES),
            vb(count, HEAD_ROWS, LANES),
            vm(count, 2, TAPS, LANES),
            vb(count, TAPS, LANES),
            vm(count, 2, TAPS, LANES),
            vb(count, TAPS, LANES),
            vb(count, LANES, TAPS),
            vb(count, LANES, TAPS),
            *buffered[:3],
            vm(channels // GROUP + 3 * SHORT, 8, TAPS),
            vm(8, LANES),
            vm(3 * rows, LANES),
            vm(SHORT - 1, 3 * rows, LANES),
            vb(2 * blocks + 1, TAPS, TAPS),
            vb(3, 16, TAPS),
            vm(blocks, TAPS, TAPS),
            vb(TAPS, TAPS),
            vm(3, 2, 2 * EDGE, LANES),
            vb(LANES, rows + 2 * TAPS),
            vb(LANES, rows + TAPS),
            vb(LANES, rows + 2 * TAPS),
            vb(rows, LANES),
            vm(LANES, rows + TAPS),
            vm(LANES, rows + TAPS),
            vm(rows + 16, LANES),
            vm(rows + 16, LANES),
            vm(rows + 16, LANES),
            vm(channels // GROUP, 8, TAPS),
            vm(2, 2, EDGE, LANES),
            vb(2, TAPS, TAPS),
            vb(LANES, TAPS),
            vb(LANES, TAPS),
            vm(LANES // GROUP, TAPS, TAPS),
            pltpu.SemaphoreType.DMA((1, 3)),
            pltpu.SemaphoreType.DMA((2, 4)),
            pltpu.SemaphoreType.DMA((2, 10)),
            pltpu.SemaphoreType.DMA((count, 3)),
        ],
        compiler_params=pltpu.CompilerParams(vmem_limit_bytes=63 << 20),
        name="mixer",
    )(*operands)


AXES = ("fsdp", "ctx")


def exchanged(x, bits):
    size = lax.axis_size(AXES)
    return lax.ppermute(x, AXES, [(i, i ^ bits) for i in range(size)]).astype(F32)


def sum_pair(x):
    return x + exchanged(x, 1)


def sum_rest(x):
    size = lax.axis_size(AXES)
    bit = 2
    while bit < size:
        sent = x.astype(BF16)
        x = sent.astype(F32) + exchanged(sent, bit)
        if 2 * bit < size:
            x = x + (exchanged(sent, 2 * bit) + exchanged(sent, 3 * bit))
        bit *= 4
    return x


def all_taps(long_filter):
    if lax.axis_size("fsdp") != 2:
        return lax.all_gather(long_filter, "fsdp", axis=1, tiled=True)
    other = lax.ppermute(long_filter, "fsdp", [(0, 1), (1, 0)])
    first = lax.axis_index("fsdp") == 0
    return jnp.where(
        first,
        jnp.concatenate([long_filter, other], axis=1),
        jnp.concatenate([other, long_filter], axis=1),
    )


def body(q_in, k_in, v_in, grad_out, genome_ids, long_filter, short_filter):
    rows, channels = q_in.shape[1:]
    seq_count = lax.axis_size("fsdp")
    length = rows * lax.axis_size("ctx")
    filters = all_taps(long_filter)
    groups = filters.shape[0]
    arrays = (genome_ids, short_filter, q_in, k_in, v_in, grad_out)
    conv_late, dzr_early, sent_near, sent_far = half_part(True, *arrays)
    near, far = swapped(sent_near, sent_far, "ctx")
    sent_near, sent_far, genome_ids = lax.optimization_barrier((sent_near, sent_far, genome_ids))
    conv_early, dzr_late, u_early, dz_late = half_part(False, genome_ids, *arrays[1:])
    scales = (
        1.0 / math.sqrt(seq_count * length * (channels // groups)),
        1.0 / math.sqrt(seq_count * length),
    )
    operands = (
        genome_ids, filters, short_filter, near, far, q_in, k_in, v_in, grad_out,
        sent_near, sent_far, conv_late, dzr_early, conv_early, dzr_late, u_early, dz_late,
    )
    out_q, out_k, out_v, sums = mixer(operands, rows, channels, scales)
    power = lax.axis_size(AXES)
    if power & (power - 1):
        sums = lax.psum(sums, AXES)
    else:
        sums = sum_rest(sum_pair(sums))
    grad_short = sums[: 3 * SHORT].reshape(3, SHORT, channels)
    grad_long = sums[24:].reshape(8, channels // LANES, LANES).transpose(1, 0, 2)
    grad_long = grad_long.reshape(groups, TAPS)
    own = TAPS // seq_count
    grad_long = lax.dynamic_slice_in_dim(grad_long, lax.axis_index("fsdp") * own, own, 1)
    return out_q, out_k, out_v, grad_long, grad_short


def solution(mesh):
    return jax.shard_map(
        body,
        mesh=mesh,
        in_specs=(
            P("fsdp", "ctx", "tp"),
            P("fsdp", "ctx", "tp"),
            P("fsdp", "ctx", "tp"),
            P("fsdp", "ctx", "tp"),
            P("fsdp", "ctx"),
            P("tp", "fsdp"),
            P(None, None, "tp"),
        ),
        out_specs=(
            P("fsdp", "ctx", "tp"),
            P("fsdp", "ctx", "tp"),
            P("fsdp", "ctx", "tp"),
            P("tp", "fsdp"),
            P(None, None, "tp"),
        ),
        check_vma=False,
    )
```

time: 51.4 us -> 47.5 us (0.924)
  waiting for transfers between devices: 9.94 us -> 4.86 us
  Pallas kernels: 24.6 us -> 27.4 us
  starting transfers between devices: 12 us -> 10.4 us
    ppermute x3 -> x4, waiting for transfers between devices: 8.21 us -> 4.85 us  [exchanged(): lax.ppermute(x, AXES, [(i, i ^ bits) for i in range(size)]).astype(F32)]
    pallas_call x1 -> x2, Pallas kernels: 7.08 us -> 9.71 us  [half_part(): pl.pallas_call(functools.partial(half_kernel, rows, edge), in_specs=[HBM]...]
    ppermute x1, waiting for transfers between devices: 1.72 us -> 0.01 us  [all_taps(): other = lax.ppermute(long_filter, 'fsdp', [(0, 1), (1, 0)])]
    ppermute x3 -> x4, starting transfers between devices: 8.28 us -> 6.66 us  [exchanged(): lax.ppermute(x, AXES, [(i, i ^ bits) for i in range(size)]).astype(F32)]
    convert_element_type x0 -> x1, other arithmetic: none -> 0.92 us  [sum_rest(): sent = x.astype(BF16)]
    add x3 -> x1, other arithmetic: 0.96 us -> 0.03 us  [sum_rest(): x = x + (exchanged(sent, 2 * bit) + exchanged(sent, 3 * bit))]
  transfers between devices with their start and end apart: 6 -> 7, of which waited for: 4 -> 4; matrix products, arithmetic and copies ran while one was open for 1% -> 1% of each run, Pallas kernels for 0% -> 21%
where the time goes in v2:
time: 47.5 us; the launch traced here: 47.3 us
  Pallas kernels  27.4 us (58%)
  starting transfers between devices  10.4 us (22%)
  waiting for transfers between devices  4.86 us (10%)
  local copies, waits for them, and re-layouts  2.21 us (5%)
  other arithmetic  1.65 us (3%)
  between operations  0.74 us (2%)
    pallas_call x1, Pallas kernels, mixer(): pl.pallas_call(functools.partial(mixer_kernel, rows, *scales), in_specs=[...  17.7 us
    pallas_call x2, Pallas kernels, half_part(): pl.pallas_call(functools.partial(half_kernel, rows, edge), in_specs=[HBM]...  9.71 us
    ppermute x4, starting transfers between devices, exchanged(): lax.ppermute(x, AXES, [(i, i ^ bits) for i in range(size)]).astype(F32)  6.66 us
    ppermute x4, waiting for transfers between devices, exchanged(): lax.ppermute(x, AXES, [(i, i ^ bits) for i in range(size)]).astype(F32)  4.85 us
    ppermute x1, starting transfers between devices, all_taps(): other = lax.ppermute(long_filter, 'fsdp', [(0, 1), (1, 0)])  3 us
  transfers between devices with their start and end apart: 7, of which 4 were waited for; matrix products, arithmetic and copies ran while one was open for 1% of the time, Pallas kernels for 21%

profile of v2, /device:TPU:0, one launch (start us, length us, event | category | flops | bytes accessed | tf_op | source)
XLA Modules:
  0.0 47.3 jit_solution(2360599131514229884)
XLA Ops:
  0.6 3.0 %collective-permute-start = (bf16[64,64]{1,0:T(8,128)(2,1)}, bf16[64,64]{1,0:T(8,128)(2,1)S(1)}, u32[]{:S(2)}, u32[]{:S(2)}) collective-permute-start(bf16[64,64]{1,0:T(8,128)(2,1)} %param.12), channel_id=1, source_target_pairs={{0,16},{16,0},{1,17},{17,1},{2,18},{18,2},{3,19},{19,3},{4,20},{20... | collective-permute-start | bytes 24584 | tf_op jit(solution)/shard_map/ppermute | solution.py:761
  3.6 4.9 %edge_half.1 = (f32[8,2,128,128]{3,2,1,0:T(8,128)}, bf16[8,128,128]{2,1,0:T(8,128)(2,1)}, bf16[8,176,128]{2,1,0:T(8,128)(2,1)}, bf16[8,176,128]{2,1,0:T(8,128)(2,1)}) custom-call(s32[1,256]{1,0:T(1,128)} %ids_hbm.3, f32[3,7,1024]{2,1,0:T(8,128)} %w_hbm.5, bf16[1,256,1024]{2,1,0:T(8,128)(2,1)} %q_hbm.5, bf16[1,256,1024]{2,1,0:T(8,128)(2,1)} %k_hbm.5, ...), custom_call_target="tpu_custom_call" | custom-call | flops 8000000000 | bytes 16000000 | tf_op jit(solution)/shard_map/edge_half/pallas_call | solution.py:229
  8.5 0.1 collective-permute-start.1
  8.6 0.7 %collective-permute-start.2 = (bf16[8,176,128]{2,1,0:T(8,128)(2,1)}, bf16[8,176,128]{2,1,0:T(8,128)(2,1)S(1)}, u32[]{:S(2)}, u32[]{:S(2)}) collective-permute-start(bf16[8,176,128]{2,1,0:T(8,128)(2,1)} %get-tuple-element.24.sent_far_hbm), channel_id=1, source_target_pairs={{8,4},{4,8},{9,5},{5,9},{10,6},{6,10},{11,7},{7,11},{24,20},{20,24... | collective-permute-start | bytes 1081352 | tf_op jit(solution)/shard_map/ppermute | solution.py:31
  9.3 0.0 copy-start.2
  9.3 4.8 %other_half.1 = (f32[8,2,128,128]{3,2,1,0:T(8,128)}, bf16[8,128,128]{2,1,0:T(8,128)(2,1)}, bf16[8,128,128]{2,1,0:T(8,128)(2,1)}, bf16[8,128,128]{2,1,0:T(8,128)(2,1)}) custom-call(s32[1,256]{1,0:T(1,128)} %ids_hbm.3, f32[3,7,1024]{2,1,0:T(8,128)} %w_hbm.5, bf16[1,256,1024]{2,1,0:T(8,128)(2,1)} %q_hbm.5, bf16[1,256,1024]{2,1,0:T(8,128)(2,1)} %k_hbm.5, ...), custom_call_target="tpu_custom_call" | custom-call | flops 8000000000 | bytes 16000000 | tf_op jit(solution)/shard_map/other_half/pallas_call | solution.py:229
  14.1 0.0 collective-permute-done
  14.2 0.0 copy-done.2
  14.2 0.7 %maximum_select_fusion.filters_hbm = bf16[64,128]{1,0:T(8,128)(2,1)} fusion(bf16[64,64]{1,0:T(8,128)(2,1)S(1)} %collective-permute-done, bf16[64,64]{1,0:T(8,128)(2,1)S(1)} %copy-done.2, pred[]{:T(512)S(6)} %eq.3), kind=kLoop, calls=%fused_computation.3 | loop fusion | flops 73728 | bytes 32769 | tf_op jit(solution)/shard_map/jit(_where)/select_n | solution.py:763
  14.9 0.0 collective-permute-done.1.near_hbm
  14.9 0.0 copy-start
  14.9 0.0 collective-permute-done.2.far_hbm
  14.9 0.0 copy-start.1
  14.9 0.7 %copy-done = bf16[8,176,128]{2,1,0:T(8,128)(2,1)} copy-done((bf16[8,176,128]{2,1,0:T(8,128)(2,1)}, bf16[8,176,128]{2,1,0:T(8,128)(2,1)S(1)}, u32[]{:S(2)}) %copy-start) | copy-done | bytes 360472
  15.6 0.1 copy-done.1
  15.7 17.7 %mixer.1 = (bf16[1,256,1024]{2,1,0:T(8,128)(2,1)}, bf16[1,256,1024]{2,1,0:T(8,128)(2,1)}, bf16[1,256,1024]{2,1,0:T(8,128)(2,1)}, f32[32,1024]{1,0:T(8,128)}) custom-call(s32[1,256]{1,0:T(1,128)} %ids_hbm.3, bf16[64,128]{1,0:T(8,128)(2,1)} %maximum_select_fusion.filters_hbm, f32[3,7,1024]{2,1,0:T(8,128)} %w_hbm.5, bf16[8,176,128]{2,1,0:T(8,128)(2,1)} %copy-done, ...), custom_call_target="tpu_custom_call" | custom-call | tf_op jit(solution)/shard_map/mixer/pallas_call | solution.py:679
  33.5 3.1 %collective-permute-start.3 = (f32[32,1024]{1,0:T(8,128)}, f32[32,1024]{1,0:T(8,128)S(1)}, u32[]{:S(2)}, u32[]{:S(2)}) collective-permute-start(f32[32,1024]{1,0:T(8,128)} %get-tuple-element.34), channel_id=1, source_target_pairs={{0,4},{4,0},{8,12},{12,8},{16,20},{20,16},{24,28},{28,24},{1,5},{5... | collective-permute-start | bytes 393224 | tf_op jit(solution)/shard_map/ppermute | solution.py:739
  36.5 1.2 %collective-permute-done.3 = f32[32,1024]{1,0:T(8,128)S(1)} collective-permute-done((f32[32,1024]{1,0:T(8,128)}, f32[32,1024]{1,0:T(8,128)S(1)}, u32[]{:S(2)}, u32[]{:S(2)}) %collective-permute-start.3) | collective-permute-done | bytes 131104 | tf_op jit(solution)/shard_map/ppermute | solution.py:739
  37.7 0.9 %add_convert_fusion = bf16[32,1024]{1,0:T(8,128)(2,1)S(1)} fusion(f32[32,1024]{1,0:T(8,128)} %get-tuple-element.34, f32[32,1024]{1,0:T(8,128)S(1)} %collective-permute-done.3), kind=kLoop, calls=%fused_computation.1 | loop fusion | flops 65536 | bytes 327680 | tf_op jit(solution)/shard_map/convert_element_type | solution.py:750
  38.7 1.4 %collective-permute-start.6 = (bf16[32,1024]{1,0:T(8,128)(2,1)S(1)}, bf16[32,1024]{1,0:T(8,128)(2,1)S(1)}, u32[]{:S(2)}, u32[]{:S(2)}) collective-permute-start(bf16[32,1024]{1,0:T(8,128)(2,1)S(1)} %add_convert_fusion), channel_id=1, source_target_pairs={{0,24},{4,28},{8,16},{12,20},{16,8},{20,12},{24,0},{28,4},{1,25},{... | collective-permute-start | bytes 196616 | tf_op jit(solution)/shard_map/ppermute | solution.py:739
  40.1 1.5 %collective-permute-start.5 = (bf16[32,1024]{1,0:T(8,128)(2,1)S(1)}, bf16[32,1024]{1,0:T(8,128)(2,1)S(1)}, u32[]{:S(2)}, u32[]{:S(2)}) collective-permute-start(bf16[32,1024]{1,0:T(8,128)(2,1)S(1)} %add_convert_fusion), channel_id=1, source_target_pairs={{0,16},{4,20},{8,24},{12,28},{16,0},{20,4},{24,8},{28,12},{1,17},{... | collective-permute-start | bytes 196616 | tf_op jit(solution)/shard_map/ppermute | solution.py:739
  41.6 0.6 %collective-permute-start.4 = (bf16[32,1024]{1,0:T(8,128)(2,1)S(1)}, bf16[32,1024]{1,0:T(8,128)(2,1)S(1)}, u32[]{:S(2)}, u32[]{:S(2)}) collective-permute-start(bf16[32,1024]{1,0:T(8,128)(2,1)S(1)} %add_convert_fusion), channel_id=1, source_target_pairs={{0,8},{4,12},{8,0},{12,4},{16,24},{20,28},{24,16},{28,20},{1,9},{5... | collective-permute-start | bytes 196616 | tf_op jit(solution)/shard_map/ppermute | solution.py:739
  42.2 2.3 %collective-permute-done.6 = bf16[32,1024]{1,0:T(8,128)(2,1)S(1)} collective-permute-done((bf16[32,1024]{1,0:T(8,128)(2,1)S(1)}, bf16[32,1024]{1,0:T(8,128)(2,1)S(1)}, u32[]{:S(2)}, u32[]{:S(2)}) %collective-permute-start.6) | collective-permute-done | bytes 65568 | tf_op jit(solution)/shard_map/ppermute | solution.py:739
  44.6 0.6 %collective-permute-done.5 = bf16[32,1024]{1,0:T(8,128)(2,1)S(1)} collective-permute-done((bf16[32,1024]{1,0:T(8,128)(2,1)S(1)}, bf16[32,1024]{1,0:T(8,128)(2,1)S(1)}, u32[]{:S(2)}, u32[]{:S(2)}) %collective-permute-start.5) | collective-permute-done | bytes 65568 | tf_op jit(solution)/shard_map/ppermute | solution.py:739
  45.1 0.7 %collective-permute-done.4 = bf16[32,1024]{1,0:T(8,128)(2,1)S(1)} collective-permute-done((bf16[32,1024]{1,0:T(8,128)(2,1)S(1)}, bf16[32,1024]{1,0:T(8,128)(2,1)S(1)}, u32[]{:S(2)}, u32[]{:S(2)}) %collective-permute-start.4) | collective-permute-done | bytes 65568 | tf_op jit(solution)/shard_map/ppermute | solution.py:739
  46.0 0.7 %reshape.21 = f32[3,7,1024]{2,1,0:T(8,128)} reshape(f32[21,1024]{1,0:T(8,128)S(1)} %slice.9) | data formatting | bytes 172032 | tf_op jit(solution)/shard_map/reshape | solution.py:795
  46.6 0.7 %constant_dynamic-slice_fusion = f32[64,64]{1,0:T(8,128)} fusion(f32[64,128]{1,0:T(8,128)S(1)} %slice_bitcast_fusion, s32[]{:T(128)S(6)} %select_n.13), kind=kLoop, calls=%fused_computation.4 | loop fusion | bytes 32772 | tf_op jit(solution)/shard_map/dynamic_slice | solution.py:799
  (3 shorter events, 0.0 us)
Async XLA Ops:
  0.6 13.5 %collective-permute-start = (bf16[64,64]{1,0:T(8,128)(2,1)}, bf16[64,64]{1,0:T(8,128)(2,1)S(1)}, u32[]{:S(2)}, u32[]{:S(2)}) collective-permute-start(bf16[64,64]{1,0:T(8,128)(2,1)} %param.12), channel_id=1, source_target_pairs={{0,16},{16,0},{1,17},{17,1},{2,18},{18,2},{3,19},{19,3},{4,20},{20... | collective-permute-start | bytes 24584 | tf_op jit(solution)/shard_map/ppermute | solution.py:761
  8.5 6.4 %collective-permute-start.1 = (bf16[8,176,128]{2,1,0:T(8,128)(2,1)}, bf16[8,176,128]{2,1,0:T(8,128)(2,1)S(1)}, u32[]{:S(2)}, u32[]{:S(2)}) collective-permute-start(bf16[8,176,128]{2,1,0:T(8,128)(2,1)} %get-tuple-element.23.sent_near_hbm), channel_id=1, source_target_pairs={{0,4},{4,0},{8,12},{12,8},{1,5},{5,1},{9,13},{13,9},{2,6},{6,2},{1... | collective-permute-start | bytes 1081352 | tf_op jit(solution)/shard_map/ppermute | solution.py:31
  8.6 6.3 %collective-permute-start.2 = (bf16[8,176,128]{2,1,0:T(8,128)(2,1)}, bf16[8,176,128]{2,1,0:T(8,128)(2,1)S(1)}, u32[]{:S(2)}, u32[]{:S(2)}) collective-permute-start(bf16[8,176,128]{2,1,0:T(8,128)(2,1)} %get-tuple-element.24.sent_far_hbm), channel_id=1, source_target_pairs={{8,4},{4,8},{9,5},{5,9},{10,6},{6,10},{11,7},{7,11},{24,20},{20,24... | collective-permute-start | bytes 1081352 | tf_op jit(solution)/shard_map/ppermute | solution.py:31
  9.3 4.9 %copy-start.2 = (bf16[64,64]{1,0:T(8,128)(2,1)S(1)}, bf16[64,64]{1,0:T(8,128)(2,1)}, u32[]{:S(2)}) copy-start(bf16[64,64]{1,0:T(8,128)(2,1)} %param.12) | copy-start | bytes 24580
  14.9 0.8 %copy-start = (bf16[8,176,128]{2,1,0:T(8,128)(2,1)}, bf16[8,176,128]{2,1,0:T(8,128)(2,1)S(1)}, u32[]{:S(2)}) copy-start(bf16[8,176,128]{2,1,0:T(8,128)(2,1)S(1)} %collective-permute-done.1.near_hbm) | copy-start | bytes 1081348
  14.9 0.9 %copy-start.1 = (bf16[8,176,128]{2,1,0:T(8,128)(2,1)}, bf16[8,176,128]{2,1,0:T(8,128)(2,1)S(1)}, u32[]{:S(2)}) copy-start(bf16[8,176,128]{2,1,0:T(8,128)(2,1)S(1)} %collective-permute-done.2.far_hbm) | copy-start | bytes 1081348
  33.5 4.3 %collective-permute-start.3 = (f32[32,1024]{1,0:T(8,128)}, f32[32,1024]{1,0:T(8,128)S(1)}, u32[]{:S(2)}, u32[]{:S(2)}) collective-permute-start(f32[32,1024]{1,0:T(8,128)} %get-tuple-element.34), channel_id=1, source_target_pairs={{0,4},{4,0},{8,12},{12,8},{16,20},{20,16},{24,28},{28,24},{1,5},{5... | collective-permute-start | bytes 393224 | tf_op jit(solution)/shard_map/ppermute | solution.py:739
  38.7 5.9 %collective-permute-start.6 = (bf16[32,1024]{1,0:T(8,128)(2,1)S(1)}, bf16[32,1024]{1,0:T(8,128)(2,1)S(1)}, u32[]{:S(2)}, u32[]{:S(2)}) collective-permute-start(bf16[32,1024]{1,0:T(8,128)(2,1)S(1)} %add_convert_fusion), channel_id=1, source_target_pairs={{0,24},{4,28},{8,16},{12,20},{16,8},{20,12},{24,0},{28,4},{1,25},{... | collective-permute-start | bytes 196616 | tf_op jit(solution)/shard_map/ppermute | solution.py:739
  40.1 5.0 %collective-permute-start.5 = (bf16[32,1024]{1,0:T(8,128)(2,1)S(1)}, bf16[32,1024]{1,0:T(8,128)(2,1)S(1)}, u32[]{:S(2)}, u32[]{:S(2)}) collective-permute-start(bf16[32,1024]{1,0:T(8,128)(2,1)S(1)} %add_convert_fusion), channel_id=1, source_target_pairs={{0,16},{4,20},{8,24},{12,28},{16,0},{20,4},{24,8},{28,12},{1,17},{... | collective-permute-start | bytes 196616 | tf_op jit(solution)/shard_map/ppermute | solution.py:739
  41.6 4.3 %collective-permute-start.4 = (bf16[32,1024]{1,0:T(8,128)(2,1)S(1)}, bf16[32,1024]{1,0:T(8,128)(2,1)S(1)}, u32[]{:S(2)}, u32[]{:S(2)}) collective-permute-start(bf16[32,1024]{1,0:T(8,128)(2,1)S(1)} %add_convert_fusion), channel_id=1, source_target_pairs={{0,8},{4,12},{8,0},{12,4},{16,24},{20,28},{24,16},{28,20},{1,9},{5... | collective-permute-start | bytes 196616 | tf_op jit(solution)/shard_map/ppermute | solution.py:739

commit v3 on v2

--- a/solution.py
+++ b/solution.py
@@ -13,7 +13,7 @@
 LANES = 128
 GROUP = 16
 EDGE = 8
-VMEM_LIMIT = 63 << 20
+VMEM_LIMIT = 65300 << 10
 HEAD_ROWS = LANES + 48
 F32 = jnp.float32
 BF16 = jnp.bfloat16
@@ -259,7 +259,8 @@
     long_scale,
     short_scale,
     ids_hbm,
-    filters_hbm,
+    one_half_hbm,
+    other_half_hbm,
     w_hbm,
     near_hbm,
     far_hbm,
@@ -278,9 +279,10 @@
     oq_hbm,
     ok_hbm,
     ov_hbm,
-    part_ref,
+    part_hbm,
     ids_ref,
-    filters_ref,
+    one_half,
+    other_half,
     w_ref,
     prev_ref,
     next_ref,
@@ -299,6 +301,7 @@
     oq_ref,
     ok_ref,
     ov_ref,
+    part_ref,
     tiles,
     idr,
     idc,
@@ -335,9 +338,14 @@
     odd = lax.rem(lax.axis_index("ctx"), 2)
 
     def small():
-        return ((ids_hbm, ids_ref), (filters_hbm, filters_ref), (w_hbm, w_ref))
-
-    waves = ((0, 1), (1, count - 1))
+        return (
+            (ids_hbm, ids_ref),
+            (one_half_hbm, one_half),
+            (other_half_hbm, other_half),
+            (w_hbm, w_ref),
+        )
+
+    waves = ((0, 1), (1, 2), (3, count - 3))
 
     def halos(wave):
         span = pl.ds(*waves[wave])
@@ -371,10 +379,7 @@
         pairs = ((oq_ref, oq_hbm), (ok_ref, ok_hbm), (ov_ref, ov_hbm))
         return [(a.at[:, lane], b.at[0, :, lane]) for a, b in pairs]
 
-    copy_all(small(), small_sems, 0)
-
-    for wave in range(2):
-
+    def start_wave(wave):
         @pl.when(odd == 0)
         def even_halos():
             copy_all(halos(wave)[0], halo_sems, wave)
@@ -385,12 +390,17 @@
 
         copy_all(inputs(wave), in_sems, wave)
 
+    def arrive_halos(wave):
+        copy_all(halos(wave)[0], halo_sems, wave, wait=True)
+
     def arrive(wave):
-        copy_all(halos(wave)[0], halo_sems, wave, wait=True)
         copy_all(inputs(wave), in_sems, wave, wait=True)
 
+    copy_all(small(), small_sems, 0)
+    start_wave(0)
     copy_all(small(), small_sems, 0, wait=True)
-    arrive(0)
+    arrive_halos(0)
+    start_wave(1)
 
     row = lax.broadcasted_iota(jnp.int32, (TAPS, TAPS), 0)
     col = lax.broadcasted_iota(jnp.int32, (TAPS, TAPS), 1)
@@ -432,8 +442,12 @@
         both = same(b, b, TAPS) * lower + same(b, b - 1, TAPS) * upper
         mp[b] = dot(both.astype(BF16), flip[...], NN)
     negated = jnp.logical_or(row + col == TAPS, row + col == 0).astype(BF16)
-    reversed_taps = dot(filters_ref[...], negated, NN)
-    forward_taps = filters_ref[...].astype(F32)
+    first, second = one_half[...].astype(F32), other_half[...].astype(F32)
+    if lax.axis_size("fsdp") == 2:
+        mine = lax.axis_index("fsdp") == 0
+        first, second = jnp.where(mine, first, second), jnp.where(mine, second, first)
+    forward_taps = jnp.concatenate([first, second], axis=1)
+    reversed_taps = dot(forward_taps.astype(BF16), negated, NN)
     for i in range(count * per):
         tiles[i, 0:1, :] = reversed_taps[i : i + 1]
         tiles[i, 1:2, :] = forward_taps[i : i + 1]
@@ -637,13 +651,21 @@
             sum_taps(i, m)
             between(m)
 
+    arrive(0)
+    start_wave(2)
     prepare(0)
     long_block(0, lambda m: None)
     close(0)
+    arrive_halos(1)
     arrive(1)
     prepare(1)
 
     def both(i, carry):
+        @pl.when(i == 2)
+        def rest_arrives():
+            arrive_halos(2)
+            arrive(2)
+
         one_part, close_finish = finish_steps(i - 1)
         long_block(i, one_part)
         close_finish()
@@ -661,17 +683,20 @@
         here = slice(LANES * i, LANES * (i + 1))
         part_ref[24:32, here] = jnp.concatenate(lines, axis=0) * long_scale
 
+    copy_all([(part_ref, part_hbm)], small_sems, 0)
+
     def drain(i, carry):
         copy_all(outputs(i), out_sems, i, wait=True)
         return carry
 
     lax.fori_loop(0, count, drain, 0)
+    copy_all([(part_ref, part_hbm)], small_sems, 0, wait=True)
 
 
 def mixer(operands, rows, channels, scales):
     blocks = rows // TAPS
     count = channels // LANES
-    ids, filters, short_filter = operands[:3]
+    ids, short_filter = operands[0], operands[3]
     vm = lambda *shape: pltpu.VMEM(shape, F32)
     vb = lambda *shape: pltpu.VMEM(shape, BF16)
     out = jax.ShapeDtypeStruct((1, rows, channels), BF16)
@@ -679,11 +704,12 @@
     return pl.pallas_call(
         functools.partial(mixer_kernel, rows, *scales),
         in_specs=[HBM] * len(operands),
-        out_specs=[HBM, HBM, HBM, VMEM],
+        out_specs=[HBM] * 4,
         out_shape=[out, out, out, jax.ShapeDtypeStruct((32, channels), F32)],
         scratch_shapes=[
             pltpu.VMEM(ids.shape, jnp.int32),
-            vb(*filters.shape),
+            vb(*operands[1].shape),
+            vb(*operands[2].shape),
             vm(*short_filter.shape),
             vb(count, HEAD_ROWS, LANES),
             vb(count, HEAD_ROWS, LANES),
@@ -697,6 +723,7 @@
             vb(count, LANES, TAPS),
             vb(count, LANES, TAPS),
             *buffered[:3],
+            vm(32, channels),
             vm(channels // GROUP + 3 * SHORT, 8, TAPS),
             vm(8, LANES),
             vm(3 * rows, LANES),
@@ -721,9 +748,9 @@
             vb(LANES, TAPS),
             vb(LANES, TAPS),
             vm(LANES // GROUP, TAPS, TAPS),
-            pltpu.SemaphoreType.DMA((1, 3)),
-            pltpu.SemaphoreType.DMA((2, 4)),
-            pltpu.SemaphoreType.DMA((2, 10)),
+            pltpu.SemaphoreType.DMA((1, 4)),
+            pltpu.SemaphoreType.DMA((3, 4)),
+            pltpu.SemaphoreType.DMA((3, 10)),
             pltpu.SemaphoreType.DMA((count, 3)),
         ],
         compiler_params=pltpu.CompilerParams(vmem_limit_bytes=63 << 20),
@@ -755,24 +782,19 @@
     return x
 
 
-def all_taps(long_filter):
-    if lax.axis_size("fsdp") != 2:
-        return lax.all_gather(long_filter, "fsdp", axis=1, tiled=True)
-    other = lax.ppermute(long_filter, "fsdp", [(0, 1), (1, 0)])
-    first = lax.axis_index("fsdp") == 0
-    return jnp.where(
-        first,
-        jnp.concatenate([long_filter, other], axis=1),
-        jnp.concatenate([other, long_filter], axis=1),
-    )
+def tap_halves(long_filter):
+    if lax.axis_size("fsdp") == 2:
+        return long_filter, lax.ppermute(long_filter, "fsdp", [(0, 1), (1, 0)])
+    filters = lax.all_gather(long_filter, "fsdp", axis=1, tiled=True)
+    return filters[:, : TAPS // 2], filters[:, TAPS // 2 :]
 
 
 def body(q_in, k_in, v_in, grad_out, genome_ids, long_filter, short_filter):
     rows, channels = q_in.shape[1:]
     seq_count = lax.axis_size("fsdp")
     length = rows * lax.axis_size("ctx")
-    filters = all_taps(long_filter)
-    groups = filters.shape[0]
+    halves = tap_halves(long_filter)
+    groups = long_filter.shape[0]
     arrays = (genome_ids, short_filter, q_in, k_in, v_in, grad_out)
     conv_late, dzr_early, sent_near, sent_far = half_part(True, *arrays)
     near, far = swapped(sent_near, sent_far, "ctx")
@@ -783,7 +805,7 @@
         1.0 / math.sqrt(seq_count * length),
     )
     operands = (
-        genome_ids, filters, short_filter, near, far, q_in, k_in, v_in, grad_out,
+        genome_ids, *halves, short_filter, near, far, q_in, k_in, v_in, grad_out,
         sent_near, sent_far, conv_late, dzr_early, conv_early, dzr_late, u_early, dz_late,
     )
     out_q, out_k, out_v, sums = mixer(operands, rows, channels, scales)

time: 47.5 us -> 44.3 us (0.933)
  Pallas kernels: 27.4 us -> 25.5 us
  other arithmetic: 1.65 us -> 0.96 us
    pallas_call x1, Pallas kernels: 17.7 us -> 15.8 us  [mixer(): pl.pallas_call(functools.partial(mixer_kernel, rows, *scales), in_specs=[...]
    ppermute x4, starting transfers between devices: 6.66 us -> 5.57 us  [exchanged(): lax.ppermute(x, AXES, [(i, i ^ bits) for i in range(size)]).astype(F32)]
    ppermute x1, starting transfers between devices: 0.68 us -> 1.4 us  [swapped(): lax.ppermute(far, axis, far_route)]
    select_n x1 -> x0, other arithmetic: 0.69 us -> none  [all_taps(): jnp.where(first, jnp.concatenate([long_filter, other], axis=1), jnp.conca...]
    ppermute x1, starting transfers between devices: 3 us -> 2.51 us  [tap_halves(): return (long_filter, lax.ppermute(long_filter, 'fsdp', [(0, 1), (1, 0)]))]
  transfers between devices with their start and end apart: 7 -> 7, of which waited for: 4 -> 4; matrix products, arithmetic and copies ran while one was open for 1% -> 0% of each run, Pallas kernels for 21% -> 11%
where the time goes in v3:
time: 44.3 us; the launch traced here: 44.1 us
  Pallas kernels  25.5 us (58%)
  starting transfers between devices  9.99 us (23%)
  waiting for transfers between devices  5.01 us (11%)
  local copies, waits for them, and re-layouts  1.94 us (4%)
  other arithmetic  0.96 us (2%)
  between operations  0.72 us (2%)
    pallas_call x1, Pallas kernels, mixer(): pl.pallas_call(functools.partial(mixer_kernel, rows, *scales), in_specs=[...  15.8 us
    pallas_call x2, Pallas kernels, half_part(): pl.pallas_call(functools.partial(half_kernel, rows, edge), in_specs=[HBM]...  9.69 us
    ppermute x4, starting transfers between devices, exchanged(): lax.ppermute(x, AXES, [(i, i ^ bits) for i in range(size)]).astype(F32)  5.57 us
    ppermute x4, waiting for transfers between devices, exchanged(): lax.ppermute(x, AXES, [(i, i ^ bits) for i in range(size)]).astype(F32)  5 us
    ppermute x1, starting transfers between devices, tap_halves(): return (long_filter, lax.ppermute(long_filter, 'fsdp', [(0, 1), (1, 0)]))  2.51 us
    ppermute x1, starting transfers between devices, swapped(): lax.ppermute(far, axis, far_route)  1.4 us
    convert_element_type x1, other arithmetic, sum_rest(): sent = x.astype(BF16)  0.92 us
  transfers between devices with their start and end apart: 7, of which 4 were waited for; matrix products, arithmetic and copies ran while one was open for 0% of the time, Pallas kernels for 11%

profile of v3, /device:TPU:0, one launch (start us, length us, event | category | flops | bytes accessed | tf_op | source)
XLA Modules:
  0.0 44.1 jit_solution(212609244907297913)
XLA Ops:
  0.6 0.0 copy-start
  0.6 4.9 %edge_half.1 = (f32[8,2,128,128]{3,2,1,0:T(8,128)}, bf16[8,128,128]{2,1,0:T(8,128)(2,1)}, bf16[8,176,128]{2,1,0:T(8,128)(2,1)}, bf16[8,176,128]{2,1,0:T(8,128)(2,1)}) custom-call(s32[1,256]{1,0:T(1,128)} %ids_hbm.3, f32[3,7,1024]{2,1,0:T(8,128)} %w_hbm.5, bf16[1,256,1024]{2,1,0:T(8,128)(2,1)} %q_hbm.5, bf16[1,256,1024]{2,1,0:T(8,128)(2,1)} %k_hbm.5, ...), custom_call_target="tpu_custom_call" | custom-call | flops 8000000000 | bytes 16000000 | tf_op jit(solution)/shard_map/edge_half/pallas_call | solution.py:229
  5.5 0.5 %collective-permute-start.1 = (bf16[8,176,128]{2,1,0:T(8,128)(2,1)}, bf16[8,176,128]{2,1,0:T(8,128)(2,1)}, u32[]{:S(2)}, u32[]{:S(2)}) collective-permute-start(bf16[8,176,128]{2,1,0:T(8,128)(2,1)} %get-tuple-element.23.sent_near_hbm), channel_id=1, source_target_pairs={{0,4},{4,0},{8,12},{12,8},{1,5},{5,1},{9,13},{13,9},{2,6},{6,2},{1... | collective-permute-start | bytes 1081352 | tf_op jit(solution)/shard_map/ppermute | solution.py:31
  6.0 1.4 %collective-permute-start.2 = (bf16[8,176,128]{2,1,0:T(8,128)(2,1)}, bf16[8,176,128]{2,1,0:T(8,128)(2,1)}, u32[]{:S(2)}, u32[]{:S(2)}) collective-permute-start(bf16[8,176,128]{2,1,0:T(8,128)(2,1)} %get-tuple-element.24.sent_far_hbm), channel_id=1, source_target_pairs={{8,4},{4,8},{9,5},{5,9},{10,6},{6,10},{11,7},{7,11},{24,20},{20,24... | collective-permute-start | bytes 1081352 | tf_op jit(solution)/shard_map/ppermute | solution.py:31
  7.4 0.0 copy-done
  7.4 2.5 %collective-permute-start = (bf16[64,64]{1,0:T(8,128)(2,1)S(1)}, bf16[64,64]{1,0:T(8,128)(2,1)S(1)}, u32[]{:S(2)}, u32[]{:S(2)}) collective-permute-start(bf16[64,64]{1,0:T(8,128)(2,1)S(1)} %copy-done), channel_id=1, source_target_pairs={{0,16},{16,0},{1,17},{17,1},{2,18},{18,2},{3,19},{19,3},{4,20},{20... | collective-permute-start | bytes 24584 | tf_op jit(solution)/shard_map/ppermute | solution.py:787
  10.0 4.8 %other_half.1 = (f32[8,2,128,128]{3,2,1,0:T(8,128)}, bf16[8,128,128]{2,1,0:T(8,128)(2,1)}, bf16[8,128,128]{2,1,0:T(8,128)(2,1)}, bf16[8,128,128]{2,1,0:T(8,128)(2,1)}) custom-call(s32[1,256]{1,0:T(1,128)} %ids_hbm.3, f32[3,7,1024]{2,1,0:T(8,128)} %w_hbm.5, bf16[1,256,1024]{2,1,0:T(8,128)(2,1)} %q_hbm.5, bf16[1,256,1024]{2,1,0:T(8,128)(2,1)} %k_hbm.5, ...), custom_call_target="tpu_custom_call" | custom-call | flops 8000000000 | bytes 16000000 | tf_op jit(solution)/shard_map/other_half/pallas_call | solution.py:229
  14.8 0.0 collective-permute-done.other_half_hbm
  14.8 0.0 copy-start.1
  14.8 0.0 collective-permute-done.1.near_hbm
  14.8 0.0 collective-permute-done.2.far_hbm
  14.8 0.6 %copy-done.1 = bf16[64,64]{1,0:T(8,128)(2,1)} copy-done((bf16[64,64]{1,0:T(8,128)(2,1)}, bf16[64,64]{1,0:T(8,128)(2,1)S(1)}, u32[]{:S(2)}) %copy-start.1) | copy-done | bytes 8216
  15.4 15.8 %mixer.1 = (bf16[1,256,1024]{2,1,0:T(8,128)(2,1)}, bf16[1,256,1024]{2,1,0:T(8,128)(2,1)}, bf16[1,256,1024]{2,1,0:T(8,128)(2,1)}, f32[32,1024]{1,0:T(8,128)}) custom-call(s32[1,256]{1,0:T(1,128)} %ids_hbm.3, bf16[64,64]{1,0:T(8,128)(2,1)} %one_half_hbm.1, bf16[64,64]{1,0:T(8,128)(2,1)} %copy-done.1, f32[3,7,1024]{2,1,0:T(8,128)} %w_hbm.5, ...), custom_call_target="tpu_custom_call" | custom-call | tf_op jit(solution)/shard_map/mixer/pallas_call | solution.py:704
  31.2 2.0 %collective-permute-start.3 = (f32[32,1024]{1,0:T(8,128)}, f32[32,1024]{1,0:T(8,128)S(1)}, u32[]{:S(2)}, u32[]{:S(2)}) collective-permute-start(f32[32,1024]{1,0:T(8,128)} %get-tuple-element.34), channel_id=1, source_target_pairs={{0,4},{4,0},{8,12},{12,8},{16,20},{20,16},{24,28},{28,24},{1,5},{5... | collective-permute-start | bytes 393224 | tf_op jit(solution)/shard_map/ppermute | solution.py:766
  33.2 1.2 %collective-permute-done.3 = f32[32,1024]{1,0:T(8,128)S(1)} collective-permute-done((f32[32,1024]{1,0:T(8,128)}, f32[32,1024]{1,0:T(8,128)S(1)}, u32[]{:S(2)}, u32[]{:S(2)}) %collective-permute-start.3) | collective-permute-done | bytes 131104 | tf_op jit(solution)/shard_map/ppermute | solution.py:766
  34.4 0.9 %add_convert_fusion = bf16[32,1024]{1,0:T(8,128)(2,1)S(1)} fusion(f32[32,1024]{1,0:T(8,128)} %get-tuple-element.34, f32[32,1024]{1,0:T(8,128)S(1)} %collective-permute-done.3), kind=kLoop, calls=%fused_computation.1 | loop fusion | flops 65536 | bytes 327680 | tf_op jit(solution)/shard_map/convert_element_type | solution.py:777
  35.3 1.2 %collective-permute-start.4 = (bf16[32,1024]{1,0:T(8,128)(2,1)S(1)}, bf16[32,1024]{1,0:T(8,128)(2,1)S(1)}, u32[]{:S(2)}, u32[]{:S(2)}) collective-permute-start(bf16[32,1024]{1,0:T(8,128)(2,1)S(1)} %add_convert_fusion), channel_id=1, source_target_pairs={{0,8},{4,12},{8,0},{12,4},{16,24},{20,28},{24,16},{28,20},{1,9},{5... | collective-permute-start | bytes 196616 | tf_op jit(solution)/shard_map/ppermute | solution.py:766
  36.5 1.0 %collective-permute-start.5 = (bf16[32,1024]{1,0:T(8,128)(2,1)S(1)}, bf16[32,1024]{1,0:T(8,128)(2,1)S(1)}, u32[]{:S(2)}, u32[]{:S(2)}) collective-permute-start(bf16[32,1024]{1,0:T(8,128)(2,1)S(1)} %add_convert_fusion), channel_id=1, source_target_pairs={{0,16},{4,20},{8,24},{12,28},{16,0},{20,4},{24,8},{28,12},{1,17},{... | collective-permute-start | bytes 196616 | tf_op jit(solution)/shard_map/ppermute | solution.py:766
  37.5 1.4 %collective-permute-start.6 = (bf16[32,1024]{1,0:T(8,128)(2,1)S(1)}, bf16[32,1024]{1,0:T(8,128)(2,1)S(1)}, u32[]{:S(2)}, u32[]{:S(2)}) collective-permute-start(bf16[32,1024]{1,0:T(8,128)(2,1)S(1)} %add_convert_fusion), channel_id=1, source_target_pairs={{0,24},{4,28},{8,16},{12,20},{16,8},{20,12},{24,0},{28,4},{1,25},{... | collective-permute-start | bytes 196616 | tf_op jit(solution)/shard_map/ppermute | solution.py:766
  38.9 0.9 %collective-permute-done.4 = bf16[32,1024]{1,0:T(8,128)(2,1)S(1)} collective-permute-done((bf16[32,1024]{1,0:T(8,128)(2,1)S(1)}, bf16[32,1024]{1,0:T(8,128)(2,1)S(1)}, u32[]{:S(2)}, u32[]{:S(2)}) %collective-permute-start.4) | collective-permute-done | bytes 65568 | tf_op jit(solution)/shard_map/ppermute | solution.py:766
  39.7 1.7 %collective-permute-done.5 = bf16[32,1024]{1,0:T(8,128)(2,1)S(1)} collective-permute-done((bf16[32,1024]{1,0:T(8,128)(2,1)S(1)}, bf16[32,1024]{1,0:T(8,128)(2,1)S(1)}, u32[]{:S(2)}, u32[]{:S(2)}) %collective-permute-start.5) | collective-permute-done | bytes 65568 | tf_op jit(solution)/shard_map/ppermute | solution.py:766
  41.4 1.3 %collective-permute-done.6 = bf16[32,1024]{1,0:T(8,128)(2,1)S(1)} collective-permute-done((bf16[32,1024]{1,0:T(8,128)(2,1)S(1)}, bf16[32,1024]{1,0:T(8,128)(2,1)S(1)}, u32[]{:S(2)}, u32[]{:S(2)}) %collective-permute-start.6) | collective-permute-done | bytes 65568 | tf_op jit(solution)/shard_map/ppermute | solution.py:766
  42.8 0.7 %reshape.21 = f32[3,7,1024]{2,1,0:T(8,128)} reshape(f32[21,1024]{1,0:T(8,128)S(1)} %slice.9) | data formatting | bytes 172032 | tf_op jit(solution)/shard_map/reshape | solution.py:817
  43.4 0.7 %constant_dynamic-slice_fusion = f32[64,64]{1,0:T(8,128)} fusion(f32[64,128]{1,0:T(8,128)S(1)} %slice_bitcast_fusion, s32[]{:T(128)S(6)} %select_n.3), kind=kLoop, calls=%fused_computation.3 | loop fusion | bytes 32772 | tf_op jit(solution)/shard_map/dynamic_slice | solution.py:821
  (3 shorter events, 0.0 us)
Async XLA Ops:
  0.6 6.8 %copy-start = (bf16[64,64]{1,0:T(8,128)(2,1)S(1)}, bf16[64,64]{1,0:T(8,128)(2,1)}, u32[]{:S(2)}) copy-start(bf16[64,64]{1,0:T(8,128)(2,1)} %one_half_hbm.1) | copy-start | bytes 24580
  5.5 9.3 %collective-permute-start.1 = (bf16[8,176,128]{2,1,0:T(8,128)(2,1)}, bf16[8,176,128]{2,1,0:T(8,128)(2,1)}, u32[]{:S(2)}, u32[]{:S(2)}) collective-permute-start(bf16[8,176,128]{2,1,0:T(8,128)(2,1)} %get-tuple-element.23.sent_near_hbm), channel_id=1, source_target_pairs={{0,4},{4,0},{8,12},{12,8},{1,5},{5,1},{9,13},{13,9},{2,6},{6,2},{1... | collective-permute-start | bytes 1081352 | tf_op jit(solution)/shard_map/ppermute | solution.py:31
  6.0 8.8 %collective-permute-start.2 = (bf16[8,176,128]{2,1,0:T(8,128)(2,1)}, bf16[8,176,128]{2,1,0:T(8,128)(2,1)}, u32[]{:S(2)}, u32[]{:S(2)}) collective-permute-start(bf16[8,176,128]{2,1,0:T(8,128)(2,1)} %get-tuple-element.24.sent_far_hbm), channel_id=1, source_target_pairs={{8,4},{4,8},{9,5},{5,9},{10,6},{6,10},{11,7},{7,11},{24,20},{20,24... | collective-permute-start | bytes 1081352 | tf_op jit(solution)/shard_map/ppermute | solution.py:31
  7.4 7.3 %collective-permute-start = (bf16[64,64]{1,0:T(8,128)(2,1)S(1)}, bf16[64,64]{1,0:T(8,128)(2,1)S(1)}, u32[]{:S(2)}, u32[]{:S(2)}) collective-permute-start(bf16[64,64]{1,0:T(8,128)(2,1)S(1)} %copy-done), channel_id=1, source_target_pairs={{0,16},{16,0},{1,17},{17,1},{2,18},{18,2},{3,19},{19,3},{4,20},{20... | collective-permute-start | bytes 24584 | tf_op jit(solution)/shard_map/ppermute | solution.py:787
  14.8 0.6 %copy-start.1 = (bf16[64,64]{1,0:T(8,128)(2,1)}, bf16[64,64]{1,0:T(8,128)(2,1)S(1)}, u32[]{:S(2)}) copy-start(bf16[64,64]{1,0:T(8,128)(2,1)S(1)} %collective-permute-done.other_half_hbm) | copy-start | bytes 24580
  31.2 3.2 %collective-permute-start.3 = (f32[32,1024]{1,0:T(8,128)}, f32[32,1024]{1,0:T(8,128)S(1)}, u32[]{:S(2)}, u32[]{:S(2)}) collective-permute-start(f32[32,1024]{1,0:T(8,128)} %get-tuple-element.34), channel_id=1, source_target_pairs={{0,4},{4,0},{8,12},{12,8},{16,20},{20,16},{24,28},{28,24},{1,5},{5... | collective-permute-start | bytes 393224 | tf_op jit(solution)/shard_map/ppermute | solution.py:766
  35.3 4.4 %collective-permute-start.4 = (bf16[32,1024]{1,0:T(8,128)(2,1)S(1)}, bf16[32,1024]{1,0:T(8,128)(2,1)S(1)}, u32[]{:S(2)}, u32[]{:S(2)}) collective-permute-start(bf16[32,1024]{1,0:T(8,128)(2,1)S(1)} %add_convert_fusion), channel_id=1, source_target_pairs={{0,8},{4,12},{8,0},{12,4},{16,24},{20,28},{24,16},{28,20},{1,9},{5... | collective-permute-start | bytes 196616 | tf_op jit(solution)/shard_map/ppermute | solution.py:766
  36.5 4.9 %collective-permute-start.5 = (bf16[32,1024]{1,0:T(8,128)(2,1)S(1)}, bf16[32,1024]{1,0:T(8,128)(2,1)S(1)}, u32[]{:S(2)}, u32[]{:S(2)}) collective-permute-start(bf16[32,1024]{1,0:T(8,128)(2,1)S(1)} %add_convert_fusion), channel_id=1, source_target_pairs={{0,16},{4,20},{8,24},{12,28},{16,0},{20,4},{24,8},{28,12},{1,17},{... | collective-permute-start | bytes 196616 | tf_op jit(solution)/shard_map/ppermute | solution.py:766
  37.5 5.2 %collective-permute-start.6 = (bf16[32,1024]{1,0:T(8,128)(2,1)S(1)}, bf16[32,1024]{1,0:T(8,128)(2,1)S(1)}, u32[]{:S(2)}, u32[]{:S(2)}) collective-permute-start(bf16[32,1024]{1,0:T(8,128)(2,1)S(1)} %add_convert_fusion), channel_id=1, source_target_pairs={{0,24},{4,28},{8,16},{12,20},{16,8},{20,12},{24,0},{28,4},{1,25},{... | collective-permute-start | bytes 196616 | tf_op jit(solution)/shard_map/ppermute | solution.py:766

commit v4 on v3

--- a/solution.py
+++ b/solution.py
@@ -14,7 +14,7 @@
 GROUP = 16
 EDGE = 8
 VMEM_LIMIT = 65300 << 10
-HEAD_ROWS = LANES + 48
+HEAD_ROWS = LANES + 32
 F32 = jnp.float32
 BF16 = jnp.bfloat16
 NT = (((1,), (1,)), ((), ()))
@@ -135,7 +135,7 @@
     for b in range(2):
         idc[EDGE + TAPS * b : EDGE + TAPS * (b + 1)] = spread(ids[:, TAPS * b : TAPS * (b + 1)])
     for x in (xq, xk, xv):
-        x[0:lead] = jnp.zeros((lead, LANES), F32)
+        x[:, 0:lead] = jnp.zeros((2, lead, LANES), F32)
 
     def masks(i, carry):
         base = pl.multiple_of(16 * i, 16)
@@ -148,63 +148,77 @@
     pad = jnp.zeros((EDGE - 2, LANES), F32)
     id_rows = [ids[:, TAPS * b : TAPS * (b + 1)] for b in range(2)]
     id_tile = jnp.concatenate(id_rows + [pad], axis=0)
+    id_late = jnp.concatenate([pad] + id_rows, axis=0)
+    sub = lax.broadcasted_iota(jnp.int32, (EDGE, LANES), 0)
     part = 32
 
     def pair(a, b):
         return jnp.concatenate([a, b], axis=0).astype(BF16)
 
-    def one_block(i, carry):
-        lane = lanes_of(i)
-        copy_all(inputs(i), in_sems, i, wait=True)
-        w = [[w_ref[n, j : j + 1, lane] for j in range(SHORT)] for n in range(3)]
-        for x, source, low in ((xq, bq, q_low), (xk, bk, kv_low), (xv, bv, kv_low)):
-            if low:
-                x[0:lead] = source[low - lead : low, lane].astype(F32)
-            size = TAPS if low else TAPS + lead
-            x[lead : lead + size] = source[low : low + size, lane].astype(F32)
-
-        def filtered(x, taps, low, at, size):
-            total = taps[0] * x[pl.ds(at + lead, size), :]
-            for j in range(1, SHORT):
-                mask = mj[j - 1, pl.ds(at + low, size), :]
-                total += taps[j] * (mask * x[pl.ds(at + lead - j, size), :])
-            return total
+    def filtered(x, h, taps, low, at, size):
+        total = taps[0] * x[h, pl.ds(at + lead, size), :]
+        for j in range(1, SHORT):
+            mask = mj[j - 1, pl.ds(at + low, size), :]
+            total += taps[j] * (mask * x[h, pl.ds(at + lead - j, size), :])
+        return total
+
+    def two_blocks(half, carry):
+        pair_of = [2 * half, 2 * half + 1]
+        for h, i in enumerate(pair_of):
+            lane = lanes_of(i)
+            copy_all(inputs(i), in_sems, i, wait=True)
+            for x, source, low in ((xq, bq, q_low), (xk, bk, kv_low), (xv, bv, kv_low)):
+                if low:
+                    x[h, 0:lead] = source[low - lead : low, lane].astype(F32)
+                size = TAPS if low else TAPS + lead
+                x[h, lead : lead + size] = source[low : low + size, lane].astype(F32)
+
+        def taps_of(n, i):
+            return [w_ref[n, j : j + 1, lanes_of(i)] for j in range(SHORT)]
 
         def convolve(n, inner):
             at = pl.multiple_of(part * n, part)
-            key = filtered(xk, w[1], kv_low, at, part)
-            value = filtered(xv, w[2], kv_low, at, part)
-            query = filtered(xq, w[0], q_low, at, part)
-            conv_ref[i, 0, pl.ds(at, part), :] = key
-            conv_ref[i, 1, pl.ds(at, part), :] = value
-            uf[pl.ds(at, part), :] = key * value
-            dz = bg[pl.ds(at + q_low, part), lane].astype(F32) * query
-            dzf[pl.ds(at, part), :] = dz
-            dzr_ref[i, pl.ds(at, part), :] = dz.astype(BF16)
+            for h, i in enumerate(pair_of):
+                key = filtered(xk, h, taps_of(1, i), kv_low, at, part)
+                value = filtered(xv, h, taps_of(2, i), kv_low, at, part)
+                query = filtered(xq, h, taps_of(0, i), q_low, at, part)
+                conv_ref[i, 0, pl.ds(at, part), :] = key
+                conv_ref[i, 1, pl.ds(at, part), :] = value
+                uf[h, pl.ds(at, part), :] = key * value
+                dz = bg[pl.ds(at + q_low, part), lanes_of(i)].astype(F32) * query
+                dzf[h, pl.ds(at, part), :] = dz
+                dzr_ref[i, pl.ds(at, part), :] = dz.astype(BF16)
             return inner
 
         lax.fori_loop(0, TAPS // part, convolve, 0)
-        one_ref[i, 0:LANES, :] = uf[...].T.astype(BF16)
-        two_ref[i, 0:LANES, :] = dzf[...].T.astype(BF16)
-        if edge:
-            beyond = bg[TAPS : TAPS + 16, lane].astype(F32)[:EDGE]
-            beyond = beyond * filtered(xq, w[0], q_low, TAPS, EDGE)
-            last = slice(lead + TAPS - EDGE, lead + TAPS)
-            q_last = bq[rows - 16 : rows, lane].astype(F32)[EDGE:]
-            k_first = bk[0:16, lane].astype(F32)[:EDGE]
-            v_first = bv[0:16, lane].astype(F32)[:EDGE]
-            g_first = bg[0:16, lane].astype(F32)[:EDGE]
-            one_ref[i, LANES : LANES + 16, :] = pair(xk[last, :], xv[last, :])
-            one_ref[i, LANES + 16 : LANES + 32, :] = pair(q_last, id_tile)
-            one_ref[i, LANES + 32 : LANES + 48, :] = jnp.zeros((16, LANES), BF16)
-            two_ref[i, LANES : LANES + 16, :] = pair(xq[lead : lead + EDGE, :], g_first)
-            two_ref[i, LANES + 16 : LANES + 32, :] = pair(k_first, v_first)
-            two_ref[i, LANES + 32 : LANES + 48, :] = pair(beyond, id_tile)
-        send_packets(i)
-        copy_all(outputs(i), out_sems, i)
+        for h, i in enumerate(pair_of):
+            one_ref[i, 0:LANES, :] = uf[h].T.astype(BF16)
+            two_ref[i, 0:LANES, :] = dzf[h].T.astype(BF16)
+            if edge:
+                lane = lanes_of(i)
+                beyond = bg[TAPS : TAPS + 16, lane].astype(F32)[:EDGE]
+                beyond = beyond * filtered(xq, h, taps_of(0, i), q_low, TAPS, EDGE)
+                last = slice(lead + TAPS - EDGE, lead + TAPS)
+                q_last = bq[rows - 16 : rows, lane].astype(F32)[EDGE:]
+                k_first = bk[0:16, lane].astype(F32)[:EDGE]
+                v_first = bv[0:16, lane].astype(F32)[:EDGE]
+                g_first = bg[0:16, lane].astype(F32)[:EDGE]
+                q_first = xq[h, lead : lead + EDGE, :]
+                one_ref[i, LANES : LANES + 16, :] = pair(xk[h, last, :], xv[h, last, :])
+                one_ref[i, LANES + 16 : LANES + 32, :] = pair(q_last, id_tile)
+                late = sub >= EDGE - 2
+                q_first = jnp.where(late, id_late, q_first)
+                g_first = jnp.where(late, pltpu.roll(beyond, 6, 0), g_first)
+                k_first = jnp.where(late, pltpu.roll(beyond, 4, 0), k_first)
+                v_first = jnp.where(late, pltpu.roll(beyond, 2, 0), v_first)
+                two_ref[i, LANES : LANES + 16, :] = pair(q_first, g_first)
+                two_ref[i, LANES + 16 : LANES + 32, :] = pair(k_first, v_first)
+        for i in pair_of:
+            send_packets(i)
+            copy_all(outputs(i), out_sems, i)
         return carry
 
-    lax.fori_loop(0, count, one_block, 0)
+    lax.fori_loop(0, count // 2, two_blocks, 0)
 
     def drain(i, carry):
         copy_all(packets(i)[0], packet_sems, i, wait=True)
@@ -238,9 +252,9 @@
             *[pltpu.VMEM(*r) for r in results],
             vm(rows + EDGE, LANES),
             vm(SHORT - 1, rows, LANES),
-            *[vm(TAPS + 32, LANES)] * 3,
-            vm(TAPS, LANES),
-            vm(TAPS, LANES),
+            *[vm(2, TAPS + 32, LANES)] * 3,
+            vm(2, TAPS, LANES),
+            vm(2, TAPS, LANES),
             pltpu.SemaphoreType.DMA((1, 2)),
             pltpu.SemaphoreType.DMA((count, 4)),
             pltpu.SemaphoreType.DMA((count, 2)),
@@ -406,11 +420,11 @@
     col = lax.broadcasted_iota(jnp.int32, (TAPS, TAPS), 1)
     own_ids = (ids_ref[...] + 1).astype(F32)
     prev_ids = prev_ref[0, LANES + 16 : LANES + 32, :].astype(F32)
-    next_ids = next_ref[0, LANES + 32 : LANES + 48, :].astype(F32)
+    next_ids = next_ref[0, LANES : LANES + 16, :].astype(F32)
     for b in range(blocks):
         idr[b : b + 1, :] = prev_ids[EDGE + b : EDGE + b + 1]
         idr[blocks + b : blocks + b + 1, :] = own_ids[:, TAPS * b : TAPS * (b + 1)]
-        idr[2 * blocks + b : 2 * blocks + b + 1, :] = next_ids[EDGE + b : EDGE + b + 1]
+        idr[2 * blocks + b : 2 * blocks + b + 1, :] = next_ids[EDGE - blocks + b : EDGE - blocks + b + 1]
     for b in range(3 * blocks):
         idc[TAPS * b : TAPS * (b + 1), :] = spread(idr[b : b + 1, :])
 
@@ -455,6 +469,8 @@
     lane_group = col // GROUP
     lower_flipped = row + col >= TAPS - 1
     first_lanes = col < EDGE
+    next_lanes = col < SHORT - 1
+    sub = lax.broadcasted_iota(jnp.int32, (EDGE, LANES), 0)
     blank = jnp.zeros((TAPS - EDGE, LANES), F32)
 
     def turned(x):
@@ -469,7 +485,15 @@
         prev_q = prev_ref[i, LANES + 16 : LANES + 32, :].astype(F32)
         next_qg = next_ref[i, LANES : LANES + 16, :].astype(F32)
         next_kv = next_ref[i, LANES + 16 : LANES + 32, :].astype(F32)
-        next_dz = next_ref[i, LANES + 32 : LANES + 48, :].astype(F32)
+        next_dz = jnp.where(
+            sub < 2,
+            pltpu.roll(next_qg[EDGE:], 2, 0),
+            jnp.where(
+                sub < 4,
+                pltpu.roll(next_kv[:EDGE], 4, 0),
+                jnp.where(sub < 5, pltpu.roll(next_kv[EDGE:], 6, 0), 0.0),
+            ),
+        )
         for n, (source, before, after) in enumerate(
             (
                 (bq, prev_q[:EDGE], next_qg[:EDGE]),
@@ -503,7 +527,7 @@
         dzt[:, 0:TAPS] = jnp.where(first_lanes, turned(fixed[0][3]), head_ref[i, 0:LANES, :])
         dzt[:, TAPS : 2 * TAPS] = dz_late[i]
         dzt[:, 2 * TAPS : 3 * TAPS] = jnp.where(
-            first_lanes, turned(fixed[1][3]), next_ref[i, 0:LANES, :]
+            next_lanes, turned(fixed[1][3]), next_ref[i, 0:LANES, :]
         )
         dzt[:, 3 * TAPS :] = turned(next_dz[:EDGE])
         dzr[0:TAPS] = dzr_early[i]
@@ -642,12 +666,10 @@
     part_ref[3 * SHORT : 24, :] = jnp.zeros((24 - 3 * SHORT, part_ref.shape[1]), F32)
 
     def long_block(i, between):
-        make_bands(i, 0, 0)
         multiply_taps()
         for m in range(per):
-            if m + 1 < per:
-                make_bands(i, m + 1, (m + 1) % 2)
-            multiply(m, m % 2)
+            make_bands(i, m, m)
+            multiply(m, m)
             sum_taps(i, m)
             between(m)
 
@@ -744,7 +766,7 @@
             vm(rows + 16, LANES),
             vm(channels // GROUP, 8, TAPS),
             vm(2, 2, EDGE, LANES),
-            vb(2, TAPS, TAPS),
+            vb(LANES // GROUP, TAPS, TAPS),
             vb(LANES, TAPS),
             vb(LANES, TAPS),
             vm(LANES // GROUP, TAPS, TAPS),

time: 44.3 us -> 43.4 us (0.980)
  Pallas kernels: 25.5 us -> 24.4 us
    pallas_call x2, Pallas kernels: 9.69 us -> 8.88 us  [half_part(): pl.pallas_call(functools.partial(half_kernel, rows, edge), in_specs=[HBM]...]
  transfers between devices with their start and end apart: 7 -> 7, of which waited for: 4 -> 4; matrix products, arithmetic and copies ran while one was open for 0% -> 0% of each run, Pallas kernels for 11% -> 10%
where the time goes in v4:
time: 43.4 us; the launch traced here: 43.1 us
  Pallas kernels  24.4 us (56%)
  starting transfers between devices  10 us (23%)
  waiting for transfers between devices  5.09 us (12%)
  local copies, waits for them, and re-layouts  1.94 us (4%)
  other arithmetic  0.96 us (2%)
  between operations  0.72 us (2%)
    pallas_call x1, Pallas kernels, mixer(): pl.pallas_call(functools.partial(mixer_kernel, rows, *scales), in_specs=[...  15.5 us
    pallas_call x2, Pallas kernels, half_part(): pl.pallas_call(functools.partial(half_kernel, rows, edge), in_specs=[HBM]...  8.88 us
    ppermute x4, starting transfers between devices, exchanged(): lax.ppermute(x, AXES, [(i, i ^ bits) for i in range(size)]).astype(F32)  5.59 us
    ppermute x4, waiting for transfers between devices, exchanged(): lax.ppermute(x, AXES, [(i, i ^ bits) for i in range(size)]).astype(F32)  5.09 us
    ppermute x1, starting transfers between devices, tap_halves(): return (long_filter, lax.ppermute(long_filter, 'fsdp', [(0, 1), (1, 0)]))  2.51 us
    ppermute x1, starting transfers between devices, swapped(): lax.ppermute(far, axis, far_route)  1.39 us
    convert_element_type x1, other arithmetic, sum_rest(): sent = x.astype(BF16)  0.92 us
  transfers between devices with their start and end apart: 7, of which 4 were waited for; matrix products, arithmetic and copies ran while one was open for 0% of the time, Pallas kernels for 10%

profile of v4, /device:TPU:0, one launch (start us, length us, event | category | flops | bytes accessed | tf_op | source)
XLA Modules:
  0.0 43.1 jit_solution(4724787015983561272)
XLA Ops:
  0.6 0.0 copy-start
  0.6 4.5 %edge_half.1 = (f32[8,2,128,128]{3,2,1,0:T(8,128)}, bf16[8,128,128]{2,1,0:T(8,128)(2,1)}, bf16[8,160,128]{2,1,0:T(8,128)(2,1)}, bf16[8,160,128]{2,1,0:T(8,128)(2,1)}) custom-call(s32[1,256]{1,0:T(1,128)} %ids_hbm.3, f32[3,7,1024]{2,1,0:T(8,128)} %w_hbm.5, bf16[1,256,1024]{2,1,0:T(8,128)(2,1)} %q_hbm.5, bf16[1,256,1024]{2,1,0:T(8,128)(2,1)} %k_hbm.5, ...), custom_call_target="tpu_custom_call" | custom-call | flops 8000000000 | bytes 16000000 | tf_op jit(solution)/shard_map/edge_half/pallas_call | solution.py:243
  5.1 0.5 %collective-permute-start.1 = (bf16[8,160,128]{2,1,0:T(8,128)(2,1)}, bf16[8,160,128]{2,1,0:T(8,128)(2,1)}, u32[]{:S(2)}, u32[]{:S(2)}) collective-permute-start(bf16[8,160,128]{2,1,0:T(8,128)(2,1)} %get-tuple-element.23.sent_near_hbm), channel_id=1, source_target_pairs={{0,4},{4,0},{8,12},{12,8},{1,5},{5,1},{9,13},{13,9},{2,6},{6,2},{1... | collective-permute-start | bytes 983048 | tf_op jit(solution)/shard_map/ppermute | solution.py:31
  5.7 1.4 %collective-permute-start.2 = (bf16[8,160,128]{2,1,0:T(8,128)(2,1)}, bf16[8,160,128]{2,1,0:T(8,128)(2,1)}, u32[]{:S(2)}, u32[]{:S(2)}) collective-permute-start(bf16[8,160,128]{2,1,0:T(8,128)(2,1)} %get-tuple-element.24.sent_far_hbm), channel_id=1, source_target_pairs={{8,4},{4,8},{9,5},{5,9},{10,6},{6,10},{11,7},{7,11},{24,20},{20,24... | collective-permute-start | bytes 983048 | tf_op jit(solution)/shard_map/ppermute | solution.py:31
  7.1 0.0 copy-done
  7.1 2.5 %collective-permute-start = (bf16[64,64]{1,0:T(8,128)(2,1)S(1)}, bf16[64,64]{1,0:T(8,128)(2,1)S(1)}, u32[]{:S(2)}, u32[]{:S(2)}) collective-permute-start(bf16[64,64]{1,0:T(8,128)(2,1)S(1)} %copy-done), channel_id=1, source_target_pairs={{0,16},{16,0},{1,17},{17,1},{2,18},{18,2},{3,19},{19,3},{4,20},{20... | collective-permute-start | bytes 24584 | tf_op jit(solution)/shard_map/ppermute | solution.py:809
  9.6 4.4 %other_half.1 = (f32[8,2,128,128]{3,2,1,0:T(8,128)}, bf16[8,128,128]{2,1,0:T(8,128)(2,1)}, bf16[8,128,128]{2,1,0:T(8,128)(2,1)}, bf16[8,128,128]{2,1,0:T(8,128)(2,1)}) custom-call(s32[1,256]{1,0:T(1,128)} %ids_hbm.3, f32[3,7,1024]{2,1,0:T(8,128)} %w_hbm.5, bf16[1,256,1024]{2,1,0:T(8,128)(2,1)} %q_hbm.5, bf16[1,256,1024]{2,1,0:T(8,128)(2,1)} %k_hbm.5, ...), custom_call_target="tpu_custom_call" | custom-call | flops 8000000000 | bytes 16000000 | tf_op jit(solution)/shard_map/other_half/pallas_call | solution.py:243
  14.0 0.0 collective-permute-done.other_half_hbm
  14.0 0.0 copy-start.1
  14.0 0.0 collective-permute-done.1.near_hbm
  14.0 0.0 collective-permute-done.2.far_hbm
  14.0 0.6 %copy-done.1 = bf16[64,64]{1,0:T(8,128)(2,1)} copy-done((bf16[64,64]{1,0:T(8,128)(2,1)}, bf16[64,64]{1,0:T(8,128)(2,1)S(1)}, u32[]{:S(2)}) %copy-start.1) | copy-done | bytes 8216
  14.6 15.5 %mixer.1 = (bf16[1,256,1024]{2,1,0:T(8,128)(2,1)}, bf16[1,256,1024]{2,1,0:T(8,128)(2,1)}, bf16[1,256,1024]{2,1,0:T(8,128)(2,1)}, f32[32,1024]{1,0:T(8,128)}) custom-call(s32[1,256]{1,0:T(1,128)} %ids_hbm.3, bf16[64,64]{1,0:T(8,128)(2,1)} %one_half_hbm.1, bf16[64,64]{1,0:T(8,128)(2,1)} %copy-done.1, f32[3,7,1024]{2,1,0:T(8,128)} %w_hbm.5, ...), custom_call_target="tpu_custom_call" | custom-call | tf_op jit(solution)/shard_map/mixer/pallas_call | solution.py:726
  30.1 2.0 %collective-permute-start.3 = (f32[32,1024]{1,0:T(8,128)}, f32[32,1024]{1,0:T(8,128)S(1)}, u32[]{:S(2)}, u32[]{:S(2)}) collective-permute-start(f32[32,1024]{1,0:T(8,128)} %get-tuple-element.34), channel_id=1, source_target_pairs={{0,4},{4,0},{8,12},{12,8},{16,20},{20,16},{24,28},{28,24},{1,5},{5... | collective-permute-start | bytes 393224 | tf_op jit(solution)/shard_map/ppermute | solution.py:788
  32.1 1.2 %collective-permute-done.3 = f32[32,1024]{1,0:T(8,128)S(1)} collective-permute-done((f32[32,1024]{1,0:T(8,128)}, f32[32,1024]{1,0:T(8,128)S(1)}, u32[]{:S(2)}, u32[]{:S(2)}) %collective-permute-start.3) | collective-permute-done | bytes 131104 | tf_op jit(solution)/shard_map/ppermute | solution.py:788
  33.3 0.9 %add_convert_fusion = bf16[32,1024]{1,0:T(8,128)(2,1)S(1)} fusion(f32[32,1024]{1,0:T(8,128)} %get-tuple-element.34, f32[32,1024]{1,0:T(8,128)S(1)} %collective-permute-done.3), kind=kLoop, calls=%fused_computation.1 | loop fusion | flops 65536 | bytes 327680 | tf_op jit(solution)/shard_map/convert_element_type | solution.py:799
  34.2 1.2 %collective-permute-start.4 = (bf16[32,1024]{1,0:T(8,128)(2,1)S(1)}, bf16[32,1024]{1,0:T(8,128)(2,1)S(1)}, u32[]{:S(2)}, u32[]{:S(2)}) collective-permute-start(bf16[32,1024]{1,0:T(8,128)(2,1)S(1)} %add_convert_fusion), channel_id=1, source_target_pairs={{0,8},{4,12},{8,0},{12,4},{16,24},{20,28},{24,16},{28,20},{1,9},{5... | collective-permute-start | bytes 196616 | tf_op jit(solution)/shard_map/ppermute | solution.py:788
  35.4 1.1 %collective-permute-start.5 = (bf16[32,1024]{1,0:T(8,128)(2,1)S(1)}, bf16[32,1024]{1,0:T(8,128)(2,1)S(1)}, u32[]{:S(2)}, u32[]{:S(2)}) collective-permute-start(bf16[32,1024]{1,0:T(8,128)(2,1)S(1)} %add_convert_fusion), channel_id=1, source_target_pairs={{0,16},{4,20},{8,24},{12,28},{16,0},{20,4},{24,8},{28,12},{1,17},{... | collective-permute-start | bytes 196616 | tf_op jit(solution)/shard_map/ppermute | solution.py:788
  36.5 1.3 %collective-permute-start.6 = (bf16[32,1024]{1,0:T(8,128)(2,1)S(1)}, bf16[32,1024]{1,0:T(8,128)(2,1)S(1)}, u32[]{:S(2)}, u32[]{:S(2)}) collective-permute-start(bf16[32,1024]{1,0:T(8,128)(2,1)S(1)} %add_convert_fusion), channel_id=1, source_target_pairs={{0,24},{4,28},{8,16},{12,20},{16,8},{20,12},{24,0},{28,4},{1,25},{... | collective-permute-start | bytes 196616 | tf_op jit(solution)/shard_map/ppermute | solution.py:788
  37.8 0.9 %collective-permute-done.4 = bf16[32,1024]{1,0:T(8,128)(2,1)S(1)} collective-permute-done((bf16[32,1024]{1,0:T(8,128)(2,1)S(1)}, bf16[32,1024]{1,0:T(8,128)(2,1)S(1)}, u32[]{:S(2)}, u32[]{:S(2)}) %collective-permute-start.4) | collective-permute-done | bytes 65568 | tf_op jit(solution)/shard_map/ppermute | solution.py:788
  38.7 1.7 %collective-permute-done.5 = bf16[32,1024]{1,0:T(8,128)(2,1)S(1)} collective-permute-done((bf16[32,1024]{1,0:T(8,128)(2,1)S(1)}, bf16[32,1024]{1,0:T(8,128)(2,1)S(1)}, u32[]{:S(2)}, u32[]{:S(2)}) %collective-permute-start.5) | collective-permute-done | bytes 65568 | tf_op jit(solution)/shard_map/ppermute | solution.py:788
  40.4 1.3 %collective-permute-done.6 = bf16[32,1024]{1,0:T(8,128)(2,1)S(1)} collective-permute-done((bf16[32,1024]{1,0:T(8,128)(2,1)S(1)}, bf16[32,1024]{1,0:T(8,128)(2,1)S(1)}, u32[]{:S(2)}, u32[]{:S(2)}) %collective-permute-start.6) | collective-permute-done | bytes 65568 | tf_op jit(solution)/shard_map/ppermute | solution.py:788
  41.8 0.7 %reshape.21 = f32[3,7,1024]{2,1,0:T(8,128)} reshape(f32[21,1024]{1,0:T(8,128)S(1)} %slice.9) | data formatting | bytes 172032 | tf_op jit(solution)/shard_map/reshape | solution.py:839
  42.4 0.7 %constant_dynamic-slice_fusion = f32[64,64]{1,0:T(8,128)} fusion(f32[64,128]{1,0:T(8,128)S(1)} %slice_bitcast_fusion, s32[]{:T(128)S(6)} %select_n.3), kind=kLoop, calls=%fused_computation.3 | loop fusion | bytes 32772 | tf_op jit(solution)/shard_map/dynamic_slice | solution.py:843
  (3 shorter events, 0.0 us)
Async XLA Ops:
  0.6 6.4 %copy-start = (bf16[64,64]{1,0:T(8,128)(2,1)S(1)}, bf16[64,64]{1,0:T(8,128)(2,1)}, u32[]{:S(2)}) copy-start(bf16[64,64]{1,0:T(8,128)(2,1)} %one_half_hbm.1) | copy-start | bytes 24580
  5.1 8.8 %collective-permute-start.1 = (bf16[8,160,128]{2,1,0:T(8,128)(2,1)}, bf16[8,160,128]{2,1,0:T(8,128)(2,1)}, u32[]{:S(2)}, u32[]{:S(2)}) collective-permute-start(bf16[8,160,128]{2,1,0:T(8,128)(2,1)} %get-tuple-element.23.sent_near_hbm), channel_id=1, source_target_pairs={{0,4},{4,0},{8,12},{12,8},{1,5},{5,1},{9,13},{13,9},{2,6},{6,2},{1... | collective-permute-start | bytes 983048 | tf_op jit(solution)/shard_map/ppermute | solution.py:31
  5.7 8.3 %collective-permute-start.2 = (bf16[8,160,128]{2,1,0:T(8,128)(2,1)}, bf16[8,160,128]{2,1,0:T(8,128)(2,1)}, u32[]{:S(2)}, u32[]{:S(2)}) collective-permute-start(bf16[8,160,128]{2,1,0:T(8,128)(2,1)} %get-tuple-element.24.sent_far_hbm), channel_id=1, source_target_pairs={{8,4},{4,8},{9,5},{5,9},{10,6},{6,10},{11,7},{7,11},{24,20},{20,24... | collective-permute-start | bytes 983048 | tf_op jit(solution)/shard_map/ppermute | solution.py:31
  7.1 6.9 %collective-permute-start = (bf16[64,64]{1,0:T(8,128)(2,1)S(1)}, bf16[64,64]{1,0:T(8,128)(2,1)S(1)}, u32[]{:S(2)}, u32[]{:S(2)}) collective-permute-start(bf16[64,64]{1,0:T(8,128)(2,1)S(1)} %copy-done), channel_id=1, source_target_pairs={{0,16},{16,0},{1,17},{17,1},{2,18},{18,2},{3,19},{19,3},{4,20},{20... | collective-permute-start | bytes 24584 | tf_op jit(solution)/shard_map/ppermute | solution.py:809
  14.0 0.6 %copy-start.1 = (bf16[64,64]{1,0:T(8,128)(2,1)}, bf16[64,64]{1,0:T(8,128)(2,1)S(1)}, u32[]{:S(2)}) copy-start(bf16[64,64]{1,0:T(8,128)(2,1)S(1)} %collective-permute-done.other_half_hbm) | copy-start | bytes 24580
  30.1 3.2 %collective-permute-start.3 = (f32[32,1024]{1,0:T(8,128)}, f32[32,1024]{1,0:T(8,128)S(1)}, u32[]{:S(2)}, u32[]{:S(2)}) collective-permute-start(f32[32,1024]{1,0:T(8,128)} %get-tuple-element.34), channel_id=1, source_target_pairs={{0,4},{4,0},{8,12},{12,8},{16,20},{20,16},{24,28},{28,24},{1,5},{5... | collective-permute-start | bytes 393224 | tf_op jit(solution)/shard_map/ppermute | solution.py:788
  34.2 4.4 %collective-permute-start.4 = (bf16[32,1024]{1,0:T(8,128)(2,1)S(1)}, bf16[32,1024]{1,0:T(8,128)(2,1)S(1)}, u32[]{:S(2)}, u32[]{:S(2)}) collective-permute-start(bf16[32,1024]{1,0:T(8,128)(2,1)S(1)} %add_convert_fusion), channel_id=1, source_target_pairs={{0,8},{4,12},{8,0},{12,4},{16,24},{20,28},{24,16},{28,20},{1,9},{5... | collective-permute-start | bytes 196616 | tf_op jit(solution)/shard_map/ppermute | solution.py:788
  35.4 4.9 %collective-permute-start.5 = (bf16[32,1024]{1,0:T(8,128)(2,1)S(1)}, bf16[32,1024]{1,0:T(8,128)(2,1)S(1)}, u32[]{:S(2)}, u32[]{:S(2)}) collective-permute-start(bf16[32,1024]{1,0:T(8,128)(2,1)S(1)} %add_convert_fusion), channel_id=1, source_target_pairs={{0,16},{4,20},{8,24},{12,28},{16,0},{20,4},{24,8},{28,12},{1,17},{... | collective-permute-start | bytes 196616 | tf_op jit(solution)/shard_map/ppermute | solution.py:788
  36.5 5.2 %collective-permute-start.6 = (bf16[32,1024]{1,0:T(8,128)(2,1)S(1)}, bf16[32,1024]{1,0:T(8,128)(2,1)S(1)}, u32[]{:S(2)}, u32[]{:S(2)}) collective-permute-start(bf16[32,1024]{1,0:T(8,128)(2,1)S(1)} %add_convert_fusion), channel_id=1, source_target_pairs={{0,24},{4,28},{8,16},{12,20},{16,8},{20,12},{24,0},{28,4},{1,25},{... | collective-permute-start | bytes 196616 | tf_op jit(solution)/shard_map/ppermute | solution.py:788

commit v5 on v4

--- a/solution.py
+++ b/solution.py
@@ -86,6 +86,7 @@
     in_sems,
     out_sems,
     packet_sems,
+    border_sems,
 ):
     count = q_hbm.shape[2] // LANES
     odd = lax.rem(lax.axis_index("ctx"), 2)
@@ -95,18 +96,34 @@
     def small():
         return ((ids_hbm, ids_ref), (w_hbm, w_ref))
 
-    def inputs(i):
-        lane = lanes_of(i)
-        pairs = ((q_hbm, bq), (k_hbm, bk), (v_hbm, bv), (g_hbm, bg))
-        return [(a.at[0, :, lane], b.at[:, lane]) for a, b in pairs]
-
-    def outputs(i):
+    def rows_from(low, before):
+        start = low - before if low else 0
+        return pl.ds(start, rows - start if low else TAPS + lead)
+
+    def inputs(half):
+        lane = pl.ds(pl.multiple_of(2 * LANES * half, 2 * LANES), 2 * LANES)
+        spans = (
+            (q_hbm, bq, rows_from(q_low, lead)),
+            (k_hbm, bk, rows_from(kv_low, lead)),
+            (v_hbm, bv, rows_from(kv_low, lead)),
+            (g_hbm, bg, rows_from(q_low, 0)),
+        )
+        return [(a.at[0, span, lane], b.at[span, lane]) for a, b, span in spans]
+
+    def borders():
+        first, last = pl.ds(0, 16), pl.ds(rows - 16, 16)
+        spans = ((k_hbm, bk, first), (v_hbm, bv, first), (q_hbm, bq, last))
+        return [(a.at[0, span], b.at[span]) for a, b, span in spans]
+
+    def outputs(half):
+        span = pl.ds(2 * half, 2)
         pairs = [(conv_ref, conv_hbm), (dzr_ref, dzr_hbm)]
-        return [(a.at[i], b.at[i]) for a, b in pairs]
-
-    def packets(i):
-        one, two = one_ref.at[i], two_ref.at[i]
-        near, far = one_hbm.at[i], two_hbm.at[i]
+        return [(a.at[span], b.at[span]) for a, b in pairs]
+
+    def packets(half):
+        span = pl.ds(2 * half, 2)
+        one, two = one_ref.at[span], two_ref.at[span]
+        near, far = one_hbm.at[span], two_hbm.at[span]
         return ((one, near), (two, far)), ((two, near), (one, far))
 
     def send_packets(i):
@@ -128,7 +145,9 @@
         copy_all(inputs(i), in_sems, i)
         return carry
 
-    lax.fori_loop(0, count, fetch, 0)
+    lax.fori_loop(0, count // 2, fetch, 0)
+    if edge:
+        copy_all(borders(), border_sems, 0)
     copy_all(small(), small_sems, 0, wait=True)
     ids = (ids_ref[...] + 1).astype(F32)
     idc[0:EDGE] = jnp.zeros((EDGE, LANES), F32)
@@ -164,9 +183,9 @@
 
     def two_blocks(half, carry):
         pair_of = [2 * half, 2 * half + 1]
+        copy_all(inputs(half), in_sems, half, wait=True)
         for h, i in enumerate(pair_of):
             lane = lanes_of(i)
-            copy_all(inputs(i), in_sems, i, wait=True)
             for x, source, low in ((xq, bq, q_low), (xk, bk, kv_low), (xv, bv, kv_low)):
                 if low:
                     x[h, 0:lead] = source[low - lead : low, lane].astype(F32)
@@ -213,11 +232,12 @@
                 v_first = jnp.where(late, pltpu.roll(beyond, 2, 0), v_first)
                 two_ref[i, LANES : LANES + 16, :] = pair(q_first, g_first)
                 two_ref[i, LANES + 16 : LANES + 32, :] = pair(k_first, v_first)
-        for i in pair_of:
-            send_packets(i)
-            copy_all(outputs(i), out_sems, i)
+        send_packets(half)
+        copy_all(outputs(half), out_sems, half)
         return carry
 
+    if edge:
+        copy_all(borders(), border_sems, 0, wait=True)
     lax.fori_loop(0, count // 2, two_blocks, 0)
 
     def drain(i, carry):
@@ -225,7 +245,7 @@
         copy_all(outputs(i), out_sems, i, wait=True)
         return carry
 
-    lax.fori_loop(0, count, drain, 0)
+    lax.fori_loop(0, count // 2, drain, 0)
 
 
 def half_part(edge, ids, short_filter, q_in, k_in, v_in, grad_out):
@@ -256,9 +276,10 @@
             vm(2, TAPS, LANES),
             vm(2, TAPS, LANES),
             pltpu.SemaphoreType.DMA((1, 2)),
-            pltpu.SemaphoreType.DMA((count, 4)),
-            pltpu.SemaphoreType.DMA((count, 2)),
-            pltpu.SemaphoreType.DMA((count, 2)),
+            pltpu.SemaphoreType.DMA((count // 2, 4)),
+            pltpu.SemaphoreType.DMA((count // 2, 2)),
+            pltpu.SemaphoreType.DMA((count // 2, 2)),
+            pltpu.SemaphoreType.DMA((1, 3)),
         ],
         compiler_params=pltpu.CompilerParams(vmem_limit_bytes=VMEM_LIMIT),
         cost_estimate=pl.CostEstimate(

time: 43.4 us -> 43.2 us (level)
  Pallas kernels: 24.4 us -> 23.9 us
    pallas_call x2, Pallas kernels: 8.88 us -> 8.44 us  [half_part(): pl.pallas_call(functools.partial(half_kernel, rows, edge), in_specs=[HBM]...]
where the time goes in v5:
time: 43.2 us; the launch traced here: 43 us
  Pallas kernels  23.9 us (55%)
  starting transfers between devices  10 us (23%)
  waiting for transfers between devices  5.4 us (12%)
  local copies, waits for them, and re-layouts  1.94 us (4%)
  other arithmetic  0.96 us (2%)
  between operations  0.72 us (2%)
    pallas_call x1, Pallas kernels, mixer(): pl.pallas_call(functools.partial(mixer_kernel, rows, *scales), in_specs=[...  15.5 us
    pallas_call x2, Pallas kernels, half_part(): pl.pallas_call(functools.partial(half_kernel, rows, edge), in_specs=[HBM]...  8.44 us
    ppermute x4, starting transfers between devices, exchanged(): lax.ppermute(x, AXES, [(i, i ^ bits) for i in range(size)]).astype(F32)  5.58 us
    ppermute x4, waiting for transfers between devices, exchanged(): lax.ppermute(x, AXES, [(i, i ^ bits) for i in range(size)]).astype(F32)  5.39 us
    ppermute x1, starting transfers between devices, tap_halves(): return (long_filter, lax.ppermute(long_filter, 'fsdp', [(0, 1), (1, 0)]))  2.51 us
    ppermute x1, starting transfers between devices, swapped(): lax.ppermute(far, axis, far_route)  1.39 us
    convert_element_type x1, other arithmetic, sum_rest(): sent = x.astype(BF16)  0.92 us
  transfers between devices with their start and end apart: 7, of which 4 were waited for; matrix products, arithmetic and copies ran while one was open for 0% of the time, Pallas kernels for 10%

profile of v5, /device:TPU:0, one launch (start us, length us, event | category | flops | bytes accessed | tf_op | source)
XLA Modules:
  0.0 43.0 jit_solution(1707661707426680226)
XLA Ops:
  0.6 0.0 copy-start
  0.6 4.3 %edge_half.1 = (f32[8,2,128,128]{3,2,1,0:T(8,128)}, bf16[8,128,128]{2,1,0:T(8,128)(2,1)}, bf16[8,160,128]{2,1,0:T(8,128)(2,1)}, bf16[8,160,128]{2,1,0:T(8,128)(2,1)}) custom-call(s32[1,256]{1,0:T(1,128)} %ids_hbm.3, f32[3,7,1024]{2,1,0:T(8,128)} %w_hbm.5, bf16[1,256,1024]{2,1,0:T(8,128)(2,1)} %q_hbm.5, bf16[1,256,1024]{2,1,0:T(8,128)(2,1)} %k_hbm.5, ...), custom_call_target="tpu_custom_call" | custom-call | flops 8000000000 | bytes 16000000 | tf_op jit(solution)/shard_map/edge_half/pallas_call | solution.py:263
  5.0 0.5 %collective-permute-start.1 = (bf16[8,160,128]{2,1,0:T(8,128)(2,1)}, bf16[8,160,128]{2,1,0:T(8,128)(2,1)}, u32[]{:S(2)}, u32[]{:S(2)}) collective-permute-start(bf16[8,160,128]{2,1,0:T(8,128)(2,1)} %get-tuple-element.23.sent_near_hbm), channel_id=1, source_target_pairs={{0,4},{4,0},{8,12},{12,8},{1,5},{5,1},{9,13},{13,9},{2,6},{6,2},{1... | collective-permute-start | bytes 983048 | tf_op jit(solution)/shard_map/ppermute | solution.py:31
  5.5 1.4 %collective-permute-start.2 = (bf16[8,160,128]{2,1,0:T(8,128)(2,1)}, bf16[8,160,128]{2,1,0:T(8,128)(2,1)}, u32[]{:S(2)}, u32[]{:S(2)}) collective-permute-start(bf16[8,160,128]{2,1,0:T(8,128)(2,1)} %get-tuple-element.24.sent_far_hbm), channel_id=1, source_target_pairs={{8,4},{4,8},{9,5},{5,9},{10,6},{6,10},{11,7},{7,11},{24,20},{20,24... | collective-permute-start | bytes 983048 | tf_op jit(solution)/shard_map/ppermute | solution.py:31
  6.9 0.0 copy-done
  6.9 2.5 %collective-permute-start = (bf16[64,64]{1,0:T(8,128)(2,1)S(1)}, bf16[64,64]{1,0:T(8,128)(2,1)S(1)}, u32[]{:S(2)}, u32[]{:S(2)}) collective-permute-start(bf16[64,64]{1,0:T(8,128)(2,1)S(1)} %copy-done), channel_id=1, source_target_pairs={{0,16},{16,0},{1,17},{17,1},{2,18},{18,2},{3,19},{19,3},{4,20},{20... | collective-permute-start | bytes 24584 | tf_op jit(solution)/shard_map/ppermute | solution.py:830
  9.4 4.1 %other_half.1 = (f32[8,2,128,128]{3,2,1,0:T(8,128)}, bf16[8,128,128]{2,1,0:T(8,128)(2,1)}, bf16[8,128,128]{2,1,0:T(8,128)(2,1)}, bf16[8,128,128]{2,1,0:T(8,128)(2,1)}) custom-call(s32[1,256]{1,0:T(1,128)} %ids_hbm.3, f32[3,7,1024]{2,1,0:T(8,128)} %w_hbm.5, bf16[1,256,1024]{2,1,0:T(8,128)(2,1)} %q_hbm.5, bf16[1,256,1024]{2,1,0:T(8,128)(2,1)} %k_hbm.5, ...), custom_call_target="tpu_custom_call" | custom-call | flops 8000000000 | bytes 16000000 | tf_op jit(solution)/shard_map/other_half/pallas_call | solution.py:263
  13.5 0.0 collective-permute-done.other_half_hbm
  13.5 0.0 copy-start.1
  13.5 0.0 collective-permute-done.1.near_hbm
  13.6 0.0 collective-permute-done.2.far_hbm
  13.6 0.6 %copy-done.1 = bf16[64,64]{1,0:T(8,128)(2,1)} copy-done((bf16[64,64]{1,0:T(8,128)(2,1)}, bf16[64,64]{1,0:T(8,128)(2,1)S(1)}, u32[]{:S(2)}) %copy-start.1) | copy-done | bytes 8216
  14.1 15.5 %mixer.1 = (bf16[1,256,1024]{2,1,0:T(8,128)(2,1)}, bf16[1,256,1024]{2,1,0:T(8,128)(2,1)}, bf16[1,256,1024]{2,1,0:T(8,128)(2,1)}, f32[32,1024]{1,0:T(8,128)}) custom-call(s32[1,256]{1,0:T(1,128)} %ids_hbm.3, bf16[64,64]{1,0:T(8,128)(2,1)} %one_half_hbm.1, bf16[64,64]{1,0:T(8,128)(2,1)} %copy-done.1, f32[3,7,1024]{2,1,0:T(8,128)} %w_hbm.5, ...), custom_call_target="tpu_custom_call" | custom-call | tf_op jit(solution)/shard_map/mixer/pallas_call | solution.py:747
  29.7 2.0 %collective-permute-start.3 = (f32[32,1024]{1,0:T(8,128)}, f32[32,1024]{1,0:T(8,128)S(1)}, u32[]{:S(2)}, u32[]{:S(2)}) collective-permute-start(f32[32,1024]{1,0:T(8,128)} %get-tuple-element.34), channel_id=1, source_target_pairs={{0,4},{4,0},{8,12},{12,8},{16,20},{20,16},{24,28},{28,24},{1,5},{5... | collective-permute-start | bytes 393224 | tf_op jit(solution)/shard_map/ppermute | solution.py:809
  31.7 1.2 %collective-permute-done.3 = f32[32,1024]{1,0:T(8,128)S(1)} collective-permute-done((f32[32,1024]{1,0:T(8,128)}, f32[32,1024]{1,0:T(8,128)S(1)}, u32[]{:S(2)}, u32[]{:S(2)}) %collective-permute-start.3) | collective-permute-done | bytes 131104 | tf_op jit(solution)/shard_map/ppermute | solution.py:809
  32.9 0.9 %add_convert_fusion = bf16[32,1024]{1,0:T(8,128)(2,1)S(1)} fusion(f32[32,1024]{1,0:T(8,128)} %get-tuple-element.34, f32[32,1024]{1,0:T(8,128)S(1)} %collective-permute-done.3), kind=kLoop, calls=%fused_computation.1 | loop fusion | flops 65536 | bytes 327680 | tf_op jit(solution)/shard_map/convert_element_type | solution.py:820
  33.8 1.2 %collective-permute-start.4 = (bf16[32,1024]{1,0:T(8,128)(2,1)S(1)}, bf16[32,1024]{1,0:T(8,128)(2,1)S(1)}, u32[]{:S(2)}, u32[]{:S(2)}) collective-permute-start(bf16[32,1024]{1,0:T(8,128)(2,1)S(1)} %add_convert_fusion), channel_id=1, source_target_pairs={{0,8},{4,12},{8,0},{12,4},{16,24},{20,28},{24,16},{28,20},{1,9},{5... | collective-permute-start | bytes 196616 | tf_op jit(solution)/shard_map/ppermute | solution.py:809
  35.0 1.4 %collective-permute-start.5 = (bf16[32,1024]{1,0:T(8,128)(2,1)S(1)}, bf16[32,1024]{1,0:T(8,128)(2,1)S(1)}, u32[]{:S(2)}, u32[]{:S(2)}) collective-permute-start(bf16[32,1024]{1,0:T(8,128)(2,1)S(1)} %add_convert_fusion), channel_id=1, source_target_pairs={{0,16},{4,20},{8,24},{12,28},{16,0},{20,4},{24,8},{28,12},{1,17},{... | collective-permute-start | bytes 196616 | tf_op jit(solution)/shard_map/ppermute | solution.py:809
  36.4 1.0 %collective-permute-start.6 = (bf16[32,1024]{1,0:T(8,128)(2,1)S(1)}, bf16[32,1024]{1,0:T(8,128)(2,1)S(1)}, u32[]{:S(2)}, u32[]{:S(2)}) collective-permute-start(bf16[32,1024]{1,0:T(8,128)(2,1)S(1)} %add_convert_fusion), channel_id=1, source_target_pairs={{0,24},{4,28},{8,16},{12,20},{16,8},{20,12},{24,0},{28,4},{1,25},{... | collective-permute-start | bytes 196616 | tf_op jit(solution)/shard_map/ppermute | solution.py:809
  37.4 0.9 %collective-permute-done.4 = bf16[32,1024]{1,0:T(8,128)(2,1)S(1)} collective-permute-done((bf16[32,1024]{1,0:T(8,128)(2,1)S(1)}, bf16[32,1024]{1,0:T(8,128)(2,1)S(1)}, u32[]{:S(2)}, u32[]{:S(2)}) %collective-permute-start.4) | collective-permute-done | bytes 65568 | tf_op jit(solution)/shard_map/ppermute | solution.py:809
  38.2 1.4 %collective-permute-done.5 = bf16[32,1024]{1,0:T(8,128)(2,1)S(1)} collective-permute-done((bf16[32,1024]{1,0:T(8,128)(2,1)S(1)}, bf16[32,1024]{1,0:T(8,128)(2,1)S(1)}, u32[]{:S(2)}, u32[]{:S(2)}) %collective-permute-start.5) | collective-permute-done | bytes 65568 | tf_op jit(solution)/shard_map/ppermute | solution.py:809
  39.7 1.9 %collective-permute-done.6 = bf16[32,1024]{1,0:T(8,128)(2,1)S(1)} collective-permute-done((bf16[32,1024]{1,0:T(8,128)(2,1)S(1)}, bf16[32,1024]{1,0:T(8,128)(2,1)S(1)}, u32[]{:S(2)}, u32[]{:S(2)}) %collective-permute-start.6) | collective-permute-done | bytes 65568 | tf_op jit(solution)/shard_map/ppermute | solution.py:809
  41.6 0.7 %reshape.21 = f32[3,7,1024]{2,1,0:T(8,128)} reshape(f32[21,1024]{1,0:T(8,128)S(1)} %slice.9) | data formatting | bytes 172032 | tf_op jit(solution)/shard_map/reshape | solution.py:860
  42.3 0.7 %constant_dynamic-slice_fusion = f32[64,64]{1,0:T(8,128)} fusion(f32[64,128]{1,0:T(8,128)S(1)} %slice_bitcast_fusion, s32[]{:T(128)S(6)} %select_n.3), kind=kLoop, calls=%fused_computation.3 | loop fusion | bytes 32772 | tf_op jit(solution)/shard_map/dynamic_slice | solution.py:864
  (3 shorter events, 0.0 us)
Async XLA Ops:
  0.6 6.3 %copy-start = (bf16[64,64]{1,0:T(8,128)(2,1)S(1)}, bf16[64,64]{1,0:T(8,128)(2,1)}, u32[]{:S(2)}) copy-start(bf16[64,64]{1,0:T(8,128)(2,1)} %one_half_hbm.1) | copy-start | bytes 24580
  5.0 8.6 %collective-permute-start.1 = (bf16[8,160,128]{2,1,0:T(8,128)(2,1)}, bf16[8,160,128]{2,1,0:T(8,128)(2,1)}, u32[]{:S(2)}, u32[]{:S(2)}) collective-permute-start(bf16[8,160,128]{2,1,0:T(8,128)(2,1)} %get-tuple-element.23.sent_near_hbm), channel_id=1, source_target_pairs={{0,4},{4,0},{8,12},{12,8},{1,5},{5,1},{9,13},{13,9},{2,6},{6,2},{1... | collective-permute-start | bytes 983048 | tf_op jit(solution)/shard_map/ppermute | solution.py:31
  5.5 8.0 %collective-permute-start.2 = (bf16[8,160,128]{2,1,0:T(8,128)(2,1)}, bf16[8,160,128]{2,1,0:T(8,128)(2,1)}, u32[]{:S(2)}, u32[]{:S(2)}) collective-permute-start(bf16[8,160,128]{2,1,0:T(8,128)(2,1)} %get-tuple-element.24.sent_far_hbm), channel_id=1, source_target_pairs={{8,4},{4,8},{9,5},{5,9},{10,6},{6,10},{11,7},{7,11},{24,20},{20,24... | collective-permute-start | bytes 983048 | tf_op jit(solution)/shard_map/ppermute | solution.py:31
  6.9 6.6 %collective-permute-start = (bf16[64,64]{1,0:T(8,128)(2,1)S(1)}, bf16[64,64]{1,0:T(8,128)(2,1)S(1)}, u32[]{:S(2)}, u32[]{:S(2)}) collective-permute-start(bf16[64,64]{1,0:T(8,128)(2,1)S(1)} %copy-done), channel_id=1, source_target_pairs={{0,16},{16,0},{1,17},{17,1},{2,18},{18,2},{3,19},{19,3},{4,20},{20... | collective-permute-start | bytes 24584 | tf_op jit(solution)/shard_map/ppermute | solution.py:830
  13.5 0.6 %copy-start.1 = (bf16[64,64]{1,0:T(8,128)(2,1)}, bf16[64,64]{1,0:T(8,128)(2,1)S(1)}, u32[]{:S(2)}) copy-start(bf16[64,64]{1,0:T(8,128)(2,1)S(1)} %collective-permute-done.other_half_hbm) | copy-start | bytes 24580
  29.7 3.2 %collective-permute-start.3 = (f32[32,1024]{1,0:T(8,128)}, f32[32,1024]{1,0:T(8,128)S(1)}, u32[]{:S(2)}, u32[]{:S(2)}) collective-permute-start(f32[32,1024]{1,0:T(8,128)} %get-tuple-element.34), channel_id=1, source_target_pairs={{0,4},{4,0},{8,12},{12,8},{16,20},{20,16},{24,28},{28,24},{1,5},{5... | collective-permute-start | bytes 393224 | tf_op jit(solution)/shard_map/ppermute | solution.py:809
  33.8 4.4 %collective-permute-start.4 = (bf16[32,1024]{1,0:T(8,128)(2,1)S(1)}, bf16[32,1024]{1,0:T(8,128)(2,1)S(1)}, u32[]{:S(2)}, u32[]{:S(2)}) collective-permute-start(bf16[32,1024]{1,0:T(8,128)(2,1)S(1)} %add_convert_fusion), channel_id=1, source_target_pairs={{0,8},{4,12},{8,0},{12,4},{16,24},{20,28},{24,16},{28,20},{1,9},{5... | collective-permute-start | bytes 196616 | tf_op jit(solution)/shard_map/ppermute | solution.py:809
  35.0 4.7 %collective-permute-start.5 = (bf16[32,1024]{1,0:T(8,128)(2,1)S(1)}, bf16[32,1024]{1,0:T(8,128)(2,1)S(1)}, u32[]{:S(2)}, u32[]{:S(2)}) collective-permute-start(bf16[32,1024]{1,0:T(8,128)(2,1)S(1)} %add_convert_fusion), channel_id=1, source_target_pairs={{0,16},{4,20},{8,24},{12,28},{16,0},{20,4},{24,8},{28,12},{1,17},{... | collective-permute-start | bytes 196616 | tf_op jit(solution)/shard_map/ppermute | solution.py:809
  36.4 5.2 %collective-permute-start.6 = (bf16[32,1024]{1,0:T(8,128)(2,1)S(1)}, bf16[32,1024]{1,0:T(8,128)(2,1)S(1)}, u32[]{:S(2)}, u32[]{:S(2)}) collective-permute-start(bf16[32,1024]{1,0:T(8,128)(2,1)S(1)} %add_convert_fusion), channel_id=1, source_target_pairs={{0,24},{4,28},{8,16},{12,20},{16,8},{20,12},{24,0},{28,4},{1,25},{... | collective-permute-start | bytes 196616 | tf_op jit(solution)/shard_map/ppermute | solution.py:809

commit v6 on v5

--- a/solution.py
+++ b/solution.py
@@ -13,7 +13,7 @@
 LANES = 128
 GROUP = 16
 EDGE = 8
-VMEM_LIMIT = 65300 << 10
+VMEM_LIMIT = 65528 << 10
 HEAD_ROWS = LANES + 32
 F32 = jnp.float32
 BF16 = jnp.bfloat16
@@ -66,6 +66,7 @@
     one_hbm,
     two_hbm,
     ids_ref,
+    ids_scalar,
     w_ref,
     bq,
     bk,
@@ -94,7 +95,7 @@
     lead = 16
 
     def small():
-        return ((ids_hbm, ids_ref), (w_hbm, w_ref))
+        return ((ids_hbm, ids_ref), (ids_hbm, ids_scalar), (w_hbm, w_ref))
 
     def rows_from(low, before):
         start = low - before if low else 0
@@ -174,11 +175,13 @@
     def pair(a, b):
         return jnp.concatenate([a, b], axis=0).astype(BF16)
 
-    def filtered(x, h, taps, low, at, size):
+    def filtered(x, h, taps, low, at, size, masked=True):
         total = taps[0] * x[h, pl.ds(at + lead, size), :]
         for j in range(1, SHORT):
-            mask = mj[j - 1, pl.ds(at + low, size), :]
-            total += taps[j] * (mask * x[h, pl.ds(at + lead - j, size), :])
+            piece = x[h, pl.ds(at + lead - j, size), :]
+            if masked:
+                piece = mj[j - 1, pl.ds(at + low, size), :] * piece
+            total += taps[j] * piece
         return total
 
     def two_blocks(half, carry):
@@ -195,18 +198,34 @@
         def taps_of(n, i):
             return [w_ref[n, j : j + 1, lanes_of(i)] for j in range(SHORT)]
 
-        def convolve(n, inner):
-            at = pl.multiple_of(part * n, part)
+        def convolve_part(at, masked):
             for h, i in enumerate(pair_of):
-                key = filtered(xk, h, taps_of(1, i), kv_low, at, part)
-                value = filtered(xv, h, taps_of(2, i), kv_low, at, part)
-                query = filtered(xq, h, taps_of(0, i), q_low, at, part)
+                key = filtered(xk, h, taps_of(1, i), kv_low, at, part, masked)
+                value = filtered(xv, h, taps_of(2, i), kv_low, at, part, masked)
+                query = filtered(xq, h, taps_of(0, i), q_low, at, part, masked)
                 conv_ref[i, 0, pl.ds(at, part), :] = key
                 conv_ref[i, 1, pl.ds(at, part), :] = value
                 uf[h, pl.ds(at, part), :] = key * value
                 dz = bg[pl.ds(at + q_low, part), lanes_of(i)].astype(F32) * query
                 dzf[h, pl.ds(at, part), :] = dz
                 dzr_ref[i, pl.ds(at, part), :] = dz.astype(BF16)
+
+        def one_genome(low, at):
+            start = jnp.maximum(low + at - (SHORT - 1), 0)
+            return ids_scalar[0, start] == ids_scalar[0, low + at + part - 1]
+
+        def convolve(n, inner):
+            at = pl.multiple_of(part * n, part)
+            plain = jnp.logical_and(one_genome(kv_low, at), one_genome(q_low, at))
+
+            @pl.when(plain)
+            def without_masks():
+                convolve_part(at, False)
+
+            @pl.when(jnp.logical_not(plain))
+            def with_masks():
+                convolve_part(at, True)
+
             return inner
 
         lax.fori_loop(0, TAPS // part, convolve, 0)
@@ -267,6 +286,7 @@
         out_shape=[jax.ShapeDtypeStruct(*r) for r in results],
         scratch_shapes=[
             pltpu.VMEM(ids.shape, jnp.int32),
+            pltpu.SMEM(ids.shape, jnp.int32),
             vm(*short_filter.shape),
             *[vb(rows, channels)] * 4,
             *[pltpu.VMEM(*r) for r in results],
@@ -275,7 +295,7 @@
             *[vm(2, TAPS + 32, LANES)] * 3,
             vm(2, TAPS, LANES),
             vm(2, TAPS, LANES),
-            pltpu.SemaphoreType.DMA((1, 2)),
+            pltpu.SemaphoreType.DMA((1, 3)),
             pltpu.SemaphoreType.DMA((count // 2, 4)),
             pltpu.SemaphoreType.DMA((count // 2, 2)),
             pltpu.SemaphoreType.DMA((count // 2, 2)),

time: 43.2 us -> 43.1 us (level)
  local copies, waits for them, and re-layouts: 1.94 us -> 1.36 us
  waiting for transfers between devices: 5.4 us -> 5.84 us
    unnamed x4 -> x0, local copies, waits for them, and re-layouts: 0.59 us -> none
    ppermute x4, waiting for transfers between devices: 5.39 us -> 5.84 us  [exchanged(): lax.ppermute(x, AXES, [(i, i ^ bits) for i in range(size)]).astype(F32)]
  transfers between devices with their start and end apart: 7 -> 7, of which waited for: 4 -> 4; matrix products, arithmetic and copies ran while one was open for 0% -> 0% of each run, Pallas kernels for 10% -> 9%
where the time goes in v6:
time: 43.1 us; the launch traced here: 43 us
  Pallas kernels  23.8 us (55%)
  starting transfers between devices  10.3 us (24%)
  waiting for transfers between devices  5.84 us (14%)
  local copies, waits for them, and re-layouts  1.36 us (3%)
  other arithmetic  0.96 us (2%)
  between operations  0.7 us (2%)
    pallas_call x1, Pallas kernels, mixer(): pl.pallas_call(functools.partial(mixer_kernel, rows, *scales), in_specs=[...  15.5 us
    pallas_call x2, Pallas kernels, half_part(): pl.pallas_call(functools.partial(half_kernel, rows, edge), in_specs=[HBM]...  8.31 us
    ppermute x4, starting transfers between devices, exchanged(): lax.ppermute(x, AXES, [(i, i ^ bits) for i in range(size)]).astype(F32)  5.88 us
    ppermute x4, waiting for transfers between devices, exchanged(): lax.ppermute(x, AXES, [(i, i ^ bits) for i in range(size)]).astype(F32)  5.84 us
    ppermute x1, starting transfers between devices, tap_halves(): return (long_filter, lax.ppermute(long_filter, 'fsdp', [(0, 1), (1, 0)]))  2.3 us
    ppermute x1, starting transfers between devices, swapped(): lax.ppermute(far, axis, far_route)  1.38 us
    convert_element_type x1, other arithmetic, sum_rest(): sent = x.astype(BF16)  0.92 us
  transfers between devices with their start and end apart: 7, of which 4 were waited for; matrix products, arithmetic and copies ran while one was open for 0% of the time, Pallas kernels for 9%

profile of v6, /device:TPU:0, one launch (start us, length us, event | category | flops | bytes accessed | tf_op | source)
XLA Modules:
  0.0 43.0 jit_solution(14747938918479782705)
XLA Ops:
  0.6 4.3 %edge_half.1 = (f32[8,2,128,128]{3,2,1,0:T(8,128)}, bf16[8,128,128]{2,1,0:T(8,128)(2,1)}, bf16[8,160,128]{2,1,0:T(8,128)(2,1)}, bf16[8,160,128]{2,1,0:T(8,128)(2,1)}) custom-call(s32[1,256]{1,0:T(1,128)} %ids_hbm.3, f32[3,7,1024]{2,1,0:T(8,128)} %w_hbm.5, bf16[1,256,1024]{2,1,0:T(8,128)(2,1)} %q_hbm.5, bf16[1,256,1024]{2,1,0:T(8,128)(2,1)} %k_hbm.5, ...), custom_call_target="tpu_custom_call" | custom-call | flops 8000000000 | bytes 16000000 | tf_op jit(solution)/shard_map/edge_half/pallas_call | solution.py:282
  4.9 0.7 %collective-permute-start.1 = (bf16[8,160,128]{2,1,0:T(8,128)(2,1)}, bf16[8,160,128]{2,1,0:T(8,128)(2,1)}, u32[]{:S(2)}, u32[]{:S(2)}) collective-permute-start(bf16[8,160,128]{2,1,0:T(8,128)(2,1)} %get-tuple-element.23.sent_near_hbm), channel_id=1, source_target_pairs={{0,4},{4,0},{8,12},{12,8},{1,5},{5,1},{9,13},{13,9},{2,6},{6,2},{1... | collective-permute-start | bytes 983048 | tf_op jit(solution)/shard_map/ppermute | solution.py:31
  5.6 1.4 %collective-permute-start.2 = (bf16[8,160,128]{2,1,0:T(8,128)(2,1)}, bf16[8,160,128]{2,1,0:T(8,128)(2,1)}, u32[]{:S(2)}, u32[]{:S(2)}) collective-permute-start(bf16[8,160,128]{2,1,0:T(8,128)(2,1)} %get-tuple-element.24.sent_far_hbm), channel_id=1, source_target_pairs={{8,4},{4,8},{9,5},{5,9},{10,6},{6,10},{11,7},{7,11},{24,20},{20,24... | collective-permute-start | bytes 983048 | tf_op jit(solution)/shard_map/ppermute | solution.py:31
  7.0 2.3 %collective-permute-start = (bf16[64,64]{1,0:T(8,128)(2,1)}, bf16[64,64]{1,0:T(8,128)(2,1)}, u32[]{:S(2)}, u32[]{:S(2)}) collective-permute-start(bf16[64,64]{1,0:T(8,128)(2,1)} %one_half_hbm.1), channel_id=1, source_target_pairs={{0,16},{16,0},{1,17},{17,1},{2,18},{18,2},{3,19},{19,3},{4,20},{20... | collective-permute-start | bytes 24584 | tf_op jit(solution)/shard_map/ppermute | solution.py:850
  9.3 4.0 %other_half.1 = (f32[8,2,128,128]{3,2,1,0:T(8,128)}, bf16[8,128,128]{2,1,0:T(8,128)(2,1)}, bf16[8,128,128]{2,1,0:T(8,128)(2,1)}, bf16[8,128,128]{2,1,0:T(8,128)(2,1)}) custom-call(s32[1,256]{1,0:T(1,128)} %ids_hbm.3, f32[3,7,1024]{2,1,0:T(8,128)} %w_hbm.5, bf16[1,256,1024]{2,1,0:T(8,128)(2,1)} %q_hbm.5, bf16[1,256,1024]{2,1,0:T(8,128)(2,1)} %k_hbm.5, ...), custom_call_target="tpu_custom_call" | custom-call | flops 8000000000 | bytes 16000000 | tf_op jit(solution)/shard_map/other_half/pallas_call | solution.py:282
  13.3 0.0 collective-permute-done.other_half_hbm
  13.4 0.0 collective-permute-done.1.near_hbm
  13.4 0.0 collective-permute-done.2.far_hbm
  13.4 15.5 %mixer.1 = (bf16[1,256,1024]{2,1,0:T(8,128)(2,1)}, bf16[1,256,1024]{2,1,0:T(8,128)(2,1)}, bf16[1,256,1024]{2,1,0:T(8,128)(2,1)}, f32[32,1024]{1,0:T(8,128)}) custom-call(s32[1,256]{1,0:T(1,128)} %ids_hbm.3, bf16[64,64]{1,0:T(8,128)(2,1)} %one_half_hbm.1, bf16[64,64]{1,0:T(8,128)(2,1)} %collective-permute-done.other_half_hbm, f32[3,7,1024]{2,1,0:T(8,128)} %w_hbm.5, ...), custom_call_target="tpu_custom_call" | custom-call | tf_op jit(solution)/shard_map/mixer/pallas_call | solution.py:767
  28.9 2.3 %collective-permute-start.3 = (f32[32,1024]{1,0:T(8,128)}, f32[32,1024]{1,0:T(8,128)S(1)}, u32[]{:S(2)}, u32[]{:S(2)}) collective-permute-start(f32[32,1024]{1,0:T(8,128)} %get-tuple-element.34), channel_id=1, source_target_pairs={{0,4},{4,0},{8,12},{12,8},{16,20},{20,16},{24,28},{28,24},{1,5},{5... | collective-permute-start | bytes 393224 | tf_op jit(solution)/shard_map/ppermute | solution.py:829
  31.2 1.2 %collective-permute-done.3 = f32[32,1024]{1,0:T(8,128)S(1)} collective-permute-done((f32[32,1024]{1,0:T(8,128)}, f32[32,1024]{1,0:T(8,128)S(1)}, u32[]{:S(2)}, u32[]{:S(2)}) %collective-permute-start.3) | collective-permute-done | bytes 131104 | tf_op jit(solution)/shard_map/ppermute | solution.py:829
  32.4 0.9 %add_convert_fusion = bf16[32,1024]{1,0:T(8,128)(2,1)S(1)} fusion(f32[32,1024]{1,0:T(8,128)} %get-tuple-element.34, f32[32,1024]{1,0:T(8,128)S(1)} %collective-permute-done.3), kind=kLoop, calls=%fused_computation.1 | loop fusion | flops 65536 | bytes 327680 | tf_op jit(solution)/shard_map/convert_element_type | solution.py:840
  33.4 1.6 %collective-permute-start.4 = (bf16[32,1024]{1,0:T(8,128)(2,1)S(1)}, bf16[32,1024]{1,0:T(8,128)(2,1)S(1)}, u32[]{:S(2)}, u32[]{:S(2)}) collective-permute-start(bf16[32,1024]{1,0:T(8,128)(2,1)S(1)} %add_convert_fusion), channel_id=1, source_target_pairs={{0,8},{4,12},{8,0},{12,4},{16,24},{20,28},{24,16},{28,20},{1,9},{5... | collective-permute-start | bytes 196616 | tf_op jit(solution)/shard_map/ppermute | solution.py:829
  34.9 1.5 %collective-permute-start.5 = (bf16[32,1024]{1,0:T(8,128)(2,1)S(1)}, bf16[32,1024]{1,0:T(8,128)(2,1)S(1)}, u32[]{:S(2)}, u32[]{:S(2)}) collective-permute-start(bf16[32,1024]{1,0:T(8,128)(2,1)S(1)} %add_convert_fusion), channel_id=1, source_target_pairs={{0,16},{4,20},{8,24},{12,28},{16,0},{20,4},{24,8},{28,12},{1,17},{... | collective-permute-start | bytes 196616 | tf_op jit(solution)/shard_map/ppermute | solution.py:829
  36.4 0.5 %collective-permute-start.6 = (bf16[32,1024]{1,0:T(8,128)(2,1)S(1)}, bf16[32,1024]{1,0:T(8,128)(2,1)S(1)}, u32[]{:S(2)}, u32[]{:S(2)}) collective-permute-start(bf16[32,1024]{1,0:T(8,128)(2,1)S(1)} %add_convert_fusion), channel_id=1, source_target_pairs={{0,24},{4,28},{8,16},{12,20},{16,8},{20,12},{24,0},{28,4},{1,25},{... | collective-permute-start | bytes 196616 | tf_op jit(solution)/shard_map/ppermute | solution.py:829
  36.9 0.9 %collective-permute-done.4 = bf16[32,1024]{1,0:T(8,128)(2,1)S(1)} collective-permute-done((bf16[32,1024]{1,0:T(8,128)(2,1)S(1)}, bf16[32,1024]{1,0:T(8,128)(2,1)S(1)}, u32[]{:S(2)}, u32[]{:S(2)}) %collective-permute-start.4) | collective-permute-done | bytes 65568 | tf_op jit(solution)/shard_map/ppermute | solution.py:829
  37.8 1.8 %collective-permute-done.5 = bf16[32,1024]{1,0:T(8,128)(2,1)S(1)} collective-permute-done((bf16[32,1024]{1,0:T(8,128)(2,1)S(1)}, bf16[32,1024]{1,0:T(8,128)(2,1)S(1)}, u32[]{:S(2)}, u32[]{:S(2)}) %collective-permute-start.5) | collective-permute-done | bytes 65568 | tf_op jit(solution)/shard_map/ppermute | solution.py:829
  39.6 2.0 %collective-permute-done.6 = bf16[32,1024]{1,0:T(8,128)(2,1)S(1)} collective-permute-done((bf16[32,1024]{1,0:T(8,128)(2,1)S(1)}, bf16[32,1024]{1,0:T(8,128)(2,1)S(1)}, u32[]{:S(2)}, u32[]{:S(2)}) %collective-permute-start.6) | collective-permute-done | bytes 65568 | tf_op jit(solution)/shard_map/ppermute | solution.py:829
  41.6 0.7 %reshape.21 = f32[3,7,1024]{2,1,0:T(8,128)} reshape(f32[21,1024]{1,0:T(8,128)S(1)} %slice.9) | data formatting | bytes 172032 | tf_op jit(solution)/shard_map/reshape | solution.py:880
  42.3 0.7 %constant_dynamic-slice_fusion = f32[64,64]{1,0:T(8,128)} fusion(f32[64,128]{1,0:T(8,128)S(1)} %slice_bitcast_fusion, s32[]{:T(128)S(6)} %select_n.3), kind=kLoop, calls=%fused_computation.3 | loop fusion | bytes 32772 | tf_op jit(solution)/shard_map/dynamic_slice | solution.py:884
  (3 shorter events, 0.0 us)
Async XLA Ops:
  4.9 8.4 %collective-permute-start.1 = (bf16[8,160,128]{2,1,0:T(8,128)(2,1)}, bf16[8,160,128]{2,1,0:T(8,128)(2,1)}, u32[]{:S(2)}, u32[]{:S(2)}) collective-permute-start(bf16[8,160,128]{2,1,0:T(8,128)(2,1)} %get-tuple-element.23.sent_near_hbm), channel_id=1, source_target_pairs={{0,4},{4,0},{8,12},{12,8},{1,5},{5,1},{9,13},{13,9},{2,6},{6,2},{1... | collective-permute-start | bytes 983048 | tf_op jit(solution)/shard_map/ppermute | solution.py:31
  5.6 7.7 %collective-permute-start.2 = (bf16[8,160,128]{2,1,0:T(8,128)(2,1)}, bf16[8,160,128]{2,1,0:T(8,128)(2,1)}, u32[]{:S(2)}, u32[]{:S(2)}) collective-permute-start(bf16[8,160,128]{2,1,0:T(8,128)(2,1)} %get-tuple-element.24.sent_far_hbm), channel_id=1, source_target_pairs={{8,4},{4,8},{9,5},{5,9},{10,6},{6,10},{11,7},{7,11},{24,20},{20,24... | collective-permute-start | bytes 983048 | tf_op jit(solution)/shard_map/ppermute | solution.py:31
  7.0 6.3 %collective-permute-start = (bf16[64,64]{1,0:T(8,128)(2,1)}, bf16[64,64]{1,0:T(8,128)(2,1)}, u32[]{:S(2)}, u32[]{:S(2)}) collective-permute-start(bf16[64,64]{1,0:T(8,128)(2,1)} %one_half_hbm.1), channel_id=1, source_target_pairs={{0,16},{16,0},{1,17},{17,1},{2,18},{18,2},{3,19},{19,3},{4,20},{20... | collective-permute-start | bytes 24584 | tf_op jit(solution)/shard_map/ppermute | solution.py:850
  28.9 3.5 %collective-permute-start.3 = (f32[32,1024]{1,0:T(8,128)}, f32[32,1024]{1,0:T(8,128)S(1)}, u32[]{:S(2)}, u32[]{:S(2)}) collective-permute-start(f32[32,1024]{1,0:T(8,128)} %get-tuple-element.34), channel_id=1, source_target_pairs={{0,4},{4,0},{8,12},{12,8},{16,20},{20,16},{24,28},{28,24},{1,5},{5... | collective-permute-start | bytes 393224 | tf_op jit(solution)/shard_map/ppermute | solution.py:829
  33.4 4.4 %collective-permute-start.4 = (bf16[32,1024]{1,0:T(8,128)(2,1)S(1)}, bf16[32,1024]{1,0:T(8,128)(2,1)S(1)}, u32[]{:S(2)}, u32[]{:S(2)}) collective-permute-start(bf16[32,1024]{1,0:T(8,128)(2,1)S(1)} %add_convert_fusion), channel_id=1, source_target_pairs={{0,8},{4,12},{8,0},{12,4},{16,24},{20,28},{24,16},{28,20},{1,9},{5... | collective-permute-start | bytes 196616 | tf_op jit(solution)/shard_map/ppermute | solution.py:829
  34.9 4.7 %collective-permute-start.5 = (bf16[32,1024]{1,0:T(8,128)(2,1)S(1)}, bf16[32,1024]{1,0:T(8,128)(2,1)S(1)}, u32[]{:S(2)}, u32[]{:S(2)}) collective-permute-start(bf16[32,1024]{1,0:T(8,128)(2,1)S(1)} %add_convert_fusion), channel_id=1, source_target_pairs={{0,16},{4,20},{8,24},{12,28},{16,0},{20,4},{24,8},{28,12},{1,17},{... | collective-permute-start | bytes 196616 | tf_op jit(solution)/shard_map/ppermute | solution.py:829
  36.4 5.2 %collective-permute-start.6 = (bf16[32,1024]{1,0:T(8,128)(2,1)S(1)}, bf16[32,1024]{1,0:T(8,128)(2,1)S(1)}, u32[]{:S(2)}, u32[]{:S(2)}) collective-permute-start(bf16[32,1024]{1,0:T(8,128)(2,1)S(1)} %add_convert_fusion), channel_id=1, source_target_pairs={{0,24},{4,28},{8,16},{12,20},{16,8},{20,12},{24,0},{28,4},{1,25},{... | collective-permute-start | bytes 196616 | tf_op jit(solution)/shard_map/ppermute | solution.py:829
